TPU v7x, 32 devices: a whole 2x2x4 slice. The times are simulated.
32 devices in a mesh: sta: 2 (over x), tm: 16 (over z, y, core).
Axes of the slice: x: 2, y: 2, z: 4, core: 2. Of those that a mesh axis runs over, the one named last changes fastest.
Arguments:
- record: bfloat16 [96, 12288], P('sta', 'tm')
- templates: bfloat16 [64, 96, 512], P('tm', 'sta'), may hold values from -6 to 6
- shifts: int32 [96], P('sta'), may hold values from 0 to 255, as said below
- live_mask: int32 [96], P('sta'), may hold values 0 or 1
- plan: int32 [64], replicated, may hold values from 0 to 63, each once
Outputs:
- stacks: float32 [64, 12288], P('sta', 'tm')
Inputs may be any that keep to these rules, and one draw needn't show every extreme that they name: `shifts`: some channel has the shift 256 - 1. `plan`: each bank slot appears once.
All inputs are finite; a program needn't handle non-finite values. No bound on the sum of `live_mask` on one device may be relied on, other than what follows from the above.
Results may differ from a plain program's by a relative error of at most 0.0003.
Values may be sent and summed in bfloat16 or wider, within the bound.
No kernel may reach another device: no remote copies, remote signals or barrier semaphores. Data moves between devices by JAX's collectives and lax.ppermute only.
A program may use at most 64 MiB of HBM per device.

v0:
```python
import math

import jax
import jax.numpy as jnp
from jax import lax
from jax.sharding import PartitionSpec as P

CHANNELS = 96


def passed_along(shard, axis, by):
    count = lax.axis_size(axis)
    pairs = [(i, i + by) for i in range(count) if 0 <= i + by < count]
    return lax.ppermute(shard, axis, pairs)


def hankel_rows(signal, taps_len, span_len):
    length = signal.shape[0]
    copies = jnp.tile(signal, taps_len + 1)
    skewed = copies[: taps_len * (length + 1)].reshape(taps_len, length + 1)
    return skewed[:, :span_len]


def correlate(panels_in, aligned, live_vals, taps_len, span_len, group_cap):
    tmpl_rows, chan_count, _ = panels_in.shape
    group_size = math.gcd(chan_count, group_cap)
    overall = math.sqrt(taps_len / CHANNELS)
    norm_vals = jnp.sqrt(jnp.sum(jnp.square(panels_in.astype(jnp.float32)), axis=2) + 1e-06)
    weights = live_vals[None, :] * overall / norm_vals
    in_pos = lax.broadcasted_iota(jnp.int32, (span_len + taps_len, span_len), 0)
    out_pos = lax.broadcasted_iota(jnp.int32, (span_len + taps_len, span_len), 1)
    band_ones = ((in_pos >= out_pos) & (in_pos < out_pos + taps_len)).astype(jnp.float32)

    def add_group(group_idx, running):
        first_chan = group_idx * group_size
        panel_part = lax.dynamic_slice_in_dim(panels_in, first_chan, group_size, 1)
        window = lax.dynamic_slice_in_dim(aligned, first_chan, group_size, 0)
        stacked = jax.vmap(lambda signal_row: hankel_rows(signal_row, taps_len, span_len))(window)
        products = jnp.einsum(
            "rgl,glt->rgt", panel_part, stacked, preferred_element_type=jnp.float32
        )
        squares = jnp.square(window.astype(jnp.float32))
        energy = jnp.dot(squares, band_ones, precision=lax.Precision.HIGHEST)
        weighting = lax.dynamic_slice_in_dim(weights, first_chan, group_size, 1)
        scaled = products * weighting[:, :, None] * lax.rsqrt(energy + 1e-06)[None, :, :]
        return running + jnp.sum(scaled, axis=1)

    start_val = jnp.zeros((tmpl_rows, span_len), jnp.float32)
    return lax.fori_loop(0, chan_count // group_size, add_group, start_val)


def per_device(record, templates, shifts, live_mask, plan):
    taps_len = templates.shape[2]
    span_len = record.shape[1]
    live_vals = live_mask.astype(jnp.float32)
    rim_part = passed_along(record, "tm", -1)
    extended = jnp.concatenate([record, rim_part], axis=1)
    aligned = jax.vmap(
        lambda signal_row, lag_val: lax.dynamic_slice_in_dim(
            signal_row, lag_val, span_len + taps_len
        )
    )(extended, shifts)
    bank_all = lax.all_gather(templates, "tm", axis=0, tiled=True)
    ordered = jnp.take(bank_all, plan, axis=0)
    partial_value = correlate(ordered, aligned, live_vals, taps_len, span_len, 8)
    return lax.psum_scatter(partial_value, "sta", scatter_dimension=0, tiled=True)


def solution(mesh):
    placed = (P("sta", "tm"), P("tm", "sta", None), P("sta"), P("sta"), P())
    return jax.shard_map(
        per_device, mesh=mesh, in_specs=placed, out_specs=P("sta", "tm"), check_vma=False
    )
```

profile of v0, /device:TPU:0, one launch (start us, length us, event | category | flops | bytes accessed | tf_op | source)
XLA Modules:
  0.0 511.8 jit_solution(9298420677472777059)
XLA Ops:
  11.5 97.8 %while.15 = (s32[]{:T(128)}, bf16[48,1536]{1,0:T(8,128)(2,1)S(1)}, s32[48,2]{0,1:T(2,128)S(1)}, bf16[48,1280]{1,0:T(8,128)(2,1)S(1)}, s32[]{:T(128)}, /*index=5*/s32[]{:T(128)}) while((s32[]{:T(128)}, bf16[48,1536]{1,0:T(8,128)(2,1)S(1)}, s32[48,2]{0,1:T(2,128)S(1)}, bf16[48,1280]{1,0:T(8,128)(2,1)S(1)}, s32[]{:T(128)}, /*index=5*/s32[]{:T(128)}) %tuple.49), condition=%wide.while_cond, body=%wide.while_body.sunk | while | flops 2 | bytes 10361 | solution.py:59
  12.2 1.3 dynamic-slice.7
  14.2 1.3 dynamic-slice.7
  16.2 1.3 dynamic-slice.7
  18.3 1.3 dynamic-slice.7
  20.3 1.3 dynamic-slice.7
  22.3 1.3 dynamic-slice.7
  26.4 1.3 dynamic-slice.7
  28.5 1.3 dynamic-slice.7
  30.5 1.3 dynamic-slice.7
  32.5 1.3 dynamic-slice.7
  34.6 1.3 dynamic-slice.7
  36.6 1.3 dynamic-slice.7
  42.7 1.3 dynamic-slice.7
  109.3 2.6 gather_fusion
  112.0 2.6 multiply_reduce_fusion
  114.7 374.5 %while.16 = (s32[]{:T(128)}, f32[64,768]{1,0:T(8,128)S(1)}, bf16[48,1280]{1,0:T(8,128)(2,1)S(1)}, bf16[64,48,512]{2,1,0:T(8,128)(2,1)}, f32[64,48]{0,1:T(8,128)S...) while((s32[]{:T(128)}, f32[64,768]{1,0:T(8,128)S(1)}, ...), condition=%wide.region_3.4_spmd.clone, body=%wide.region_1.3_spmd.clone.sunk | while | flops 502212608 | bytes 82261168 | solution.py:49
  115.4 4.6 slice.43
  120.1 23.4 %reshape.53 = bf16[5246976]{0:T(1024)(128)(2,1)} reshape(bf16[8,655872]{1,0:T(8,128)(2,1)} %slice.43) | data formatting | bytes 20987904 | tf_op jit(solution)/shard_map/while
  143.4 26.5 %reshape.54 = bf16[8,512,1281]{2,1,0:T(8,128)(2,1)} reshape(bf16[5246976]{0:T(1024)(128)(2,1)} %reshape.53) | data formatting | bytes 20987904 | tf_op jit(solution)/shard_map/while/body/eval_jaxpr/vmap()/reshape | solution.py:20
  169.9 2.0 fusion.36
  173.0 4.1 fusion.37
  177.9 4.6 slice.43
  182.5 23.4 %reshape.53 = bf16[5246976]{0:T(1024)(128)(2,1)} reshape(bf16[8,655872]{1,0:T(8,128)(2,1)} %slice.43) | data formatting | bytes 20987904 | tf_op jit(solution)/shard_map/while
  205.9 26.5 %reshape.54 = bf16[8,512,1281]{2,1,0:T(8,128)(2,1)} reshape(bf16[5246976]{0:T(1024)(128)(2,1)} %reshape.53) | data formatting | bytes 20987904 | tf_op jit(solution)/shard_map/while/body/eval_jaxpr/vmap()/reshape | solution.py:20
  232.3 2.0 fusion.36
  235.4 4.1 fusion.37
  240.3 4.6 slice.43
  244.9 23.4 %reshape.53 = bf16[5246976]{0:T(1024)(128)(2,1)} reshape(bf16[8,655872]{1,0:T(8,128)(2,1)} %slice.43) | data formatting | bytes 20987904 | tf_op jit(solution)/shard_map/while
  268.3 26.5 %reshape.54 = bf16[8,512,1281]{2,1,0:T(8,128)(2,1)} reshape(bf16[5246976]{0:T(1024)(128)(2,1)} %reshape.53) | data formatting | bytes 20987904 | tf_op jit(solution)/shard_map/while/body/eval_jaxpr/vmap()/reshape | solution.py:20
  294.8 2.0 fusion.36
  297.8 4.1 fusion.37
  302.7 4.6 slice.43
  307.3 23.4 %reshape.53 = bf16[5246976]{0:T(1024)(128)(2,1)} reshape(bf16[8,655872]{1,0:T(8,128)(2,1)} %slice.43) | data formatting | bytes 20987904 | tf_op jit(solution)/shard_map/while
  330.7 26.5 %reshape.54 = bf16[8,512,1281]{2,1,0:T(8,128)(2,1)} reshape(bf16[5246976]{0:T(1024)(128)(2,1)} %reshape.53) | data formatting | bytes 20987904 | tf_op jit(solution)/shard_map/while/body/eval_jaxpr/vmap()/reshape | solution.py:20
  357.2 2.0 fusion.36
  360.3 4.1 fusion.37
  365.1 4.6 slice.43
  369.7 23.4 %reshape.53 = bf16[5246976]{0:T(1024)(128)(2,1)} reshape(bf16[8,655872]{1,0:T(8,128)(2,1)} %slice.43) | data formatting | bytes 20987904 | tf_op jit(solution)/shard_map/while
  393.1 26.5 %reshape.54 = bf16[8,512,1281]{2,1,0:T(8,128)(2,1)} reshape(bf16[5246976]{0:T(1024)(128)(2,1)} %reshape.53) | data formatting | bytes 20987904 | tf_op jit(solution)/shard_map/while/body/eval_jaxpr/vmap()/reshape | solution.py:20
  419.6 2.0 fusion.36
  422.7 4.1 fusion.37
  427.5 4.6 slice.43
  432.2 23.4 %reshape.53 = bf16[5246976]{0:T(1024)(128)(2,1)} reshape(bf16[8,655872]{1,0:T(8,128)(2,1)} %slice.43) | data formatting | bytes 20987904 | tf_op jit(solution)/shard_map/while
  455.5 26.5 %reshape.54 = bf16[8,512,1281]{2,1,0:T(8,128)(2,1)} reshape(bf16[5246976]{0:T(1024)(128)(2,1)} %reshape.53) | data formatting | bytes 20987904 | tf_op jit(solution)/shard_map/while/body/eval_jaxpr/vmap()/reshape | solution.py:20
  482.0 2.0 fusion.36
  485.1 4.1 fusion.37
  489.9 15.0 %reduce-scatter.2.cloned.1.call-done = f32[32,768]{1,0:T(8,128)} async-done(((f32[64,768]{1,0:T(8,128)}), f32[32,768]{1,0:T(8,128)}) %reduce-scatter.2.cloned.1.call-update) | async-done | bytes 98320 | tf_op jit(solution)/shard_map/reduce_scatter | solution.py:66
  (231 shorter events, 96.4 us)
Async XLA Ops:
  6.5 102.8 %all-gather.2.cloned.1.call-start = ((), (), s32[]{:S(2)}) async-start(), calls=%async_computation.1 | async-start | bytes 3342336 | tf_op jit(solution)/shard_map/all_gather | solution.py:63
  6.5 4.0 collective-permute-start
  7.8 497.1 %reduce-scatter.2.cloned.1.call-start = ((), (), s32[]{:S(2)}) async-start(), calls=%async_computation.2 | async-start | bytes 294912 | tf_op jit(solution)/shard_map/reduce_scatter | solution.py:66
  489.2 0.7 copy-start
Sparse Core Ops, SparseCore 0:
  9.6 47.9 all-gather.1
  490.1 14.8 reduce-scatter.1
where the time goes:
time: 514 us; the launch traced here: 512 us
  local copies, waits for them, and re-layouts  438 us (85%)
  matrix products  36.2 us (7%)
  waiting for transfers between devices  15 us (3%)
  between operations  13.5 us (3%)
  other arithmetic  6.53 us (1%)
    reshape x6, local copies, waits for them, and re-layouts, hankel_rows(): skewed = copies[:taps_len * (length + 1)].reshape(taps_len, length + 1)  159 us
    while x6, local copies, waits for them, and re-layouts  140 us
    gather x192, local copies, waits for them, and re-layouts  96.7 us
    slice x6, local copies, waits for them, and re-layouts, hankel_rows(): skewed = copies[:taps_len * (length + 1)].reshape(taps_len, length + 1)  27.8 us
    dot_general x6, matrix products, add_group(): jnp.einsum('rgl,glt->rgt', panel_part, stacked, preferred_element_type=jn...  24.4 us
    reduce_scatter x1, waiting for transfers between devices, per_device(): lax.psum_scatter(partial_value, 'sta', scatter_dimension=0, tiled=True)  15 us
    dot_general x6, matrix products, add_group(): energy = jnp.dot(squares, band_ones, precision=lax.Precision.HIGHEST)  11.8 us
  transfers between devices with their start and end apart: 3, of which 1 were waited for; matrix products, arithmetic and copies ran while one was open for 20% of the time, Pallas kernels for 0%

commit v1 on v0

v1 whole, which is shorter than its diff:
```python
import functools
import math

import jax
import jax.numpy as jnp
from jax import lax
from jax.experimental import pallas as pl
from jax.experimental.pallas import tpu as pltpu
from jax.sharding import PartitionSpec as P

CHANNELS = 96
LANES = 128
MAX_SHIFT = 256


def passed_along(shard, axis, by):
    count = lax.axis_size(axis)
    pairs = [(i, i + by) for i in range(count) if 0 <= i + by < count]
    return lax.ppermute(shard, axis, pairs)


def rolled_left(values, by, axis=1):
    width = values.shape[axis]
    return pltpu.roll(values, (width - by) % width, axis)


def corr_kernel(pieces, outs, shifts, live, rows, record, rim, *rest):
    banks, out_refs = rest[:pieces], rest[pieces : pieces + outs]
    ext, scale, taps_f32, hankel, acc = rest[pieces + outs :]
    chans, span = record.shape
    taps = banks[0].shape[2]
    per_bank = banks[0].shape[0]
    tmpl = per_bank * pieces
    width, long = 2 * span, span + taps
    blocks = taps // LANES
    overall = math.sqrt(taps / CHANNELS)

    for first in range(0, chans, 16):
        part = pl.ds(first, 16)
        both = jnp.concatenate([record[part, :], rim[part, :]], axis=1).astype(jnp.float32)
        ext[part, :] = both
        window, reach = both * both, 1
        while reach < taps:
            window = window + rolled_left(window, reach)
            reach *= 2
        scale[part, :] = lax.rsqrt(window[:, : scale.shape[1]] + 1e-06)

    for idx, bank in enumerate(banks):
        flat = bank[...].reshape(per_bank * chans, taps)
        for m in range(blocks):
            taps_f32[m, pl.ds(idx * per_bank * chans, per_bank * chans), :] = flat[
                :, m * LANES : (m + 1) * LANES
            ].astype(jnp.float32)

    acc[...] = jnp.zeros_like(acc)
    flip = 7 - lax.broadcasted_iota(jnp.int32, (8, long), 0)

    def add_channel(chan, carry):
        lag = shifts[chan]
        row = pltpu.roll(ext[pl.ds(chan, 1), :], lax.rem(width - lag, width), 1)[:, :long]
        span_scale = scale.shape[1]
        level = pltpu.roll(
            scale[pl.ds(chan, 1), :], lax.rem(span_scale - lag, span_scale), 1
        )[:, :span]
        eight = pltpu.roll(
            jnp.broadcast_to(row, (8, long)), long - 7, 1, stride=1, stride_axis=0
        )
        eight = jnp.take_along_axis(eight, flip, axis=0, mode="promise_in_bounds")
        base = jnp.concatenate([eight, rolled_left(eight, 8)], axis=0).astype(jnp.bfloat16)
        keep = hankel.shape[1]
        for group in range(LANES // 16):
            hankel[pl.ds(16 * group, 16), :] = rolled_left(base, 16 * group)[:, :keep]
        panel = jnp.concatenate(
            [taps_f32[m, pl.ds(chan, tmpl, stride=chans), :] for m in range(blocks)], axis=1
        )
        power = jnp.sum(panel * panel, axis=1, keepdims=True)
        weight = live[chan].astype(jnp.float32) * overall * lax.rsqrt(power + 1e-06)
        stacked = jnp.concatenate(
            [hankel[:, m * LANES : m * LANES + span] for m in range(blocks)], axis=0
        )
        product = jnp.dot(
            panel.astype(jnp.bfloat16), stacked, preferred_element_type=jnp.float32
        )
        acc[...] += product * level * weight
        return carry

    lax.fori_loop(0, chans, add_channel, 0)
    share = tmpl // outs
    for j, out in enumerate(out_refs):
        for p in range(share):
            out[pl.ds(p, 1), :] = acc[pl.ds(rows[j * share + p], 1), :]


def correlate(banks, record, rim, shifts, live, rows, outs):
    chans, span = record.shape
    per_bank, _, taps = banks[0].shape
    tmpl = per_bank * len(banks)
    smem = pl.BlockSpec(memory_space=pltpu.SMEM)
    vmem = pl.BlockSpec(memory_space=pltpu.VMEM)
    return pl.pallas_call(
        functools.partial(corr_kernel, len(banks), outs),
        out_shape=[jax.ShapeDtypeStruct((tmpl // outs, span), jnp.float32)] * outs,
        in_specs=[smem] * 3 + [vmem] * (2 + len(banks)),
        out_specs=[vmem] * outs,
        scratch_shapes=[
            pltpu.VMEM((chans, 2 * span), jnp.float32),
            pltpu.VMEM((chans, span + MAX_SHIFT), jnp.float32),
            pltpu.VMEM((taps // LANES, tmpl * chans, LANES), jnp.float32),
            pltpu.VMEM((LANES, span + taps - LANES), jnp.bfloat16),
            pltpu.VMEM((tmpl, span), jnp.float32),
        ],
        compiler_params=pltpu.CompilerParams(vmem_limit_bytes=40 * 1024 * 1024),
        cost_estimate=pl.CostEstimate(
            flops=2 * tmpl * chans * taps * span,
            bytes_accessed=2 * tmpl * chans * taps,
            transcendentals=0,
        ),
    )(shifts, live, rows, record, rim, *banks)


def padded(values, axis, multiple):
    extra = -values.shape[axis] % multiple
    if extra == 0:
        return values
    widths = [(0, extra if i == axis else 0) for i in range(values.ndim)]
    return jnp.pad(values, widths)


def per_device(record, templates, shifts, live_mask, plan):
    record, shifts, live_mask = (padded(v, 0, 16) for v in (record, shifts, live_mask))
    templates = padded(templates, 1, 16)
    groups = lax.axis_size("sta")
    own = lax.axis_index("sta")
    rim = passed_along(record, "tm", -1)
    bank_all = lax.all_gather(templates, "tm", axis=0, tiled=True)
    share = plan.shape[0] // groups
    rows = jnp.roll(plan, -own * share)
    halves = correlate([bank_all], record, rim, shifts, live_mask, rows, groups)
    total = halves[0]
    for by in range(1, groups):
        pairs = [(i, (i + by) % groups) for i in range(groups)]
        total = total + lax.ppermute(halves[by], "sta", pairs)
    return total


def solution(mesh):
    placed = (P("sta", "tm"), P("tm", "sta", None), P("sta"), P("sta"), P())
    return jax.shard_map(
        per_device, mesh=mesh, in_specs=placed, out_specs=P("sta", "tm"), check_vma=False
    )
```

time: 514 us -> 108 us (0.21)
  local copies, waits for them, and re-layouts: 438 us -> 4.16 us
  waiting for transfers between devices: 15 us -> 52.3 us
  matrix products: 36.2 us -> 0 us
  Pallas kernels: 0 us -> 33.3 us
    reshape x6 -> x0, local copies, waits for them, and re-layouts: 159 us -> none  [hankel_rows(): skewed = copies[:taps_len * (length + 1)].reshape(taps_len, length + 1)]
    while x6 -> x0, local copies, waits for them, and re-layouts: 140 us -> none
    gather x193 -> x0, local copies, waits for them, and re-layouts: 99.3 us -> none
    all_gather x1, waiting for transfers between devices: 0.02 us -> 46.9 us  [per_device(): bank_all = lax.all_gather(templates, 'tm', axis=0, tiled=True)]
    dot_general x12 -> x0, matrix products: 36.2 us -> none  [the longest x6 24.4 us: add_group(): jnp.einsum('rgl,glt->rgt', panel_part, stacked, preferred_element_type=jn...]
    pallas_call x0 -> x1, Pallas kernels: none -> 33.3 us  [correlate(): pl.pallas_call(functools.partial(corr_kernel, len(banks), outs), out_shap...]
    slice x6 -> x0, local copies, waits for them, and re-layouts: 27.8 us -> none  [hankel_rows(): skewed = copies[:taps_len * (length + 1)].reshape(taps_len, length + 1)]
    reduce_scatter x1 -> x0, waiting for transfers between devices: 15 us -> none  [per_device(): lax.psum_scatter(partial_value, 'sta', scatter_dimension=0, tiled=True)]
  transfers between devices with their start and end apart: 3 -> 3, of which waited for: 1 -> 3; matrix products, arithmetic and copies ran while one was open for 20% -> 1% of each run, Pallas kernels for 0% -> 0%
where the time goes in v1:
time: 108 us
  waiting for transfers between devices  52.3 us (48%)
  Pallas kernels  33.3 us (31%)
  between operations  13.4 us (12%)
  local copies, waits for them, and re-layouts  4.16 us (4%)
  starting transfers between devices  2.83 us (3%)
  other arithmetic  1.46 us (1%)
    all_gather x1, waiting for transfers between devices, per_device(): bank_all = lax.all_gather(templates, 'tm', axis=0, tiled=True)  46.9 us
    pallas_call x1, Pallas kernels, correlate(): pl.pallas_call(functools.partial(corr_kernel, len(banks), outs), out_shap...  33.3 us
    unnamed x8, local copies, waits for them, and re-layouts  4.08 us
    ppermute x1, waiting for transfers between devices, per_device(): total = total + lax.ppermute(halves[by], 'sta', pairs)  3.48 us
  transfers between devices with their start and end apart: 3, of which 3 were waited for; matrix products, arithmetic and copies ran while one was open for 1% of the time, Pallas kernels for 0%

profile of v1, /device:TPU:0, one launch (start us, length us, event | category | flops | bytes accessed | tf_op | source)
XLA Modules:
  0.0 107.5 jit_solution(17095504741029321957)
XLA Ops:
  6.5 0.0 all-gather.2.cloned.1.call-start
  6.5 0.7 all-gather.2.cloned.1.call-update
  7.3 1.3 %collective-permute-start = (bf16[48,768]{1,0:T(8,128)(2,1)}, bf16[48,768]{1,0:T(8,128)(2,1)S(1)}, u32[]{:S(2)}, u32[]{:S(2)}) collective-permute-start(bf16[48,768]{1,0:T(8,128)(2,1)} %record.1), channel_id=1, source_target_pairs={{1,0},{2,1},{3,2},{4,3},{5,4},{6,5},{7,6},{8,7},{9,8},{10,9},{11,1... | collective-permute-start | bytes 221192 | tf_op jit(solution)/shard_map/ppermute | solution.py:19
  8.6 0.8 pad_add_fusion
  9.4 0.1 dynamic_slice.4.rows
  9.5 1.2 %collective-permute-done.rim = bf16[48,768]{1,0:T(8,128)(2,1)S(1)} collective-permute-done((bf16[48,768]{1,0:T(8,128)(2,1)}, bf16[48,768]{1,0:T(8,128)(2,1)S(1)}, u32[]{:S(2)}, u32[]{:S(2)}) %collective-permute-start) | collective-permute-done | bytes 73760 | tf_op jit(solution)/shard_map/ppermute | solution.py:19
  10.6 46.9 %all-gather.2.cloned.1.call-done.rest_0_ = bf16[64,48,512]{2,1,0:T(8,128)(2,1)} async-done(((bf16[4,48,512]{2,1,0:T(8,128)(2,1)}), bf16[64,48,512]{2,1,0:T(8,128)(2,1)}) %all-gather.2.cloned.1.call-update) | async-done | bytes 3145744 | tf_op jit(solution)/shard_map/all_gather | solution.py:135
  57.6 0.0 copy-start
  57.6 1.9 %copy-done = bf16[64,48,512]{2,1,0:T(8,128)(2,1)S(1)} copy-done((bf16[64,48,512]{2,1,0:T(8,128)(2,1)S(1)}, bf16[64,48,512]{2,1,0:T(8,128)(2,1)}, u32[]{:S(2)}) %copy-start) | copy-done | bytes 3145752
  59.5 0.0 copy-start.1
  59.5 0.9 copy-done.1
  60.3 0.0 copy-start.2
  60.3 0.7 copy-done.2
  61.0 0.0 copy-start.3
  61.0 0.7 copy-done.3
  61.7 33.3 %shard_map.55 = (f32[32,768]{1,0:T(8,128)S(1)}, f32[32,768]{1,0:T(8,128)S(1)}) custom-call(s32[48]{0:T(128)S(1)} %copy-done.2, s32[48]{0:T(128)S(1)} %copy-done.3, s32[64]{0:T(128)S(1)} %dynamic_slice.4.rows, bf16[48,768]{1,0:T(8,128)(2,1)S(1)} %copy-done.1, bf16[48,768]{1,0:T(8,128)(2,1)S(1)} %collective-permute-done.rim, bf16[64,48,512]{2,1,0:T(8,128)(2,1)S(1)} %copy-done), custom_call_target="tpu_custom_call" | custom-call | flops 2415919104 | bytes 3145728 | tf_op jit(solution)/shard_map/pallas_call | solution.py:100
  95.0 1.5 %collective-permute-start.1 = (f32[32,768]{1,0:T(8,128)S(1)}, f32[32,768]{1,0:T(8,128)S(1)}, u32[]{:S(2)}, u32[]{:S(2)}) collective-permute-start(f32[32,768]{1,0:T(8,128)S(1)} %get-tuple-element.8), channel_id=1, source_target_pairs={{0,16},{16,0},{1,17},{17,1},{2,18},{18,2},{3,19},{19,3},{4,20},{20... | collective-permute-start | bytes 294920 | tf_op jit(solution)/shard_map/ppermute | solution.py:142
  96.5 3.5 %collective-permute-done.1 = f32[32,768]{1,0:T(8,128)S(1)} collective-permute-done((f32[32,768]{1,0:T(8,128)S(1)}, f32[32,768]{1,0:T(8,128)S(1)}, u32[]{:S(2)}, u32[]{:S(2)}) %collective-permute-start.1) | collective-permute-done | bytes 98336 | tf_op jit(solution)/shard_map/ppermute | solution.py:142
  100.0 0.7 add.15
Async XLA Ops:
  6.5 51.0 %all-gather.2.cloned.1.call-start = ((), (), s32[]{:S(2)}) async-start(), calls=%async_computation | async-start | bytes 3342336 | tf_op jit(solution)/shard_map/all_gather | solution.py:135
  7.3 3.4 %collective-permute-start = (bf16[48,768]{1,0:T(8,128)(2,1)}, bf16[48,768]{1,0:T(8,128)(2,1)S(1)}, u32[]{:S(2)}, u32[]{:S(2)}) collective-permute-start(bf16[48,768]{1,0:T(8,128)(2,1)} %record.1), channel_id=1, source_target_pairs={{1,0},{2,1},{3,2},{4,3},{5,4},{6,5},{7,6},{8,7},{9,8},{10,9},{11,1... | collective-permute-start | bytes 221192 | tf_op jit(solution)/shard_map/ppermute | solution.py:19
  57.6 1.9 %copy-start = (bf16[64,48,512]{2,1,0:T(8,128)(2,1)S(1)}, bf16[64,48,512]{2,1,0:T(8,128)(2,1)}, u32[]{:S(2)}) copy-start(bf16[64,48,512]{2,1,0:T(8,128)(2,1)} %all-gather.2.cloned.1.call-done.rest_0_) | copy-start | bytes 9437188
  59.5 0.9 copy-start.1
  60.3 0.7 copy-start.2
  61.0 0.7 copy-start.3
  95.0 5.0 %collective-permute-start.1 = (f32[32,768]{1,0:T(8,128)S(1)}, f32[32,768]{1,0:T(8,128)S(1)}, u32[]{:S(2)}, u32[]{:S(2)}) collective-permute-start(f32[32,768]{1,0:T(8,128)S(1)} %get-tuple-element.8), channel_id=1, source_target_pairs={{0,16},{16,0},{1,17},{17,1},{2,18},{18,2},{3,19},{19,3},{4,20},{20... | collective-permute-start | bytes 294920 | tf_op jit(solution)/shard_map/ppermute | solution.py:142
Sparse Core Ops, SparseCore 0:
  9.6 47.8 all-gather.1

commit v2 on v0

v2 whole, which is shorter than its diff:
```python
import functools
import math

import jax
import jax.numpy as jnp
import numpy as np
from jax import lax
from jax.experimental import pallas as pl
from jax.experimental.pallas import tpu as pltpu
from jax.sharding import PartitionSpec as P

LANES = 128
GROUP = 16
MAX_SHIFT = 256
SMEM = pl.BlockSpec(memory_space=pltpu.SMEM)


def rolled_left(values, by):
    width = values.shape[1]
    return pltpu.roll(values, (width - by) % width, 1)


def padded(values, axis, multiple):
    extra = -values.shape[axis] % multiple
    if extra == 0:
        return values
    widths = [(0, extra if i == axis else 0) for i in range(values.ndim)]
    return jnp.pad(values, widths)


def prep_kernel(shifts, *refs):
    segs = len(refs[:-4]) // 2
    blocks, (base, level, lines, flat) = refs[:-4], refs[-4:]
    chans, span = blocks[0].shape
    taps = base.shape[3] - span
    width, long = 2 * span, span + taps
    for seg in range(segs):
        for first in range(0, chans, GROUP):
            part = pl.ds(first, GROUP)
            both = jnp.concatenate(
                [blocks[2 * seg][part, :], blocks[2 * seg + 1][part, :]], axis=1
            ).astype(jnp.float32)
            window, reach = both * both, 1
            while reach < taps:
                window = window + rolled_left(window, reach)
                reach *= 2
            rate = lax.rsqrt(window + 1e-06)
            for m in range(width // LANES):
                cols = slice(m * LANES, (m + 1) * LANES)
                flat[m, pl.ds(8 * first + seg, GROUP, stride=8), :] = both[:, cols]
                flat[m, pl.ds(8 * first + segs + seg, GROUP, stride=8), :] = rate[:, cols]

    flip = 7 - lax.broadcasted_iota(jnp.int32, (8, long), 0)

    def one(chan, slot):
        lag = shifts[chan]
        rows = pl.ds(pl.multiple_of(chan * 8, 8), 8)
        held = jnp.concatenate([flat[m, rows, :] for m in range(width // LANES)], axis=1)
        lines[slot] = pltpu.roll(held, lax.rem(width - lag, width), 1)[:, :long]
        for seg in range(segs):
            level[seg, pl.ds(chan, 1), :] = lines[slot, pl.ds(segs + seg, 1), :span]
            eight = pltpu.roll(
                jnp.broadcast_to(lines[slot, pl.ds(seg, 1), :], (8, long)),
                long - 7,
                1,
                stride=1,
                stride_axis=0,
            )
            eight = jnp.take_along_axis(eight, flip, axis=0, mode="promise_in_bounds")
            base[seg, chan] = jnp.concatenate([eight, rolled_left(eight, 8)], axis=0).astype(
                jnp.bfloat16
            )

    unroll = 4

    def body(step, carry):
        for u in range(unroll):
            one(step * unroll + u, u)
        return carry

    lax.fori_loop(0, chans // unroll, body, 0)


def prepare(shifts, blocks, taps):
    segs = len(blocks) // 2
    chans, span = blocks[0].shape
    whole = [pl.BlockSpec((chans, span), lambda i: (0, 0))] * len(blocks)
    return pl.pallas_call(
        prep_kernel,
        grid=(1,),
        out_shape=[
            jax.ShapeDtypeStruct((segs, chans, 16, span + taps), jnp.bfloat16),
            jax.ShapeDtypeStruct((segs, chans, span), jnp.float32),
        ],
        in_specs=[SMEM] + whole,
        out_specs=[
            pl.BlockSpec((segs, chans, 16, span + taps), lambda i: (0, 0, 0, 0)),
            pl.BlockSpec((segs, chans, span), lambda i: (0, 0, 0)),
        ],
        scratch_shapes=[
            pltpu.VMEM((4, 8, span + taps), jnp.float32),
            pltpu.VMEM((2 * span // LANES, chans * 8, LANES), jnp.float32),
        ],
        compiler_params=pltpu.CompilerParams(vmem_limit_bytes=40 * 1024 * 1024),
        cost_estimate=pl.CostEstimate(flops=1, bytes_accessed=10**7, transcendentals=0),
    )(shifts, *blocks)


def corr_kernel(pieces, first, overall, live, base, level, *refs):
    banks, (before, total, flat) = refs[:pieces], refs[pieces:]
    per, group, taps = banks[0].shape
    tmpl = per * pieces
    segs, span = level.shape[0], level.shape[2]
    parts, half = taps // LANES, 2 * LANES
    step = pl.program_id(0)

    @pl.when(step == 0)
    def _():
        if before is None:
            total[...] = jnp.zeros_like(total)
        else:
            total[...] = before[...]

    for idx, bank in enumerate(banks):
        rows = bank[...].reshape(per * group, taps).astype(jnp.float32)
        for m in range(parts):
            flat[m, pl.ds(idx * per * group, per * group), :] = rows[
                :, m * LANES : (m + 1) * LANES
            ]

    def one(chan):
        panel = jnp.concatenate(
            [flat[m, pl.ds(chan, tmpl, stride=group), :] for m in range(parts)], axis=1
        )
        power = jnp.sum(panel * panel, axis=1, keepdims=True)
        alive = live[first + step * group + chan].astype(jnp.float32)
        weight = alive * overall * lax.rsqrt(power + 1e-06)
        panel = panel.astype(jnp.bfloat16)
        stacked = jnp.concatenate(
            [panel[:, k * half : (k + 1) * half] for k in range(taps // half)], axis=0
        )
        for seg in range(segs):
            rows = base[seg, chan]
            sheet = jnp.concatenate(
                [rolled_left(rows, 16 * g) for g in range(LANES // 16)], axis=0
            )
            tall = span + taps - half
            hankel = jnp.concatenate([sheet[:, :tall], sheet[:, LANES : LANES + tall]], axis=0)
            product = jnp.dot(stacked, hankel, preferred_element_type=jnp.float32)
            found = product[:tmpl, :span]
            for k in range(1, taps // half):
                found = found + product[k * tmpl : (k + 1) * tmpl, k * half : k * half + span]
            total[seg] += found * level[seg, pl.ds(chan, 1), :] * weight

    unroll = 8

    def body(trip, carry):
        for u in range(unroll):
            one(trip * unroll + u)
        return carry

    lax.fori_loop(0, group // unroll, body, 0)


def correlate(live, base, level, banks, before, first, count, overall):
    segs, chans, _, long = base.shape
    span = level.shape[2]
    per, _, taps = banks[0].shape
    tmpl = per * len(banks)
    at = first // GROUP
    full = (segs, tmpl, span)
    in_specs = [
        SMEM,
        pl.BlockSpec((segs, GROUP, 16, long), lambda i: (0, at + i, 0, 0)),
        pl.BlockSpec((segs, GROUP, span), lambda i: (0, at + i, 0)),
    ]
    for bank in banks:
        skip = at if bank.shape[1] == chans else 0
        in_specs.append(pl.BlockSpec((per, GROUP, taps), lambda i, s=skip: (0, s + i, 0)))
    args = [live, base, level, *banks]
    kernel = functools.partial(corr_kernel, len(banks), first, overall)
    if before is None:
        inner = kernel

        def kernel(live, base, level, *refs):
            inner(live, base, level, *refs[: len(banks)], None, *refs[len(banks) :])
    else:
        in_specs.append(pl.BlockSpec(full, lambda i: (0, 0, 0)))
        args.append(before)
    return pl.pallas_call(
        kernel,
        grid=(count // GROUP,),
        out_shape=jax.ShapeDtypeStruct(full, jnp.float32),
        in_specs=in_specs,
        out_specs=pl.BlockSpec(full, lambda i: (0, 0, 0)),
        scratch_shapes=[pltpu.VMEM((taps // LANES, tmpl * GROUP, LANES), jnp.float32)],
        compiler_params=pltpu.CompilerParams(vmem_limit_bytes=40 * 1024 * 1024),
        cost_estimate=pl.CostEstimate(
            flops=2 * tmpl * count * taps * span * segs,
            bytes_accessed=10**7,
            transcendentals=0,
        ),
    )(*args)


def finish_kernel(counts, rows, *refs):
    parts, (out, both) = refs[:-2], refs[-2:]
    tmpl = parts[0].shape[0]
    start = 0
    for src, count in enumerate(counts):
        value = parts[start][...]
        for ref in parts[start + 1 : start + count]:
            value = value + ref[...]
        both[pl.ds(src * tmpl, tmpl), :] = value
        start += count
    for p in range(out.shape[0]):
        out[pl.ds(p, 1), :] = both[pl.ds(rows[p], 1), :]


def finish(rows, groups):
    parts = [part for group in groups for part in group]
    shape = parts[0].shape
    spec = pl.BlockSpec(shape, lambda i: (0, 0))
    return pl.pallas_call(
        functools.partial(finish_kernel, [len(group) for group in groups]),
        grid=(1,),
        out_shape=jax.ShapeDtypeStruct((rows.shape[0], shape[1]), jnp.float32),
        in_specs=[SMEM] + [spec] * len(parts),
        out_specs=pl.BlockSpec((rows.shape[0], shape[1]), lambda i: (0, 0)),
        scratch_shapes=[pltpu.VMEM((len(groups) * shape[0], shape[1]), jnp.float32)],
        compiler_params=pltpu.CompilerParams(vmem_limit_bytes=40 * 1024 * 1024),
    )(rows, *parts)


def crossed(values, bit):
    return lax.ppermute(values, "tm", [(i, i ^ bit) for i in range(lax.axis_size("tm"))])


def per_device(record, templates, shifts, live_mask, plan):
    count, groups = lax.axis_size("tm"), lax.axis_size("sta")
    per, own_chans, taps = templates.shape
    overall = math.sqrt(taps / (own_chans * groups))
    record, shifts, live_mask = (padded(v, 0, GROUP) for v in (record, shifts, live_mask))
    templates = padded(templates, 1, GROUP)
    chans = record.shape[0]
    far, shared = count // 2, count // 4
    others = [bit for bit in (1 << e for e in range(count.bit_length() - 4, -1, -1))]

    cuts = [0, chans - GROUP, chans] if chans > GROUP else [0, chans]
    spans = list(zip(cuts[:-1], cuts[1:]))
    chunked = {far: [crossed(templates[:, a:b], far) for a, b in spans]}
    whole = {0: templates}
    for bit in others:
        for mask in list(whole):
            whole[mask | bit] = crossed(whole[mask], bit)
        for mask in list(chunked):
            chunked[mask | bit] = [crossed(part, bit) for part in chunked[mask]]

    after = [(i, i - 1) for i in range(1, count)]
    blocks = [
        record,
        lax.ppermute(record, "tm", after),
        crossed(record, shared),
        lax.ppermute(record, "tm", [(i, j ^ shared) for i, j in after]),
    ]
    base, level = prepare(shifts, blocks, taps)

    total = None
    for idx, (a, b) in enumerate(spans):
        banks = list(whole.values()) + [chunked[mask][idx] for mask in chunked]
        total = correlate(live_mask, base, level, banks, total, a, b - a, overall)

    near, away = [total[0]], []
    for by in range(groups):
        if by:
            pairs = [(i, (i + by) % groups) for i in range(groups)]
            near.append(lax.ppermute(total[0], "sta", pairs))
        pairs = [
            (i * count + j, (i + by) % groups * count + (j ^ shared))
            for i in range(groups)
            for j in range(count)
        ]
        away.append(lax.ppermute(total[1], ("sta", "tm"), pairs))

    masks = list(whole) + list(chunked)
    places = np.zeros(count, np.int32)
    for place, mask in enumerate(masks):
        places[mask] = place
        places[mask | shared] = place + len(masks)
    mine = lax.axis_index("tm")
    share = plan.shape[0] // groups
    slots = lax.dynamic_slice_in_dim(plan, lax.axis_index("sta") * share, share)
    rows = jnp.asarray(places)[(slots // per) ^ mine] * per + slots % per
    return finish(rows, [near, away])


def solution(mesh):
    placed = (P("sta", "tm"), P("tm", "sta", None), P("sta"), P("sta"), P())
    return jax.shard_map(
        per_device, mesh=mesh, in_specs=placed, out_specs=P("sta", "tm"), check_vma=False
    )
```

time: 514 us -> 66.3 us (0.13)
  local copies, waits for them, and re-layouts: 438 us -> 6.25 us
  matrix products: 36.2 us -> 0 us
  starting transfers between devices: 1.32 us -> 22.4 us
  Pallas kernels: 0 us -> 20.9 us
  between operations: 13.5 us -> 0.14 us
  other arithmetic: 6.53 us -> 0.82 us
    reshape x6 -> x0, local copies, waits for them, and re-layouts: 159 us -> none  [hankel_rows(): skewed = copies[:taps_len * (length + 1)].reshape(taps_len, length + 1)]
    while x6 -> x0, local copies, waits for them, and re-layouts: 140 us -> none
    gather x193 -> x1, local copies, waits for them, and re-layouts: 99.3 us -> 1.35 us  [per_device(): rows = jnp.asarray(places)[slots // per ^ mine] * per + slots % per]
    dot_general x12 -> x0, matrix products: 36.2 us -> none  [the longest x6 24.4 us: add_group(): jnp.einsum('rgl,glt->rgt', panel_part, stacked, preferred_element_type=jn...]
    slice x6 -> x2, local copies, waits for them, and re-layouts: 27.8 us -> 1.76 us  [per_device(): chunked = {far: [crossed(templates[:, a:b], far) for a, b in spans]}]
    ppermute x1 -> x17, starting transfers between devices: 1.28 us -> 22.4 us  [the longest x12 16.3 us: crossed(): lax.ppermute(values, 'tm', [(i, i ^ bit) for i in range(lax.axis_size('tm...]
    pallas_call x0 -> x4, Pallas kernels: none -> 20.9 us  [the longest x2 12.8 us: correlate(): pl.pallas_call(kernel, grid=(count // GROUP,), out_shape=jax.ShapeDtypeSt...]
    ppermute x1 -> x17, waiting for transfers between devices: 0.01 us -> 15.5 us  [the longest x12 7.99 us: crossed(): lax.ppermute(values, 'tm', [(i, i ^ bit) for i in range(lax.axis_size('tm...]
  transfers between devices with their start and end apart: 3 -> 17, of which waited for: 1 -> 4; matrix products, arithmetic and copies ran while one was open for 20% -> 5% of each run, Pallas kernels for 0% -> 23%
where the time goes in v2:
time: 66.3 us; the launch traced here: 66 us
  starting transfers between devices  22.4 us (34%)
  Pallas kernels  20.9 us (32%)
  waiting for transfers between devices  15.5 us (23%)
  local copies, waits for them, and re-layouts  6.25 us (9%)
  other arithmetic  0.82 us (1%)
    ppermute x12, starting transfers between devices, crossed(): lax.ppermute(values, 'tm', [(i, i ^ bit) for i in range(lax.axis_size('tm...  16.3 us
    pallas_call x2, Pallas kernels, correlate(): pl.pallas_call(kernel, grid=(count // GROUP,), out_shape=jax.ShapeDtypeSt...  12.8 us
    ppermute x12, waiting for transfers between devices, crossed(): lax.ppermute(values, 'tm', [(i, i ^ bit) for i in range(lax.axis_size('tm...  7.99 us
    pallas_call x1, Pallas kernels, prepare(): pl.pallas_call(prep_kernel, grid=(1,), out_shape=[jax.ShapeDtypeStruct((s...  6.78 us
    ppermute x1, waiting for transfers between devices, per_device(): near.append(lax.ppermute(total[0], 'sta', pairs))  5.59 us
    unnamed x10, local copies, waits for them, and re-layouts  3.13 us
    ppermute x2, starting transfers between devices, per_device(): away.append(lax.ppermute(total[1], ('sta', 'tm'), pairs))  3.01 us
    ppermute x1, waiting for transfers between devices, per_device(): lax.ppermute(record, 'tm', [(i, j ^ shared) for i, j in after])  1.9 us
  transfers between devices with their start and end apart: 17, of which 4 were waited for; matrix products, arithmetic and copies ran while one was open for 5% of the time, Pallas kernels for 23%

profile of v2, /device:TPU:0, one launch (start us, length us, event | category | flops | bytes accessed | tf_op | source)
XLA Modules:
  0.0 66.0 jit_solution(18230495651342615809)
XLA Ops:
  0.0 0.9 %slice.15 = bf16[4,32,512]{2,1,0:T(8,128)(2,1)S(1)} slice(bf16[4,48,512]{2,1,0:T(8,128)(2,1)} %refs_0_.5), slice={[0:4], [0:32], [0:512]} | slice | bytes 262144 | tf_op jit(solution)/shard_map/slice | solution.py:251
  0.9 4.1 %collective-permute-start.10 = (bf16[4,32,512]{2,1,0:T(8,128)(2,1)S(1)}, bf16[4,32,512]{2,1,0:T(8,128)(2,1)S(1)}, u32[]{:S(2)}, u32[]{:S(2)}) collective-permute-start(bf16[4,32,512]{2,1,0:T(8,128)(2,1)S(1)} %slice.15), channel_id=1, source_target_pairs={{0,8},{1,9},{2,10},{3,11},{4,12},{5,13},{6,14},{7,15},{8,0},{9,1},... | collective-permute-start | bytes 393224 | tf_op jit(solution)/shard_map/ppermute | solution.py:236
  5.0 1.5 %collective-permute-start.3 = (bf16[4,48,512]{2,1,0:T(8,128)(2,1)}, bf16[4,48,512]{2,1,0:T(8,128)(2,1)S(1)}, u32[]{:S(2)}, u32[]{:S(2)}) collective-permute-start(bf16[4,48,512]{2,1,0:T(8,128)(2,1)} %refs_0_.5), channel_id=1, source_target_pairs={{0,2},{1,3},{2,0},{3,1},{4,6},{5,7},{6,4},{7,5},{8,10},{9,11},{10,... | collective-permute-start | bytes 589832 | tf_op jit(solution)/shard_map/ppermute | solution.py:236
  6.5 4.8 %collective-permute-done.10.refs_4_ = bf16[4,32,512]{2,1,0:T(8,128)(2,1)S(1)} collective-permute-done((bf16[4,32,512]{2,1,0:T(8,128)(2,1)S(1)}, bf16[4,32,512]{2,1,0:T(8,128)(2,1)S(1)}, u32[]{:S(2)}, u32[]{:S(2)}) %collective-permute-start.10) | collective-permute-done | bytes 131104 | tf_op jit(solution)/shard_map/ppermute | solution.py:236
  11.3 1.6 %collective-permute-start.11 = (bf16[4,32,512]{2,1,0:T(8,128)(2,1)S(1)}, bf16[4,32,512]{2,1,0:T(8,128)(2,1)S(1)}, u32[]{:S(2)}, u32[]{:S(2)}) collective-permute-start(bf16[4,32,512]{2,1,0:T(8,128)(2,1)S(1)} %collective-permute-done.10.refs_4_), channel_id=1, source_target_pairs={{0,2},{1,3},{2,0},{3,1},{4,6},{5,7},{6,4},{7,5},{8,10},{9,11},{10,... | collective-permute-start | bytes 393224 | tf_op jit(solution)/shard_map/ppermute | solution.py:236
  12.9 1.3 %collective-permute-start = (bf16[48,768]{1,0:T(8,128)(2,1)}, bf16[48,768]{1,0:T(8,128)(2,1)S(1)}, u32[]{:S(2)}, u32[]{:S(2)}) collective-permute-start(bf16[48,768]{1,0:T(8,128)(2,1)} %refs_0_.3), channel_id=1, source_target_pairs={{1,0},{2,1},{3,2},{4,3},{5,4},{6,5},{7,6},{8,7},{9,8},{10,9},{11,1... | collective-permute-start | bytes 221192 | tf_op jit(solution)/shard_map/ppermute | solution.py:262
  14.2 1.4 %collective-permute-start.1 = (bf16[48,768]{1,0:T(8,128)(2,1)}, bf16[48,768]{1,0:T(8,128)(2,1)S(1)}, u32[]{:S(2)}, u32[]{:S(2)}) collective-permute-start(bf16[48,768]{1,0:T(8,128)(2,1)} %refs_0_.3), channel_id=1, source_target_pairs={{0,4},{1,5},{2,6},{3,7},{4,0},{5,1},{6,2},{7,3},{8,12},{9,13},{10,... | collective-permute-start | bytes 221192 | tf_op jit(solution)/shard_map/ppermute | solution.py:236
  15.6 0.8 %slice.14 = bf16[4,16,512]{2,1,0:T(8,128)(2,1)S(1)} slice(bf16[4,48,512]{2,1,0:T(8,128)(2,1)} %refs_0_.5), slice={[0:4], [32:48], [0:512]} | slice | bytes 131072 | tf_op jit(solution)/shard_map/slice | solution.py:251
  16.4 3.4 %collective-permute-start.6 = (bf16[4,16,512]{2,1,0:T(8,128)(2,1)S(1)}, bf16[4,16,512]{2,1,0:T(8,128)(2,1)S(1)}, u32[]{:S(2)}, u32[]{:S(2)}) collective-permute-start(bf16[4,16,512]{2,1,0:T(8,128)(2,1)S(1)} %slice.14), channel_id=1, source_target_pairs={{0,8},{1,9},{2,10},{3,11},{4,12},{5,13},{6,14},{7,15},{8,0},{9,1},... | collective-permute-start | bytes 196616 | tf_op jit(solution)/shard_map/ppermute | solution.py:236
  19.8 3.2 %collective-permute-done.6.refs_4_ = bf16[4,16,512]{2,1,0:T(8,128)(2,1)S(1)} collective-permute-done((bf16[4,16,512]{2,1,0:T(8,128)(2,1)S(1)}, bf16[4,16,512]{2,1,0:T(8,128)(2,1)S(1)}, u32[]{:S(2)}, u32[]{:S(2)}) %collective-permute-start.6) | collective-permute-done | bytes 65568 | tf_op jit(solution)/shard_map/ppermute | solution.py:236
  23.0 1.3 %collective-permute-start.2 = (bf16[48,768]{1,0:T(8,128)(2,1)}, bf16[48,768]{1,0:T(8,128)(2,1)S(1)}, u32[]{:S(2)}, u32[]{:S(2)}) collective-permute-start(bf16[48,768]{1,0:T(8,128)(2,1)} %refs_0_.3), channel_id=1, source_target_pairs={{1,4},{2,5},{3,6},{4,7},{5,0},{6,1},{7,2},{8,3},{9,12},{10,13},{11... | collective-permute-start | bytes 221192 | tf_op jit(solution)/shard_map/ppermute | solution.py:264
  24.2 0.0 collective-permute-done.refs_1_
  24.2 2.1 %collective-permute-start.4 = (bf16[4,48,512]{2,1,0:T(8,128)(2,1)}, bf16[4,48,512]{2,1,0:T(8,128)(2,1)S(1)}, u32[]{:S(2)}, u32[]{:S(2)}) collective-permute-start(bf16[4,48,512]{2,1,0:T(8,128)(2,1)} %refs_0_.5), channel_id=1, source_target_pairs={{0,1},{1,0},{2,3},{3,2},{4,5},{5,4},{6,7},{7,6},{8,9},{9,8},{10,11... | collective-permute-start | bytes 589832 | tf_op jit(solution)/shard_map/ppermute | solution.py:236
  26.4 0.0 collective-permute-done.1.refs_2_
  26.4 0.1 collective-permute-start.12
  26.5 0.0 collective-permute-done.3.refs_1_
  26.5 0.4 collective-permute-start.5
  26.9 0.0 collective-permute-done.11.refs_5_
  26.9 0.1 collective-permute-start.13
  27.0 0.7 %compare_select_fusion = s32[32]{0:T(128)S(1)} fusion(s32[]{:T(128)S(6)} %axis_index.25, s32[64]{0:T(128)} %param.10, s32[]{:T(128)S(6)} %select_n.18), kind=kLoop, calls=%fused_computation.4 | loop fusion | flops 608 | bytes 264 | tf_op jit(solution)/shard_map/select_n | solution.py:293
  27.7 1.9 %collective-permute-done.2.refs_3_ = bf16[48,768]{1,0:T(8,128)(2,1)S(1)} collective-permute-done((bf16[48,768]{1,0:T(8,128)(2,1)}, bf16[48,768]{1,0:T(8,128)(2,1)S(1)}, u32[]{:S(2)}, u32[]{:S(2)}) %collective-permute-start.2) | collective-permute-done | bytes 73760 | tf_op jit(solution)/shard_map/ppermute | solution.py:264
  29.6 1.1 %collective-permute-start.7 = (bf16[4,16,512]{2,1,0:T(8,128)(2,1)S(1)}, bf16[4,16,512]{2,1,0:T(8,128)(2,1)S(1)}, u32[]{:S(2)}, u32[]{:S(2)}) collective-permute-start(bf16[4,16,512]{2,1,0:T(8,128)(2,1)S(1)} %collective-permute-done.6.refs_4_), channel_id=1, source_target_pairs={{0,2},{1,3},{2,0},{3,1},{4,6},{5,7},{6,4},{7,5},{8,10},{9,11},{10,... | collective-permute-start | bytes 196616 | tf_op jit(solution)/shard_map/ppermute | solution.py:236
  30.7 1.4 %gather_fusion = s32[32]{0:T(128)S(1)} fusion(s32[16]{0:T(128)} %constant.48.clone, s32[1024]{0:T(1024)S(1)} %pad_clamp_fusion), kind=kCustom, calls=%fused_computation | custom fusion | bytes 384 | tf_op jit(solution)/shard_map/gather | solution.py:293
  32.1 0.9 %copy-done.1 = bf16[48,768]{1,0:T(8,128)(2,1)S(1)} copy-done((bf16[48,768]{1,0:T(8,128)(2,1)S(1)}, bf16[48,768]{1,0:T(8,128)(2,1)}, u32[]{:S(2)}) %copy-start.1) | copy-done | bytes 73752
  33.0 0.7 copy-done.2
  33.6 6.8 %shard_map.64 = (bf16[2,48,16,1280]{3,2,1,0:T(8,128)(2,1)S(1)}, f32[2,48,768]{2,1,0:T(8,128)S(1)}) custom-call(s32[48]{0:T(128)S(1)} %copy-done.2, bf16[48,768]{1,0:T(8,128)(2,1)S(1)} %copy-done.1, bf16[48,768]{1,0:T(8,128)(2,1)S(1)} %collective-permute-done.refs_1_, bf16[48,768]{1,0:T(8,128)(2,1)S(1)} %collective-permute-done.1.refs_2_, ...), custom_call_target="tpu_custom_call" | custom-call | flops 1 | bytes 10000000 | tf_op jit(solution)/shard_map/pallas_call | solution.py:88
  40.4 0.0 collective-permute-done.7.refs_5_
  40.4 0.1 collective-permute-start.8
  40.5 0.0 collective-permute-done.4.refs_2_
  40.5 0.5 collective-permute-start.9
  41.0 0.0 collective-permute-done.12.refs_6_
  41.0 0.0 collective-permute-done.13.refs_7_
  41.0 0.0 collective-permute-done.5.refs_3_
  41.0 0.0 copy-start
  41.0 0.9 %copy-done = bf16[4,48,512]{2,1,0:T(8,128)(2,1)S(1)} copy-done((bf16[4,48,512]{2,1,0:T(8,128)(2,1)S(1)}, bf16[4,48,512]{2,1,0:T(8,128)(2,1)}, u32[]{:S(2)}) %copy-start) | copy-done | bytes 196632
  41.9 0.7 copy-done.3
  42.6 8.4 %shard_map.65.refs_8_ = f32[2,32,768]{2,1,0:T(8,128)S(1)} custom-call(s32[48]{0:T(128)S(1)} %copy-done.3, bf16[2,48,16,1280]{3,2,1,0:T(8,128)(2,1)S(1)} %get-tuple-element.7.base, f32[2,48,768]{2,1,0:T(8,128)S(1)} %get-tuple-element.8.level, bf16[4,48,512]{2,1,0:T(8,128)(2,1)S(1)} %copy-done, bf16[4,48,512]{2,1,0:T(8,128)(2,1)S(1)} %collective-permute-done.3.refs_1_, ...), custom_call_target="tpu_custom_call" | custom-call | flops 1610612736 | bytes 10000000 | tf_op jit(solution)/shard_map/pallas_call | solution.py:190
  51.0 0.0 copy-start.4
  51.0 0.0 collective-permute-done.8.refs_6_
  51.0 0.0 collective-permute-done.9.refs_7_
  51.1 4.4 %shard_map.66 = f32[2,32,768]{2,1,0:T(8,128)S(1)} custom-call(s32[48]{0:T(128)S(1)} %copy-done.3, bf16[2,48,16,1280]{3,2,1,0:T(8,128)(2,1)S(1)} %get-tuple-element.7.base, f32[2,48,768]{2,1,0:T(8,128)S(1)} %get-tuple-element.8.level, bf16[4,48,512]{2,1,0:T(8,128)(2,1)S(1)} %copy-done, bf16[4,48,512]{2,1,0:T(8,128)(2,1)S(1)} %collective-permute-done.3.refs_1_, ...), custom_call_target="tpu_custom_call" | custom-call | flops 805306368 | bytes 10000000 | tf_op jit(solution)/shard_map/pallas_call | solution.py:190
  55.5 0.1 collective-permute-start.15
  55.5 2.9 %collective-permute-start.16 = (f32[32,768]{1,0:T(8,128)S(1)}, f32[32,768]{1,0:T(8,128)S(1)}, u32[]{:S(2)}, u32[]{:S(2)}) collective-permute-start(f32[32,768]{1,0:T(8,128)S(1)} %get-tuple-element.9), channel_id=1, source_target_pairs={{0,20},{1,21},{2,22},{3,23},{4,16},{5,17},{6,18},{7,19},{8,28},{9,... | collective-permute-start | bytes 294920 | tf_op jit(solution)/shard_map/ppermute | solution.py:283
  58.5 0.5 collective-permute-start.14
  59.0 0.1 fusion.rows
  59.1 5.6 %collective-permute-done.14.refs_1_ = f32[32,768]{1,0:T(8,128)S(1)} collective-permute-done((f32[32,768]{1,0:T(8,128)S(1)}, f32[32,768]{1,0:T(8,128)S(1)}, u32[]{:S(2)}, u32[]{:S(2)}) %collective-permute-start.14) | collective-permute-done | bytes 98336 | tf_op jit(solution)/shard_map/ppermute | solution.py:277
  64.7 0.0 collective-permute-done.16.refs_3_
  64.7 1.3 %shard_map.67 = f32[32,768]{1,0:T(8,128)} custom-call(s32[32]{0:T(128)S(1)} %fusion.rows, f32[32,768]{1,0:T(8,128)S(1)} %get-tuple-element.10.refs_0_, f32[32,768]{1,0:T(8,128)S(1)} %collective-permute-done.14.refs_1_, f32[32,768]{1,0:T(8,128)S(1)} %collective-permute-done.15.refs_2_, f32[32,768]{1,0:T(8,128)S(1)} %collective-permute-done.16.refs_3_), custom_call_target="tpu_custom_call" | custom-call | tf_op jit(solution)/shard_map/pallas_call | solution.py:224
  (7 shorter events, 0.0 us)
Async XLA Ops:
  0.9 10.4 %collective-permute-start.10 = (bf16[4,32,512]{2,1,0:T(8,128)(2,1)S(1)}, bf16[4,32,512]{2,1,0:T(8,128)(2,1)S(1)}, u32[]{:S(2)}, u32[]{:S(2)}) collective-permute-start(bf16[4,32,512]{2,1,0:T(8,128)(2,1)S(1)} %slice.15), channel_id=1, source_target_pairs={{0,8},{1,9},{2,10},{3,11},{4,12},{5,13},{6,14},{7,15},{8,0},{9,1},... | collective-permute-start | bytes 393224 | tf_op jit(solution)/shard_map/ppermute | solution.py:236
  5.0 21.4 %collective-permute-start.3 = (bf16[4,48,512]{2,1,0:T(8,128)(2,1)}, bf16[4,48,512]{2,1,0:T(8,128)(2,1)S(1)}, u32[]{:S(2)}, u32[]{:S(2)}) collective-permute-start(bf16[4,48,512]{2,1,0:T(8,128)(2,1)} %refs_0_.5), channel_id=1, source_target_pairs={{0,2},{1,3},{2,0},{3,1},{4,6},{5,7},{6,4},{7,5},{8,10},{9,11},{10,... | collective-permute-start | bytes 589832 | tf_op jit(solution)/shard_map/ppermute | solution.py:236
  11.3 15.6 %collective-permute-start.11 = (bf16[4,32,512]{2,1,0:T(8,128)(2,1)S(1)}, bf16[4,32,512]{2,1,0:T(8,128)(2,1)S(1)}, u32[]{:S(2)}, u32[]{:S(2)}) collective-permute-start(bf16[4,32,512]{2,1,0:T(8,128)(2,1)S(1)} %collective-permute-done.10.refs_4_), channel_id=1, source_target_pairs={{0,2},{1,3},{2,0},{3,1},{4,6},{5,7},{6,4},{7,5},{8,10},{9,11},{10,... | collective-permute-start | bytes 393224 | tf_op jit(solution)/shard_map/ppermute | solution.py:236
  12.9 11.3 %collective-permute-start = (bf16[48,768]{1,0:T(8,128)(2,1)}, bf16[48,768]{1,0:T(8,128)(2,1)S(1)}, u32[]{:S(2)}, u32[]{:S(2)}) collective-permute-start(bf16[48,768]{1,0:T(8,128)(2,1)} %refs_0_.3), channel_id=1, source_target_pairs={{1,0},{2,1},{3,2},{4,3},{5,4},{6,5},{7,6},{8,7},{9,8},{10,9},{11,1... | collective-permute-start | bytes 221192 | tf_op jit(solution)/shard_map/ppermute | solution.py:262
  14.2 12.2 %collective-permute-start.1 = (bf16[48,768]{1,0:T(8,128)(2,1)}, bf16[48,768]{1,0:T(8,128)(2,1)S(1)}, u32[]{:S(2)}, u32[]{:S(2)}) collective-permute-start(bf16[48,768]{1,0:T(8,128)(2,1)} %refs_0_.3), channel_id=1, source_target_pairs={{0,4},{1,5},{2,6},{3,7},{4,0},{5,1},{6,2},{7,3},{8,12},{9,13},{10,... | collective-permute-start | bytes 221192 | tf_op jit(solution)/shard_map/ppermute | solution.py:236
  16.4 6.6 %collective-permute-start.6 = (bf16[4,16,512]{2,1,0:T(8,128)(2,1)S(1)}, bf16[4,16,512]{2,1,0:T(8,128)(2,1)S(1)}, u32[]{:S(2)}, u32[]{:S(2)}) collective-permute-start(bf16[4,16,512]{2,1,0:T(8,128)(2,1)S(1)} %slice.14), channel_id=1, source_target_pairs={{0,8},{1,9},{2,10},{3,11},{4,12},{5,13},{6,14},{7,15},{8,0},{9,1},... | collective-permute-start | bytes 196616 | tf_op jit(solution)/shard_map/ppermute | solution.py:236
  23.0 6.7 %collective-permute-start.2 = (bf16[48,768]{1,0:T(8,128)(2,1)}, bf16[48,768]{1,0:T(8,128)(2,1)S(1)}, u32[]{:S(2)}, u32[]{:S(2)}) collective-permute-start(bf16[48,768]{1,0:T(8,128)(2,1)} %refs_0_.3), channel_id=1, source_target_pairs={{1,4},{2,5},{3,6},{4,7},{5,0},{6,1},{7,2},{8,3},{9,12},{10,13},{11... | collective-permute-start | bytes 221192 | tf_op jit(solution)/shard_map/ppermute | solution.py:264
  24.2 16.2 %collective-permute-start.4 = (bf16[4,48,512]{2,1,0:T(8,128)(2,1)}, bf16[4,48,512]{2,1,0:T(8,128)(2,1)S(1)}, u32[]{:S(2)}, u32[]{:S(2)}) collective-permute-start(bf16[4,48,512]{2,1,0:T(8,128)(2,1)} %refs_0_.5), channel_id=1, source_target_pairs={{0,1},{1,0},{2,3},{3,2},{4,5},{5,4},{6,7},{7,6},{8,9},{9,8},{10,11... | collective-permute-start | bytes 589832 | tf_op jit(solution)/shard_map/ppermute | solution.py:236
  26.4 14.6 %collective-permute-start.12 = (bf16[4,32,512]{2,1,0:T(8,128)(2,1)S(1)}, bf16[4,32,512]{2,1,0:T(8,128)(2,1)S(1)}, u32[]{:S(2)}, u32[]{:S(2)}) collective-permute-start(bf16[4,32,512]{2,1,0:T(8,128)(2,1)S(1)} %collective-permute-done.10.refs_4_), channel_id=1, source_target_pairs={{0,1},{1,0},{2,3},{3,2},{4,5},{5,4},{6,7},{7,6},{8,9},{9,8},{10,11... | collective-permute-start | bytes 393224 | tf_op jit(solution)/shard_map/ppermute | solution.py:236
  26.5 14.5 %collective-permute-start.5 = (bf16[4,48,512]{2,1,0:T(8,128)(2,1)S(1)}, bf16[4,48,512]{2,1,0:T(8,128)(2,1)S(1)}, u32[]{:S(2)}, u32[]{:S(2)}) collective-permute-start(bf16[4,48,512]{2,1,0:T(8,128)(2,1)S(1)} %collective-permute-done.3.refs_1_), channel_id=1, source_target_pairs={{0,1},{1,0},{2,3},{3,2},{4,5},{5,4},{6,7},{7,6},{8,9},{9,8},{10,11... | collective-permute-start | bytes 589832 | tf_op jit(solution)/shard_map/ppermute | solution.py:236
  26.9 14.1 %collective-permute-start.13 = (bf16[4,32,512]{2,1,0:T(8,128)(2,1)S(1)}, bf16[4,32,512]{2,1,0:T(8,128)(2,1)S(1)}, u32[]{:S(2)}, u32[]{:S(2)}) collective-permute-start(bf16[4,32,512]{2,1,0:T(8,128)(2,1)S(1)} %collective-permute-done.11.refs_5_), channel_id=1, source_target_pairs={{0,1},{1,0},{2,3},{3,2},{4,5},{5,4},{6,7},{7,6},{8,9},{9,8},{10,11... | collective-permute-start | bytes 393224 | tf_op jit(solution)/shard_map/ppermute | solution.py:236
  29.6 10.8 %collective-permute-start.7 = (bf16[4,16,512]{2,1,0:T(8,128)(2,1)S(1)}, bf16[4,16,512]{2,1,0:T(8,128)(2,1)S(1)}, u32[]{:S(2)}, u32[]{:S(2)}) collective-permute-start(bf16[4,16,512]{2,1,0:T(8,128)(2,1)S(1)} %collective-permute-done.6.refs_4_), channel_id=1, source_target_pairs={{0,2},{1,3},{2,0},{3,1},{4,6},{5,7},{6,4},{7,5},{8,10},{9,11},{10,... | collective-permute-start | bytes 196616 | tf_op jit(solution)/shard_map/ppermute | solution.py:236
  32.1 0.9 %copy-start.1 = (bf16[48,768]{1,0:T(8,128)(2,1)S(1)}, bf16[48,768]{1,0:T(8,128)(2,1)}, u32[]{:S(2)}) copy-start(bf16[48,768]{1,0:T(8,128)(2,1)} %refs_0_.3) | copy-start | bytes 221188
  32.9 0.7 copy-start.2
  40.4 10.6 %collective-permute-start.8 = (bf16[4,16,512]{2,1,0:T(8,128)(2,1)S(1)}, bf16[4,16,512]{2,1,0:T(8,128)(2,1)S(1)}, u32[]{:S(2)}, u32[]{:S(2)}) collective-permute-start(bf16[4,16,512]{2,1,0:T(8,128)(2,1)S(1)} %collective-permute-done.6.refs_4_), channel_id=1, source_target_pairs={{0,1},{1,0},{2,3},{3,2},{4,5},{5,4},{6,7},{7,6},{8,9},{9,8},{10,11... | collective-permute-start | bytes 196616 | tf_op jit(solution)/shard_map/ppermute | solution.py:236
  40.5 10.6 %collective-permute-start.9 = (bf16[4,16,512]{2,1,0:T(8,128)(2,1)S(1)}, bf16[4,16,512]{2,1,0:T(8,128)(2,1)S(1)}, u32[]{:S(2)}, u32[]{:S(2)}) collective-permute-start(bf16[4,16,512]{2,1,0:T(8,128)(2,1)S(1)} %collective-permute-done.7.refs_5_), channel_id=1, source_target_pairs={{0,1},{1,0},{2,3},{3,2},{4,5},{5,4},{6,7},{7,6},{8,9},{9,8},{10,11... | collective-permute-start | bytes 196616 | tf_op jit(solution)/shard_map/ppermute | solution.py:236
  41.0 0.9 %copy-start = (bf16[4,48,512]{2,1,0:T(8,128)(2,1)S(1)}, bf16[4,48,512]{2,1,0:T(8,128)(2,1)}, u32[]{:S(2)}) copy-start(bf16[4,48,512]{2,1,0:T(8,128)(2,1)} %refs_0_.5) | copy-start | bytes 589828
  41.9 0.7 copy-start.3
  51.0 8.0 %copy-start.4 = (s32[64]{0:T(128)S(1)}, s32[64]{0:T(128)}, u32[]{:S(2)}) copy-start(s32[64]{0:T(128)} %param.10) | copy-start | bytes 772
  55.5 9.2 %collective-permute-start.15 = (f32[32,768]{1,0:T(8,128)S(1)}, f32[32,768]{1,0:T(8,128)S(1)}, u32[]{:S(2)}, u32[]{:S(2)}) collective-permute-start(f32[32,768]{1,0:T(8,128)S(1)} %get-tuple-element.9), channel_id=1, source_target_pairs={{0,4},{1,5},{2,6},{3,7},{4,0},{5,1},{6,2},{7,3},{8,12},{9,13},{10,... | collective-permute-start | bytes 294920 | tf_op jit(solution)/shard_map/ppermute | solution.py:283
  55.5 9.2 %collective-permute-start.16 = (f32[32,768]{1,0:T(8,128)S(1)}, f32[32,768]{1,0:T(8,128)S(1)}, u32[]{:S(2)}, u32[]{:S(2)}) collective-permute-start(f32[32,768]{1,0:T(8,128)S(1)} %get-tuple-element.9), channel_id=1, source_target_pairs={{0,20},{1,21},{2,22},{3,23},{4,16},{5,17},{6,18},{7,19},{8,28},{9,... | collective-permute-start | bytes 294920 | tf_op jit(solution)/shard_map/ppermute | solution.py:283
  58.5 6.2 %collective-permute-start.14 = (f32[32,768]{1,0:T(8,128)S(1)}, f32[32,768]{1,0:T(8,128)S(1)}, u32[]{:S(2)}, u32[]{:S(2)}) collective-permute-start(f32[32,768]{1,0:T(8,128)S(1)} %get-tuple-element.10.refs_0_), channel_id=1, source_target_pairs={{0,16},{16,0},{1,17},{17,1},{2,18},{18,2},{3,19},{19,3},{4,20},{20... | collective-permute-start | bytes 294920 | tf_op jit(solution)/shard_map/ppermute | solution.py:277

commit v3 on v2

--- a/solution.py
+++ b/solution.py
@@ -11,7 +11,7 @@
 
 LANES = 128
 GROUP = 16
-MAX_SHIFT = 256
+VMEM_BYTES = 24 * 1024 * 1024
 SMEM = pl.BlockSpec(memory_space=pltpu.SMEM)
 
 
@@ -101,7 +101,7 @@
             pltpu.VMEM((4, 8, span + taps), jnp.float32),
             pltpu.VMEM((2 * span // LANES, chans * 8, LANES), jnp.float32),
         ],
-        compiler_params=pltpu.CompilerParams(vmem_limit_bytes=40 * 1024 * 1024),
+        compiler_params=pltpu.CompilerParams(vmem_limit_bytes=VMEM_BYTES),
         cost_estimate=pl.CostEstimate(flops=1, bytes_accessed=10**7, transcendentals=0),
     )(shifts, *blocks)
 
@@ -162,8 +162,9 @@
     lax.fori_loop(0, group // unroll, body, 0)
 
 
-def correlate(live, base, level, banks, before, first, count, overall):
-    segs, chans, _, long = base.shape
+def correlate(live, base, level, banks, before, first, count, overall, seg=None):
+    _, chans, _, long = base.shape
+    segs, seg = (base.shape[0], 0) if seg is None else (1, seg)
     span = level.shape[2]
     per, _, taps = banks[0].shape
     tmpl = per * len(banks)
@@ -171,8 +172,8 @@
     full = (segs, tmpl, span)
     in_specs = [
         SMEM,
-        pl.BlockSpec((segs, GROUP, 16, long), lambda i: (0, at + i, 0, 0)),
-        pl.BlockSpec((segs, GROUP, span), lambda i: (0, at + i, 0)),
+        pl.BlockSpec((segs, GROUP, 16, long), lambda i: (seg, at + i, 0, 0)),
+        pl.BlockSpec((segs, GROUP, span), lambda i: (seg, at + i, 0)),
     ]
     for bank in banks:
         skip = at if bank.shape[1] == chans else 0
@@ -185,7 +186,7 @@
         def kernel(live, base, level, *refs):
             inner(live, base, level, *refs[: len(banks)], None, *refs[len(banks) :])
     else:
-        in_specs.append(pl.BlockSpec(full, lambda i: (0, 0, 0)))
+        in_specs.append(pl.BlockSpec(full, lambda i: (seg, 0, 0)))
         args.append(before)
     return pl.pallas_call(
         kernel,
@@ -194,7 +195,7 @@
         in_specs=in_specs,
         out_specs=pl.BlockSpec(full, lambda i: (0, 0, 0)),
         scratch_shapes=[pltpu.VMEM((taps // LANES, tmpl * GROUP, LANES), jnp.float32)],
-        compiler_params=pltpu.CompilerParams(vmem_limit_bytes=40 * 1024 * 1024),
+        compiler_params=pltpu.CompilerParams(vmem_limit_bytes=VMEM_BYTES),
         cost_estimate=pl.CostEstimate(
             flops=2 * tmpl * count * taps * span * segs,
             bytes_accessed=10**7,
@@ -203,9 +204,9 @@
     )(*args)
 
 
-def finish_kernel(counts, rows, *refs):
+def finish_kernel(counts, per, plan, places, *refs):
     parts, (out, both) = refs[:-2], refs[-2:]
-    tmpl = parts[0].shape[0]
+    tmpl, share = parts[0].shape[0], out.shape[0]
     start = 0
     for src, count in enumerate(counts):
         value = parts[start][...]
@@ -213,23 +214,28 @@
             value = value + ref[...]
         both[pl.ds(src * tmpl, tmpl), :] = value
         start += count
-    for p in range(out.shape[0]):
-        out[pl.ds(p, 1), :] = both[pl.ds(rows[p], 1), :]
-
-
-def finish(rows, groups):
+    mine, first = lax.axis_index("tm"), lax.axis_index("sta") * share
+    for p in range(share):
+        slot = plan[first + p]
+        owner = lax.div(slot, per)
+        row = places[lax.bitwise_xor(owner, mine)] * per + (slot - owner * per)
+        out[pl.ds(p, 1), :] = both[pl.ds(row, 1), :]
+
+
+def finish(plan, places, per, groups):
     parts = [part for group in groups for part in group]
-    shape = parts[0].shape
-    spec = pl.BlockSpec(shape, lambda i: (0, 0))
+    tmpl, span = parts[0].shape
+    share = plan.shape[0] // lax.axis_size("sta")
+    spec = pl.BlockSpec((tmpl, span), lambda i: (0, 0))
     return pl.pallas_call(
-        functools.partial(finish_kernel, [len(group) for group in groups]),
+        functools.partial(finish_kernel, [len(group) for group in groups], per),
         grid=(1,),
-        out_shape=jax.ShapeDtypeStruct((rows.shape[0], shape[1]), jnp.float32),
-        in_specs=[SMEM] + [spec] * len(parts),
-        out_specs=pl.BlockSpec((rows.shape[0], shape[1]), lambda i: (0, 0)),
-        scratch_shapes=[pltpu.VMEM((len(groups) * shape[0], shape[1]), jnp.float32)],
-        compiler_params=pltpu.CompilerParams(vmem_limit_bytes=40 * 1024 * 1024),
-    )(rows, *parts)
+        out_shape=jax.ShapeDtypeStruct((share, span), jnp.float32),
+        in_specs=[SMEM] * 2 + [spec] * len(parts),
+        out_specs=pl.BlockSpec((share, span), lambda i: (0, 0)),
+        scratch_shapes=[pltpu.VMEM((len(groups) * tmpl, span), jnp.float32)],
+        compiler_params=pltpu.CompilerParams(vmem_limit_bytes=VMEM_BYTES),
+    )(plan, jnp.asarray(places), *parts)
 
 
 def crossed(values, bit):
@@ -246,52 +252,46 @@
     far, shared = count // 2, count // 4
     others = [bit for bit in (1 << e for e in range(count.bit_length() - 4, -1, -1))]
 
-    cuts = [0, chans - GROUP, chans] if chans > GROUP else [0, chans]
-    spans = list(zip(cuts[:-1], cuts[1:]))
-    chunked = {far: [crossed(templates[:, a:b], far) for a, b in spans]}
-    whole = {0: templates}
-    for bit in others:
-        for mask in list(whole):
-            whole[mask | bit] = crossed(whole[mask], bit)
-        for mask in list(chunked):
-            chunked[mask | bit] = [crossed(part, bit) for part in chunked[mask]]
-
+    banks = {0: templates, far: crossed(templates, far)}
+    for bit in others[:-1]:
+        banks[bit] = crossed(templates, bit)
     after = [(i, i - 1) for i in range(1, count)]
-    blocks = [
-        record,
+    moved = [
         lax.ppermute(record, "tm", after),
         crossed(record, shared),
         lax.ppermute(record, "tm", [(i, j ^ shared) for i, j in after]),
     ]
-    base, level = prepare(shifts, blocks, taps)
-
-    total = None
-    for idx, (a, b) in enumerate(spans):
-        banks = list(whole.values()) + [chunked[mask][idx] for mask in chunked]
-        total = correlate(live_mask, base, level, banks, total, a, b - a, overall)
-
-    near, away = [total[0]], []
+    moved, banks[far] = lax.optimization_barrier((moved, banks[far]))
+    base, level = prepare(shifts, [record, *moved], taps)
+    for bit in others:
+        for mask in list(banks):
+            if mask | bit not in banks:
+                banks[mask | bit] = crossed(banks[mask], bit)
+        if bit == others[-2]:
+            banks[far | bit], base = lax.optimization_barrier((banks[far | bit], base))
+    masks = list(banks)
+    total = correlate(
+        live_mask, base, level, list(banks.values()), None, 0, chans, overall
+    )
+    kept, sent = total[0], total[1]
+
+    near, away = [kept], []
     for by in range(groups):
-        if by:
-            pairs = [(i, (i + by) % groups) for i in range(groups)]
-            near.append(lax.ppermute(total[0], "sta", pairs))
         pairs = [
             (i * count + j, (i + by) % groups * count + (j ^ shared))
             for i in range(groups)
             for j in range(count)
         ]
-        away.append(lax.ppermute(total[1], ("sta", "tm"), pairs))
-
-    masks = list(whole) + list(chunked)
+        away.append(lax.ppermute(sent, ("sta", "tm"), pairs))
+    for by in range(1, groups):
+        pairs = [(i, (i + by) % groups) for i in range(groups)]
+        near.append(lax.ppermute(kept, "sta", pairs))
+
     places = np.zeros(count, np.int32)
     for place, mask in enumerate(masks):
         places[mask] = place
         places[mask | shared] = place + len(masks)
-    mine = lax.axis_index("tm")
-    share = plan.shape[0] // groups
-    slots = lax.dynamic_slice_in_dim(plan, lax.axis_index("sta") * share, share)
-    rows = jnp.asarray(places)[(slots // per) ^ mine] * per + slots % per
-    return finish(rows, [near, away])
+    return finish(plan, places, per, [near, away])
 
 
 def solution(mesh):

time: 66.3 us -> 51.2 us (0.77)
  waiting for transfers between devices: 15.5 us -> 9.3 us
  starting transfers between devices: 22.4 us -> 17.8 us
  local copies, waits for them, and re-layouts: 6.25 us -> 3.14 us
  other arithmetic: 0.82 us -> 0 us
    ppermute x12 -> x8, waiting for transfers between devices: 7.99 us -> 1.37 us  [crossed(): lax.ppermute(values, 'tm', [(i, i ^ bit) for i in range(lax.axis_size('tm...]
    ppermute x12 -> x8, starting transfers between devices: 16.3 us -> 11.7 us  [crossed(): lax.ppermute(values, 'tm', [(i, i ^ bit) for i in range(lax.axis_size('tm...]
    slice x2 -> x0, local copies, waits for them, and re-layouts: 1.76 us -> none  [per_device(): chunked = {far: [crossed(templates[:, a:b], far) for a, b in spans]}]
    ppermute x1, waiting for transfers between devices: 1.9 us -> 3.41 us  [per_device(): lax.ppermute(record, 'tm', [(i, j ^ shared) for i, j in after])]
    gather x1 -> x0, local copies, waits for them, and re-layouts: 1.35 us -> none  [per_device(): rows = jnp.asarray(places)[slots // per ^ mine] * per + slots % per]
    ppermute x3, waiting for transfers between devices: 5.59 us -> 4.52 us  [the longest x2 4.52 us: per_device(): away.append(lax.ppermute(sent, ('sta', 'tm'), pairs))]
    select_n x1 -> x0, other arithmetic: 0.74 us -> none  [per_device(): rows = jnp.asarray(places)[slots // per ^ mine] * per + slots % per]
    pallas_call x2 -> x1, Pallas kernels: 12.8 us -> 12.5 us  [correlate(): pl.pallas_call(kernel, grid=(count // GROUP,), out_shape=jax.ShapeDtypeSt...]
  transfers between devices with their start and end apart: 17 -> 13, of which waited for: 4 -> 5; matrix products, arithmetic and copies ran while one was open for 5% -> 0% of each run, Pallas kernels for 23% -> 13%
where the time goes in v3:
time: 51.2 us; the launch traced here: 51 us
  Pallas kernels  20.6 us (40%)
  starting transfers between devices  17.8 us (35%)
  waiting for transfers between devices  9.3 us (18%)
  local copies, waits for them, and re-layouts  3.14 us (6%)
    pallas_call x1, Pallas kernels, correlate(): pl.pallas_call(kernel, grid=(count // GROUP,), out_shape=jax.ShapeDtypeSt...  12.5 us
    ppermute x8, starting transfers between devices, crossed(): lax.ppermute(values, 'tm', [(i, i ^ bit) for i in range(lax.axis_size('tm...  11.7 us
    pallas_call x1, Pallas kernels, prepare(): pl.pallas_call(prep_kernel, grid=(1,), out_shape=[jax.ShapeDtypeStruct((s...  6.78 us
    ppermute x2, waiting for transfers between devices, per_device(): away.append(lax.ppermute(sent, ('sta', 'tm'), pairs))  4.52 us
    ppermute x1, waiting for transfers between devices, per_device(): lax.ppermute(record, 'tm', [(i, j ^ shared) for i, j in after])  3.41 us
    unnamed x12, local copies, waits for them, and re-layouts  3.13 us
    ppermute x2, starting transfers between devices, per_device(): away.append(lax.ppermute(sent, ('sta', 'tm'), pairs))  3.02 us
    pallas_call x1, Pallas kernels, finish(): pl.pallas_call(functools.partial(finish_kernel, [len(group) for group in...  1.37 us
  transfers between devices with their start and end apart: 13, of which 5 were waited for; matrix products, arithmetic and copies ran while one was open for 0% of the time, Pallas kernels for 13%

profile of v3, /device:TPU:0, one launch (start us, length us, event | category | flops | bytes accessed | tf_op | source)
XLA Modules:
  0.0 51.0 jit_solution(2346390097624628237)
XLA Ops:
  0.0 4.0 %collective-permute-start.3 = (bf16[4,48,512]{2,1,0:T(8,128)(2,1)}, bf16[4,48,512]{2,1,0:T(8,128)(2,1)S(1)}, u32[]{:S(2)}, u32[]{:S(2)}) collective-permute-start(bf16[4,48,512]{2,1,0:T(8,128)(2,1)} %refs_0_.3), channel_id=1, source_target_pairs={{0,8},{1,9},{2,10},{3,11},{4,12},{5,13},{6,14},{7,15},{8,0},{9,1},... | collective-permute-start | bytes 589832 | tf_op jit(solution)/shard_map/ppermute | solution.py:242
  4.0 1.6 %collective-permute-start.1 = (bf16[48,768]{1,0:T(8,128)(2,1)}, bf16[48,768]{1,0:T(8,128)(2,1)S(1)}, u32[]{:S(2)}, u32[]{:S(2)}) collective-permute-start(bf16[48,768]{1,0:T(8,128)(2,1)} %refs_0_.2), channel_id=1, source_target_pairs={{0,4},{1,5},{2,6},{3,7},{4,0},{5,1},{6,2},{7,3},{8,12},{9,13},{10,... | collective-permute-start | bytes 221192 | tf_op jit(solution)/shard_map/ppermute | solution.py:242
  5.6 1.3 %collective-permute-start = (bf16[48,768]{1,0:T(8,128)(2,1)}, bf16[48,768]{1,0:T(8,128)(2,1)S(1)}, u32[]{:S(2)}, u32[]{:S(2)}) collective-permute-start(bf16[48,768]{1,0:T(8,128)(2,1)} %refs_0_.2), channel_id=1, source_target_pairs={{1,0},{2,1},{3,2},{4,3},{5,4},{6,5},{7,6},{8,7},{9,8},{10,9},{11,1... | collective-permute-start | bytes 221192 | tf_op jit(solution)/shard_map/ppermute | solution.py:260
  6.9 1.3 %collective-permute-start.2 = (bf16[48,768]{1,0:T(8,128)(2,1)}, bf16[48,768]{1,0:T(8,128)(2,1)S(1)}, u32[]{:S(2)}, u32[]{:S(2)}) collective-permute-start(bf16[48,768]{1,0:T(8,128)(2,1)} %refs_0_.2), channel_id=1, source_target_pairs={{1,4},{2,5},{3,6},{4,7},{5,0},{6,1},{7,2},{8,3},{9,12},{10,13},{11... | collective-permute-start | bytes 221192 | tf_op jit(solution)/shard_map/ppermute | solution.py:262
  8.2 3.3 %collective-permute-start.5 = (bf16[4,48,512]{2,1,0:T(8,128)(2,1)}, bf16[4,48,512]{2,1,0:T(8,128)(2,1)S(1)}, u32[]{:S(2)}, u32[]{:S(2)}) collective-permute-start(bf16[4,48,512]{2,1,0:T(8,128)(2,1)} %refs_0_.3), channel_id=1, source_target_pairs={{0,2},{1,3},{2,0},{3,1},{4,6},{5,7},{6,4},{7,5},{8,10},{9,11},{10,... | collective-permute-start | bytes 589832 | tf_op jit(solution)/shard_map/ppermute | solution.py:242
  11.5 0.0 collective-permute-done.1.refs_2_
  11.5 0.0 collective-permute-done.refs_1_
  11.5 3.4 %collective-permute-done.2.refs_3_ = bf16[48,768]{1,0:T(8,128)(2,1)S(1)} collective-permute-done((bf16[48,768]{1,0:T(8,128)(2,1)}, bf16[48,768]{1,0:T(8,128)(2,1)S(1)}, u32[]{:S(2)}, u32[]{:S(2)}) %collective-permute-start.2) | collective-permute-done | bytes 73760 | tf_op jit(solution)/shard_map/ppermute | solution.py:262
  14.9 0.0 collective-permute-done.3.refs_1_
  14.9 1.5 %collective-permute-start.4 = (bf16[4,48,512]{2,1,0:T(8,128)(2,1)S(1)}, bf16[4,48,512]{2,1,0:T(8,128)(2,1)S(1)}, u32[]{:S(2)}, u32[]{:S(2)}) collective-permute-start(bf16[4,48,512]{2,1,0:T(8,128)(2,1)S(1)} %collective-permute-done.3.refs_1_), channel_id=1, source_target_pairs={{0,2},{1,3},{2,0},{3,1},{4,6},{5,7},{6,4},{7,5},{8,10},{9,11},{10,... | collective-permute-start | bytes 589832 | tf_op jit(solution)/shard_map/ppermute | solution.py:242
  16.5 0.6 %collective-permute-start.6 = (bf16[4,48,512]{2,1,0:T(8,128)(2,1)}, bf16[4,48,512]{2,1,0:T(8,128)(2,1)S(1)}, u32[]{:S(2)}, u32[]{:S(2)}) collective-permute-start(bf16[4,48,512]{2,1,0:T(8,128)(2,1)} %refs_0_.3), channel_id=1, source_target_pairs={{0,1},{1,0},{2,3},{3,2},{4,5},{5,4},{6,7},{7,6},{8,9},{9,8},{10,11... | collective-permute-start | bytes 589832 | tf_op jit(solution)/shard_map/ppermute | solution.py:242
  17.1 0.0 collective-permute-start.7
  17.1 0.0 copy-start
  17.1 0.9 %copy-done = bf16[48,768]{1,0:T(8,128)(2,1)S(1)} copy-done((bf16[48,768]{1,0:T(8,128)(2,1)S(1)}, bf16[48,768]{1,0:T(8,128)(2,1)}, u32[]{:S(2)}) %copy-start) | copy-done | bytes 73752
  17.9 0.0 copy-start.1
  18.0 0.7 %copy-done.1 = s32[48]{0:T(128)S(1)} copy-done((s32[48]{0:T(128)S(1)}, s32[48]{0:T(128)}, u32[]{:S(2)}) %copy-start.1) | copy-done | bytes 216
  18.6 6.8 %shard_map.64 = (bf16[2,48,16,1280]{3,2,1,0:T(8,128)(2,1)S(1)}, f32[2,48,768]{2,1,0:T(8,128)S(1)}) custom-call(s32[48]{0:T(128)S(1)} %copy-done.1, bf16[48,768]{1,0:T(8,128)(2,1)S(1)} %copy-done, bf16[48,768]{1,0:T(8,128)(2,1)S(1)} %collective-permute-done.refs_1_, bf16[48,768]{1,0:T(8,128)(2,1)S(1)} %collective-permute-done.1.refs_2_, ...), custom_call_target="tpu_custom_call" | custom-call | flops 1 | bytes 10000000 | tf_op jit(solution)/shard_map/pallas_call | solution.py:88
  25.4 0.0 collective-permute-done.5.refs_2_
  25.4 0.6 %collective-permute-start.8 = (bf16[4,48,512]{2,1,0:T(8,128)(2,1)S(1)}, bf16[4,48,512]{2,1,0:T(8,128)(2,1)S(1)}, u32[]{:S(2)}, u32[]{:S(2)}) collective-permute-start(bf16[4,48,512]{2,1,0:T(8,128)(2,1)S(1)} %collective-permute-done.5.refs_2_), channel_id=1, source_target_pairs={{0,1},{1,0},{2,3},{3,2},{4,5},{5,4},{6,7},{7,6},{8,9},{9,8},{10,11... | collective-permute-start | bytes 589832 | tf_op jit(solution)/shard_map/ppermute | solution.py:242
  26.0 0.0 collective-permute-done.4.refs_3_
  26.0 0.1 collective-permute-start.9
  26.1 0.0 collective-permute-done.6.refs_4_
  26.1 1.0 %collective-permute-done.8.refs_6_ = bf16[4,48,512]{2,1,0:T(8,128)(2,1)S(1)} collective-permute-done((bf16[4,48,512]{2,1,0:T(8,128)(2,1)S(1)}, bf16[4,48,512]{2,1,0:T(8,128)(2,1)S(1)}, u32[]{:S(2)}, u32[]{:S(2)}) %collective-permute-start.8) | collective-permute-done | bytes 196640 | tf_op jit(solution)/shard_map/ppermute | solution.py:242
  27.0 0.0 collective-permute-done.7.refs_5_
  27.1 0.4 collective-permute-done.9.refs_7_
  27.4 0.0 copy-start.4
  27.4 0.9 %copy-done.4 = bf16[4,48,512]{2,1,0:T(8,128)(2,1)S(1)} copy-done((bf16[4,48,512]{2,1,0:T(8,128)(2,1)S(1)}, bf16[4,48,512]{2,1,0:T(8,128)(2,1)}, u32[]{:S(2)}) %copy-start.4) | copy-done | bytes 196632
  28.4 0.0 copy-start.5
  28.4 0.7 %copy-done.5 = s32[48]{0:T(128)S(1)} copy-done((s32[48]{0:T(128)S(1)}, s32[48]{0:T(128)}, u32[]{:S(2)}) %copy-start.5) | copy-done | bytes 216
  29.0 0.0 copy-start.2
  29.0 0.0 copy-start.3
  29.0 12.5 %shard_map.65 = f32[2,32,768]{2,1,0:T(8,128)S(1)} custom-call(s32[48]{0:T(128)S(1)} %copy-done.5, bf16[2,48,16,1280]{3,2,1,0:T(8,128)(2,1)S(1)} %get-tuple-element.18.base, f32[2,48,768]{2,1,0:T(8,128)S(1)} %get-tuple-element.19.level, bf16[4,48,512]{2,1,0:T(8,128)(2,1)S(1)} %copy-done.4, bf16[4,48,512]{2,1,0:T(8,128)(2,1)S(1)} %collective-permute-done.3.refs_1_, ...), custom_call_target="tpu_custom_call" | custom-call | flops 2415919104 | bytes 10000000 | tf_op jit(solution)/shard_map/pallas_call | solution.py:191
  41.5 0.8 %collective-permute-start.12 = (f32[32,768]{1,0:T(8,128)S(1)}, f32[32,768]{1,0:T(8,128)S(1)}, u32[]{:S(2)}, u32[]{:S(2)}) collective-permute-start(f32[32,768]{1,0:T(8,128)S(1)} %get-tuple-element.21), channel_id=1, source_target_pairs={{0,20},{1,21},{2,22},{3,23},{4,16},{5,17},{6,18},{7,19},{8,28},{9,... | collective-permute-start | bytes 294920 | tf_op jit(solution)/shard_map/ppermute | solution.py:285
  42.3 2.2 %collective-permute-start.11 = (f32[32,768]{1,0:T(8,128)S(1)}, f32[32,768]{1,0:T(8,128)S(1)}, u32[]{:S(2)}, u32[]{:S(2)}) collective-permute-start(f32[32,768]{1,0:T(8,128)S(1)} %get-tuple-element.21), channel_id=1, source_target_pairs={{0,4},{1,5},{2,6},{3,7},{4,0},{5,1},{6,2},{7,3},{8,12},{9,13},{10,... | collective-permute-start | bytes 294920 | tf_op jit(solution)/shard_map/ppermute | solution.py:285
  44.5 0.5 %collective-permute-start.10 = (f32[32,768]{1,0:T(8,128)S(1)}, f32[32,768]{1,0:T(8,128)S(1)}, u32[]{:S(2)}, u32[]{:S(2)}) collective-permute-start(f32[32,768]{1,0:T(8,128)S(1)} %get-tuple-element.22.refs_0_), channel_id=1, source_target_pairs={{0,16},{16,0},{1,17},{17,1},{2,18},{18,2},{3,19},{19,3},{4,20},{20... | collective-permute-start | bytes 294920 | tf_op jit(solution)/shard_map/ppermute | solution.py:288
  45.1 3.0 %collective-permute-done.12.refs_3_ = f32[32,768]{1,0:T(8,128)S(1)} collective-permute-done((f32[32,768]{1,0:T(8,128)S(1)}, f32[32,768]{1,0:T(8,128)S(1)}, u32[]{:S(2)}, u32[]{:S(2)}) %collective-permute-start.12) | collective-permute-done | bytes 98336 | tf_op jit(solution)/shard_map/ppermute | solution.py:285
  48.1 1.5 %collective-permute-done.11.refs_2_ = f32[32,768]{1,0:T(8,128)S(1)} collective-permute-done((f32[32,768]{1,0:T(8,128)S(1)}, f32[32,768]{1,0:T(8,128)S(1)}, u32[]{:S(2)}, u32[]{:S(2)}) %collective-permute-start.11) | collective-permute-done | bytes 98336 | tf_op jit(solution)/shard_map/ppermute | solution.py:285
  49.6 0.0 collective-permute-done.10.refs_1_
  49.6 0.0 copy-done.2
  49.6 0.0 copy-done.3
  49.6 1.4 %shard_map.66 = f32[32,768]{1,0:T(8,128)} custom-call(s32[64]{0:T(128)S(1)} %copy-done.2, s32[16]{0:T(128)S(1)} %copy-done.3, f32[32,768]{1,0:T(8,128)S(1)} %get-tuple-element.22.refs_0_, f32[32,768]{1,0:T(8,128)S(1)} %collective-permute-done.10.refs_1_, f32[32,768]{1,0:T(8,128)S(1)} %collective-permute-done.11.refs_2_, ...), custom_call_target="tpu_custom_call" | custom-call | tf_op jit(solution)/shard_map/pallas_call | solution.py:230
  (1 shorter events, 0.0 us)
Async XLA Ops:
  0.0 14.9 %collective-permute-start.3 = (bf16[4,48,512]{2,1,0:T(8,128)(2,1)}, bf16[4,48,512]{2,1,0:T(8,128)(2,1)S(1)}, u32[]{:S(2)}, u32[]{:S(2)}) collective-permute-start(bf16[4,48,512]{2,1,0:T(8,128)(2,1)} %refs_0_.3), channel_id=1, source_target_pairs={{0,8},{1,9},{2,10},{3,11},{4,12},{5,13},{6,14},{7,15},{8,0},{9,1},... | collective-permute-start | bytes 589832 | tf_op jit(solution)/shard_map/ppermute | solution.py:242
  4.0 7.5 %collective-permute-start.1 = (bf16[48,768]{1,0:T(8,128)(2,1)}, bf16[48,768]{1,0:T(8,128)(2,1)S(1)}, u32[]{:S(2)}, u32[]{:S(2)}) collective-permute-start(bf16[48,768]{1,0:T(8,128)(2,1)} %refs_0_.2), channel_id=1, source_target_pairs={{0,4},{1,5},{2,6},{3,7},{4,0},{5,1},{6,2},{7,3},{8,12},{9,13},{10,... | collective-permute-start | bytes 221192 | tf_op jit(solution)/shard_map/ppermute | solution.py:242
  5.6 5.9 %collective-permute-start = (bf16[48,768]{1,0:T(8,128)(2,1)}, bf16[48,768]{1,0:T(8,128)(2,1)S(1)}, u32[]{:S(2)}, u32[]{:S(2)}) collective-permute-start(bf16[48,768]{1,0:T(8,128)(2,1)} %refs_0_.2), channel_id=1, source_target_pairs={{1,0},{2,1},{3,2},{4,3},{5,4},{6,5},{7,6},{8,7},{9,8},{10,9},{11,1... | collective-permute-start | bytes 221192 | tf_op jit(solution)/shard_map/ppermute | solution.py:260
  6.9 8.0 %collective-permute-start.2 = (bf16[48,768]{1,0:T(8,128)(2,1)}, bf16[48,768]{1,0:T(8,128)(2,1)S(1)}, u32[]{:S(2)}, u32[]{:S(2)}) collective-permute-start(bf16[48,768]{1,0:T(8,128)(2,1)} %refs_0_.2), channel_id=1, source_target_pairs={{1,4},{2,5},{3,6},{4,7},{5,0},{6,1},{7,2},{8,3},{9,12},{10,13},{11... | collective-permute-start | bytes 221192 | tf_op jit(solution)/shard_map/ppermute | solution.py:262
  8.2 17.2 %collective-permute-start.5 = (bf16[4,48,512]{2,1,0:T(8,128)(2,1)}, bf16[4,48,512]{2,1,0:T(8,128)(2,1)S(1)}, u32[]{:S(2)}, u32[]{:S(2)}) collective-permute-start(bf16[4,48,512]{2,1,0:T(8,128)(2,1)} %refs_0_.3), channel_id=1, source_target_pairs={{0,2},{1,3},{2,0},{3,1},{4,6},{5,7},{6,4},{7,5},{8,10},{9,11},{10,... | collective-permute-start | bytes 589832 | tf_op jit(solution)/shard_map/ppermute | solution.py:242
  14.9 11.0 %collective-permute-start.4 = (bf16[4,48,512]{2,1,0:T(8,128)(2,1)S(1)}, bf16[4,48,512]{2,1,0:T(8,128)(2,1)S(1)}, u32[]{:S(2)}, u32[]{:S(2)}) collective-permute-start(bf16[4,48,512]{2,1,0:T(8,128)(2,1)S(1)} %collective-permute-done.3.refs_1_), channel_id=1, source_target_pairs={{0,2},{1,3},{2,0},{3,1},{4,6},{5,7},{6,4},{7,5},{8,10},{9,11},{10,... | collective-permute-start | bytes 589832 | tf_op jit(solution)/shard_map/ppermute | solution.py:242
  16.5 9.6 %collective-permute-start.6 = (bf16[4,48,512]{2,1,0:T(8,128)(2,1)}, bf16[4,48,512]{2,1,0:T(8,128)(2,1)S(1)}, u32[]{:S(2)}, u32[]{:S(2)}) collective-permute-start(bf16[4,48,512]{2,1,0:T(8,128)(2,1)} %refs_0_.3), channel_id=1, source_target_pairs={{0,1},{1,0},{2,3},{3,2},{4,5},{5,4},{6,7},{7,6},{8,9},{9,8},{10,11... | collective-permute-start | bytes 589832 | tf_op jit(solution)/shard_map/ppermute | solution.py:242
  17.1 10.0 %collective-permute-start.7 = (bf16[4,48,512]{2,1,0:T(8,128)(2,1)S(1)}, bf16[4,48,512]{2,1,0:T(8,128)(2,1)S(1)}, u32[]{:S(2)}, u32[]{:S(2)}) collective-permute-start(bf16[4,48,512]{2,1,0:T(8,128)(2,1)S(1)} %collective-permute-done.3.refs_1_), channel_id=1, source_target_pairs={{0,1},{1,0},{2,3},{3,2},{4,5},{5,4},{6,7},{7,6},{8,9},{9,8},{10,11... | collective-permute-start | bytes 589832 | tf_op jit(solution)/shard_map/ppermute | solution.py:242
  17.1 0.9 %copy-start = (bf16[48,768]{1,0:T(8,128)(2,1)S(1)}, bf16[48,768]{1,0:T(8,128)(2,1)}, u32[]{:S(2)}) copy-start(bf16[48,768]{1,0:T(8,128)(2,1)} %refs_0_.2) | copy-start | bytes 221188
  17.9 0.7 %copy-start.1 = (s32[48]{0:T(128)S(1)}, s32[48]{0:T(128)}, u32[]{:S(2)}) copy-start(s32[48]{0:T(128)} %shifts.1) | copy-start | bytes 580
  25.4 1.6 %collective-permute-start.8 = (bf16[4,48,512]{2,1,0:T(8,128)(2,1)S(1)}, bf16[4,48,512]{2,1,0:T(8,128)(2,1)S(1)}, u32[]{:S(2)}, u32[]{:S(2)}) collective-permute-start(bf16[4,48,512]{2,1,0:T(8,128)(2,1)S(1)} %collective-permute-done.5.refs_2_), channel_id=1, source_target_pairs={{0,1},{1,0},{2,3},{3,2},{4,5},{5,4},{6,7},{7,6},{8,9},{9,8},{10,11... | collective-permute-start | bytes 589832 | tf_op jit(solution)/shard_map/ppermute | solution.py:242
  26.0 1.4 %collective-permute-start.9 = (bf16[4,48,512]{2,1,0:T(8,128)(2,1)S(1)}, bf16[4,48,512]{2,1,0:T(8,128)(2,1)S(1)}, u32[]{:S(2)}, u32[]{:S(2)}) collective-permute-start(bf16[4,48,512]{2,1,0:T(8,128)(2,1)S(1)} %collective-permute-done.4.refs_3_), channel_id=1, source_target_pairs={{0,1},{1,0},{2,3},{3,2},{4,5},{5,4},{6,7},{7,6},{8,9},{9,8},{10,11... | collective-permute-start | bytes 589832 | tf_op jit(solution)/shard_map/ppermute | solution.py:242
  27.4 0.9 %copy-start.4 = (bf16[4,48,512]{2,1,0:T(8,128)(2,1)S(1)}, bf16[4,48,512]{2,1,0:T(8,128)(2,1)}, u32[]{:S(2)}) copy-start(bf16[4,48,512]{2,1,0:T(8,128)(2,1)} %refs_0_.3) | copy-start | bytes 589828
  28.4 0.7 %copy-start.5 = (s32[48]{0:T(128)S(1)}, s32[48]{0:T(128)}, u32[]{:S(2)}) copy-start(s32[48]{0:T(128)} %live.1) | copy-start | bytes 580
  29.0 20.6 %copy-start.2 = (s32[64]{0:T(128)S(1)}, s32[64]{0:T(128)}, u32[]{:S(2)}) copy-start(s32[64]{0:T(128)} %plan.1) | copy-start | bytes 772
  29.0 20.6 %copy-start.3 = (s32[16]{0:T(128)S(1)}, s32[16]{0:T(128)}, u32[]{:S(2)}) copy-start(s32[16]{0:T(128)} %constant.2.clone.places) | copy-start | bytes 196
  41.5 6.6 %collective-permute-start.12 = (f32[32,768]{1,0:T(8,128)S(1)}, f32[32,768]{1,0:T(8,128)S(1)}, u32[]{:S(2)}, u32[]{:S(2)}) collective-permute-start(f32[32,768]{1,0:T(8,128)S(1)} %get-tuple-element.21), channel_id=1, source_target_pairs={{0,20},{1,21},{2,22},{3,23},{4,16},{5,17},{6,18},{7,19},{8,28},{9,... | collective-permute-start | bytes 294920 | tf_op jit(solution)/shard_map/ppermute | solution.py:285
  42.3 7.3 %collective-permute-start.11 = (f32[32,768]{1,0:T(8,128)S(1)}, f32[32,768]{1,0:T(8,128)S(1)}, u32[]{:S(2)}, u32[]{:S(2)}) collective-permute-start(f32[32,768]{1,0:T(8,128)S(1)} %get-tuple-element.21), channel_id=1, source_target_pairs={{0,4},{1,5},{2,6},{3,7},{4,0},{5,1},{6,2},{7,3},{8,12},{9,13},{10,... | collective-permute-start | bytes 294920 | tf_op jit(solution)/shard_map/ppermute | solution.py:285
  44.5 5.1 %collective-permute-start.10 = (f32[32,768]{1,0:T(8,128)S(1)}, f32[32,768]{1,0:T(8,128)S(1)}, u32[]{:S(2)}, u32[]{:S(2)}) collective-permute-start(f32[32,768]{1,0:T(8,128)S(1)} %get-tuple-element.22.refs_0_), channel_id=1, source_target_pairs={{0,16},{16,0},{1,17},{17,1},{2,18},{18,2},{3,19},{19,3},{4,20},{20... | collective-permute-start | bytes 294920 | tf_op jit(solution)/shard_map/ppermute | solution.py:288

commit v4 on v3

v4 whole, which is shorter than its diff:
```python
import functools
import math

import jax
import jax.numpy as jnp
import numpy as np
from jax import lax
from jax.experimental import pallas as pl
from jax.experimental.pallas import tpu as pltpu
from jax.sharding import PartitionSpec as P

LANES = 128
GROUP = 16
VMEM_BYTES = 24 * 1024 * 1024
SMEM = pl.BlockSpec(memory_space=pltpu.SMEM)
VMEM = pl.BlockSpec(memory_space=pltpu.VMEM)


def rolled_left(values, by):
    width = values.shape[1]
    return pltpu.roll(values, (width - by) % width, 1)


def padded(values, axis, multiple):
    extra = -values.shape[axis] % multiple
    if extra == 0:
        return values
    widths = [(0, extra if i == axis else 0) for i in range(values.ndim)]
    return jnp.pad(values, widths)


def prep_kernel(half, scalars, record, *refs):
    blocks, (base, level, lines, flat, ext) = refs[:-5], refs[-5:]
    segs = (len(blocks) + 1) // 2
    chans, span = record.shape
    kept = base.shape[1]
    taps = base.shape[3] - span
    width, long = 2 * span, span + taps
    start = half() * kept

    sides = (record, *blocks)
    for seg in range(segs):
        for side in range(2):
            ext[seg, :, side * span : (side + 1) * span] = sides[2 * seg + side][...].astype(
                jnp.float32
            )
        for first in range(0, kept, 8):
            both = ext[seg, pl.ds(pl.multiple_of(start + first, 8), 8), :]
            window, reach = both * both, 1
            while reach < taps:
                window = window + rolled_left(window, reach)
                reach *= 2
            rate = lax.rsqrt(window + 1e-06)
            for m in range(width // LANES):
                cols = slice(m * LANES, (m + 1) * LANES)
                flat[m, pl.ds(8 * first + seg, 8, stride=8), :] = both[:, cols]
                flat[m, pl.ds(8 * first + segs + seg, 8, stride=8), :] = rate[:, cols]

    flip = 7 - lax.broadcasted_iota(jnp.int32, (8, long), 0)

    def one(chan, slot):
        lag = scalars[start + chan]
        alive = scalars[chans + start + chan].astype(jnp.float32)
        rows = pl.ds(pl.multiple_of(chan * 8, 8), 8)
        held = jnp.concatenate([flat[m, rows, :] for m in range(width // LANES)], axis=1)
        lines[slot] = pltpu.roll(held, lax.rem(width - lag, width), 1)[:, :long]
        for seg in range(segs):
            level[seg, pl.ds(chan, 1), :] = lines[slot, pl.ds(segs + seg, 1), :span] * alive
            eight = pltpu.roll(
                jnp.broadcast_to(lines[slot, pl.ds(seg, 1), :], (8, long)),
                long - 7,
                1,
                stride=1,
                stride_axis=0,
            )
            eight = jnp.take_along_axis(eight, flip, axis=0, mode="promise_in_bounds")
            base[seg, chan] = jnp.concatenate([eight, rolled_left(eight, 8)], axis=0).astype(
                jnp.bfloat16
            )

    unroll = 4

    def body(step, carry):
        for u in range(unroll):
            one(step * unroll + u, u)
        return carry

    lax.fori_loop(0, kept // unroll, body, 0)


def prepare(half, scalars, record, blocks, taps):
    segs = (len(blocks) + 1) // 2
    chans, span = record.shape
    kept = chans // 2
    return pl.pallas_call(
        functools.partial(prep_kernel, half),
        out_shape=[
            jax.ShapeDtypeStruct((segs, kept, 16, span + taps), jnp.bfloat16),
            jax.ShapeDtypeStruct((segs, kept, span), jnp.float32),
        ],
        in_specs=[SMEM] + [VMEM] * (1 + len(blocks)),
        out_specs=[VMEM] * 2,
        scratch_shapes=[
            pltpu.VMEM((4, 8, span + taps), jnp.float32),
            pltpu.VMEM((2 * span // LANES, kept * 8, LANES), jnp.float32),
            pltpu.VMEM((segs, chans, 2 * span), jnp.float32),
        ],
        compiler_params=pltpu.CompilerParams(vmem_limit_bytes=VMEM_BYTES),
        cost_estimate=pl.CostEstimate(flops=1, bytes_accessed=10**6, transcendentals=0),
    )(scalars, record, *blocks)


def corr_kernel(pieces, groups, overall, per, skip, scalars, base, level, *refs):
    banks, outs, (total, flat) = refs[:pieces], refs[pieces:-2], refs[-2:]
    _, chans, taps = banks[0].shape
    segs, tmpl, span = total.shape
    parts, half = taps // LANES, 2 * LANES

    at = 0
    for bank in banks:
        size = bank.shape[0] * chans
        rows = bank[...].astype(jnp.float32).reshape(size, taps)
        for m in range(parts):
            flat[m, pl.ds(at, size), :] = rows[:, m * LANES : (m + 1) * LANES]
        at += size
    total[...] = jnp.zeros_like(total)

    def one(chan):
        panel = jnp.concatenate(
            [flat[m, pl.ds(chan, tmpl, stride=chans), :] for m in range(parts)], axis=1
        )
        power = jnp.sum(panel * panel, axis=1, keepdims=True)
        weight = overall * lax.rsqrt(power + 1e-06)
        panel = panel.astype(jnp.bfloat16)
        stacked = jnp.concatenate(
            [panel[:, k * half : (k + 1) * half] for k in range(taps // half)], axis=0
        )
        for seg in range(segs):
            rows = base[seg, chan]
            sheet = jnp.concatenate(
                [rolled_left(rows, 16 * g) for g in range(LANES // 16)], axis=0
            )
            tall = span + taps - half
            hankel = jnp.concatenate([sheet[:, :tall], sheet[:, LANES : LANES + tall]], axis=0)
            product = jnp.dot(stacked, hankel, preferred_element_type=jnp.float32)
            found = product[:tmpl, :span]
            for k in range(1, taps // half):
                found = found + product[k * tmpl : (k + 1) * tmpl, k * half : k * half + span]
            total[seg] += found * level[seg, pl.ds(chan, 1), :] * weight

    unroll = 4

    def body(trip, carry):
        for u in range(unroll):
            one(trip * unroll + u)
        return carry

    lax.fori_loop(0, chans // unroll, body, 0)

    share = tmpl // groups
    mine, sta = lax.axis_index("tm"), lax.axis_index("sta")
    for by in range(groups):
        first = lax.rem(sta + by, groups) * share
        for p in range(share):
            slot = scalars[skip + first + p]
            owner = lax.div(slot, per)
            row = scalars[skip + tmpl + lax.bitwise_xor(owner, mine)] + (slot - owner * per)
            for seg in range(segs):
                outs[seg * groups + by][pl.ds(p, 1), :] = total[seg, pl.ds(row, 1), :]


def correlate(per, skip, scalars, base, level, banks, groups, overall):
    segs, chans, span = level.shape
    taps = banks[0].shape[2]
    tmpl = sum(bank.shape[0] for bank in banks)
    count = segs * groups
    return pl.pallas_call(
        functools.partial(corr_kernel, len(banks), groups, overall, per, skip),
        out_shape=[jax.ShapeDtypeStruct((tmpl // groups, span), jnp.float32)] * count,
        in_specs=[SMEM] + [VMEM] * (2 + len(banks)),
        out_specs=[VMEM] * count,
        scratch_shapes=[
            pltpu.VMEM((segs, tmpl, span), jnp.float32),
            pltpu.VMEM((taps // LANES, tmpl * chans, LANES), jnp.float32),
        ],
        compiler_params=pltpu.CompilerParams(vmem_limit_bytes=VMEM_BYTES),
        cost_estimate=pl.CostEstimate(
            flops=2 * tmpl * chans * taps * span * segs, bytes_accessed=10**7, transcendentals=0
        ),
    )(scalars, base, level, *banks)


def crossed(values, bit):
    return lax.ppermute(values, "tm", [(i, i ^ bit) for i in range(lax.axis_size("tm"))])


def per_device(record, templates, shifts, live_mask, plan):
    count, groups = lax.axis_size("tm"), lax.axis_size("sta")
    per, _, taps = templates.shape
    overall = math.sqrt(taps / (record.shape[0] * groups))
    record, shifts, live_mask = (padded(v, 0, GROUP) for v in (record, shifts, live_mask))
    templates = padded(templates, 1, GROUP)
    shared = count // 4
    kept = record.shape[0] // 2

    def half():
        return lax.rem(lax.div(lax.axis_index("tm"), shared), 2)

    mine = lax.dynamic_slice_in_dim(templates, half() * kept, kept, 1)
    other = lax.dynamic_slice_in_dim(templates, (1 - half()) * kept, kept, 1)
    banks = {0: mine}
    for mask in range(count - shared, 0, -shared):
        banks[mask] = crossed(other if mask & shared else mine, mask)
    after = [(i, i - 1) for i in range(1, count)]
    moved = [
        lax.ppermute(record, "tm", after),
        crossed(record, shared),
        lax.ppermute(record, "tm", [(i, j ^ shared) for i, j in after]),
    ]
    bit = shared // 2
    late = [mask for mask in banks if mask & (count // 2)]
    banks[bit] = crossed(mine, bit)
    for mask in [mask for mask in banks if mask not in (0, bit, *late)]:
        banks[mask | bit] = crossed(banks[mask], bit)

    order = list(range(0, count, shared)) + [mask | bit for mask in range(0, count, shared)]
    lower = bit // 2
    while lower:
        order += [mask | lower for mask in order]
        lower //= 2
    places = np.zeros(count, np.int32)
    for place, mask in enumerate(order):
        places[mask] = place * per
    scalars = jnp.concatenate([shifts, live_mask, plan, jnp.asarray(places)])

    *held, moved = lax.optimization_barrier((*(banks[mask] for mask in late), moved))
    banks.update(zip(late, held))
    base, level = prepare(half, scalars, record, moved, taps)
    for mask in late:
        banks[mask | bit] = crossed(banks[mask], bit)
    *pieces, base = lax.optimization_barrier(
        (*(banks[mask] for mask in order if mask in banks), base)
    )
    while bit > 1:
        bit //= 2
        pieces += [crossed(piece, bit) for piece in pieces]

    skip = shifts.shape[0] + live_mask.shape[0]
    stacks = correlate(per, skip, scalars, base, level, pieces, groups, overall)
    total = stacks[0]
    for by in range(groups):
        pairs = [
            (i * count + j, (i + by) % groups * count + (j ^ shared))
            for i in range(groups)
            for j in range(count)
        ]
        total = total + lax.ppermute(stacks[groups + by], ("sta", "tm"), pairs)
        if by:
            pairs = [(i, (i + by) % groups) for i in range(groups)]
            total = total + lax.ppermute(stacks[by], "sta", pairs)
    return total


def solution(mesh):
    placed = (P("sta", "tm"), P("tm", "sta", None), P("sta"), P("sta"), P())
    return jax.shard_map(
        per_device, mesh=mesh, in_specs=placed, out_specs=P("sta", "tm"), check_vma=False
    )
```

time: 51.2 us -> 47.2 us (0.922)
  Pallas kernels: 20.6 us -> 10.8 us
  starting transfers between devices: 17.8 us -> 22.1 us
  other arithmetic: 0 us -> 1.44 us
  waiting for transfers between devices: 9.3 us -> 10.7 us
  local copies, waits for them, and re-layouts: 3.14 us -> 1.84 us
    pallas_call x3 -> x2, Pallas kernels: 20.6 us -> 10.8 us  [the longest x1 7.4 us: correlate(): pl.pallas_call(functools.partial(corr_kernel, len(banks), groups, overall...]
    ppermute x8 -> x16, starting transfers between devices: 11.7 us -> 16 us  [crossed(): lax.ppermute(values, 'tm', [(i, i ^ bit) for i in range(lax.axis_size('tm...]
    unnamed x12 -> x2, local copies, waits for them, and re-layouts: 3.13 us -> 0.89 us
    ppermute x3, waiting for transfers between devices: 4.52 us -> 5.98 us  [the longest x2 4.63 us: per_device(): total = total + lax.ppermute(stacks[groups + by], ('sta', 'tm'), pairs)]
    ppermute x1, waiting for transfers between devices: 3.41 us -> 2.3 us  [per_device(): lax.ppermute(record, 'tm', [(i, j ^ shared) for i, j in after])]
    dynamic_slice x0 -> x1, local copies, waits for them, and re-layouts: none -> 0.95 us  [per_device(): other = lax.dynamic_slice_in_dim(templates, (1 - half()) * kept, kept, 1)]
    concatenate x0 -> x1, other arithmetic: none -> 0.78 us  [per_device(): scalars = jnp.concatenate([shifts, live_mask, plan, jnp.asarray(places)])]
    ppermute x1, waiting for transfers between devices: 0.01 us -> 0.76 us  [per_device(): lax.ppermute(record, 'tm', after)]
  transfers between devices with their start and end apart: 13 -> 21, of which waited for: 5 -> 10; matrix products, arithmetic and copies ran while one was open for 0% -> 4% of each run, Pallas kernels for 13% -> 7%
where the time goes in v4:
time: 47.2 us; the launch traced here: 46.9 us
  starting transfers between devices  22.1 us (47%)
  Pallas kernels  10.8 us (23%)
  waiting for transfers between devices  10.7 us (23%)
  local copies, waits for them, and re-layouts  1.84 us (4%)
  other arithmetic  1.44 us (3%)
    ppermute x16, starting transfers between devices, crossed(): lax.ppermute(values, 'tm', [(i, i ^ bit) for i in range(lax.axis_size('tm...  16 us
    pallas_call x1, Pallas kernels, correlate(): pl.pallas_call(functools.partial(corr_kernel, len(banks), groups, overall...  7.4 us
    ppermute x2, waiting for transfers between devices, per_device(): total = total + lax.ppermute(stacks[groups + by], ('sta', 'tm'), pairs)  4.63 us
    pallas_call x1, Pallas kernels, prepare(): pl.pallas_call(functools.partial(prep_kernel, half), out_shape=[jax.Shape...  3.39 us
    ppermute x2, starting transfers between devices, per_device(): total = total + lax.ppermute(stacks[groups + by], ('sta', 'tm'), pairs)  3.04 us
    ppermute x1, waiting for transfers between devices, per_device(): lax.ppermute(record, 'tm', [(i, j ^ shared) for i, j in after])  2.3 us
    ppermute x16, waiting for transfers between devices, crossed(): lax.ppermute(values, 'tm', [(i, i ^ bit) for i in range(lax.axis_size('tm...  1.66 us
    ppermute x1, waiting for transfers between devices, per_device(): total = total + lax.ppermute(stacks[by], 'sta', pairs)  1.35 us
  transfers between devices with their start and end apart: 21, of which 10 were waited for; matrix products, arithmetic and copies ran while one was open for 4% of the time, Pallas kernels for 7%

profile of v4, /device:TPU:0, one launch (start us, length us, event | category | flops | bytes accessed | tf_op | source)
XLA Modules:
  0.0 46.9 jit_solution(8935574126250634459)
XLA Ops:
  0.0 3.0 %collective-permute-start.4 = (bf16[48,768]{1,0:T(8,128)(2,1)}, bf16[48,768]{1,0:T(8,128)(2,1)S(1)}, u32[]{:S(2)}, u32[]{:S(2)}) collective-permute-start(bf16[48,768]{1,0:T(8,128)(2,1)} %record.1), channel_id=1, source_target_pairs={{0,4},{1,5},{2,6},{3,7},{4,0},{5,1},{6,2},{7,3},{8,12},{9,13},{10,... | collective-permute-start | bytes 221192 | tf_op jit(solution)/shard_map/ppermute | solution.py:194
  3.0 1.0 %constant_dynamic-slice_fusion = (bf16[4,24,512]{2,1,0:T(8,128)(2,1)S(1)}, bf16[4,24,512]{2,1,0:T(8,128)(2,1)S(1)}) fusion(bf16[4,48,512]{2,1,0:T(8,128)(2,1)} %param.7, s32[]{:T(128)S(6)} %select_n.7, s32[]{:T(128)S(6)} %select_n.6), kind=kLoop, calls=%fused_computation.2 | loop fusion | bytes 393224 | tf_op jit(solution)/shard_map/dynamic_slice | solution.py:210
  4.0 2.5 %collective-permute-start.1 = (bf16[4,24,512]{2,1,0:T(8,128)(2,1)S(1)}, bf16[4,24,512]{2,1,0:T(8,128)(2,1)S(1)}, u32[]{:S(2)}, u32[]{:S(2)}) collective-permute-start(bf16[4,24,512]{2,1,0:T(8,128)(2,1)S(1)} %get-tuple-element.45), channel_id=1, source_target_pairs={{0,12},{1,13},{2,14},{3,15},{4,8},{5,9},{6,10},{7,11},{8,4},{9,5},... | collective-permute-start | bytes 294920 | tf_op jit(solution)/shard_map/ppermute | solution.py:194
  6.5 0.2 collective-permute-start.2
  6.7 1.7 %collective-permute-start = (bf16[4,24,512]{2,1,0:T(8,128)(2,1)S(1)}, bf16[4,24,512]{2,1,0:T(8,128)(2,1)S(1)}, u32[]{:S(2)}, u32[]{:S(2)}) collective-permute-start(bf16[4,24,512]{2,1,0:T(8,128)(2,1)S(1)} %get-tuple-element.45), channel_id=1, source_target_pairs={{0,4},{1,5},{2,6},{3,7},{4,0},{5,1},{6,2},{7,3},{8,12},{9,13},{10,... | collective-permute-start | bytes 294920 | tf_op jit(solution)/shard_map/ppermute | solution.py:194
  8.4 1.3 %collective-permute-start.3 = (bf16[48,768]{1,0:T(8,128)(2,1)}, bf16[48,768]{1,0:T(8,128)(2,1)S(1)}, u32[]{:S(2)}, u32[]{:S(2)}) collective-permute-start(bf16[48,768]{1,0:T(8,128)(2,1)} %record.1), channel_id=1, source_target_pairs={{1,0},{2,1},{3,2},{4,3},{5,4},{6,5},{7,6},{8,7},{9,8},{10,9},{11,1... | collective-permute-start | bytes 221192 | tf_op jit(solution)/shard_map/ppermute | solution.py:216
  9.7 0.0 collective-permute-done.4.refs_1_
  9.7 1.3 %collective-permute-start.5 = (bf16[48,768]{1,0:T(8,128)(2,1)}, bf16[48,768]{1,0:T(8,128)(2,1)S(1)}, u32[]{:S(2)}, u32[]{:S(2)}) collective-permute-start(bf16[48,768]{1,0:T(8,128)(2,1)} %record.1), channel_id=1, source_target_pairs={{1,4},{2,5},{3,6},{4,7},{5,0},{6,1},{7,2},{8,3},{9,12},{10,13},{11... | collective-permute-start | bytes 221192 | tf_op jit(solution)/shard_map/ppermute | solution.py:218
  11.0 0.8 %collective-permute-done.3.refs_0_ = bf16[48,768]{1,0:T(8,128)(2,1)S(1)} collective-permute-done((bf16[48,768]{1,0:T(8,128)(2,1)}, bf16[48,768]{1,0:T(8,128)(2,1)S(1)}, u32[]{:S(2)}, u32[]{:S(2)}) %collective-permute-start.3) | collective-permute-done | bytes 73760 | tf_op jit(solution)/shard_map/ppermute | solution.py:216
  11.8 2.4 %collective-permute-start.6 = (bf16[4,24,512]{2,1,0:T(8,128)(2,1)S(1)}, bf16[4,24,512]{2,1,0:T(8,128)(2,1)S(1)}, u32[]{:S(2)}, u32[]{:S(2)}) collective-permute-start(bf16[4,24,512]{2,1,0:T(8,128)(2,1)S(1)} %get-tuple-element.33.refs_0_), channel_id=1, source_target_pairs={{0,2},{1,3},{2,0},{3,1},{4,6},{5,7},{6,4},{7,5},{8,10},{9,11},{10,... | collective-permute-start | bytes 294920 | tf_op jit(solution)/shard_map/ppermute | solution.py:194
  14.2 2.3 %collective-permute-done.5.refs_2_ = bf16[48,768]{1,0:T(8,128)(2,1)S(1)} collective-permute-done((bf16[48,768]{1,0:T(8,128)(2,1)}, bf16[48,768]{1,0:T(8,128)(2,1)S(1)}, u32[]{:S(2)}, u32[]{:S(2)}) %collective-permute-start.5) | collective-permute-done | bytes 73760 | tf_op jit(solution)/shard_map/ppermute | solution.py:218
  16.5 0.0 collective-permute-done.1.refs_3_
  16.5 0.0 collective-permute-done.2.refs_2_
  16.5 1.5 %collective-permute-start.8 = (bf16[4,24,512]{2,1,0:T(8,128)(2,1)S(1)}, bf16[4,24,512]{2,1,0:T(8,128)(2,1)S(1)}, u32[]{:S(2)}, u32[]{:S(2)}) collective-permute-start(bf16[4,24,512]{2,1,0:T(8,128)(2,1)S(1)} %collective-permute-done.2.refs_2_), channel_id=1, source_target_pairs={{0,2},{1,3},{2,0},{3,1},{4,6},{5,7},{6,4},{7,5},{8,10},{9,11},{10,... | collective-permute-start | bytes 294920 | tf_op jit(solution)/shard_map/ppermute | solution.py:194
  18.0 0.5 %collective-permute-start.9 = (bf16[4,24,512]{2,1,0:T(8,128)(2,1)S(1)}, bf16[4,24,512]{2,1,0:T(8,128)(2,1)S(1)}, u32[]{:S(2)}, u32[]{:S(2)}) collective-permute-start(bf16[4,24,512]{2,1,0:T(8,128)(2,1)S(1)} %collective-permute-done.1.refs_3_), channel_id=1, source_target_pairs={{0,2},{1,3},{2,0},{3,1},{4,6},{5,7},{6,4},{7,5},{8,10},{9,11},{10,... | collective-permute-start | bytes 294920 | tf_op jit(solution)/shard_map/ppermute | solution.py:194
  18.6 0.0 collective-permute-done.refs_1_
  18.6 1.5 %collective-permute-start.7 = (bf16[4,24,512]{2,1,0:T(8,128)(2,1)S(1)}, bf16[4,24,512]{2,1,0:T(8,128)(2,1)S(1)}, u32[]{:S(2)}, u32[]{:S(2)}) collective-permute-start(bf16[4,24,512]{2,1,0:T(8,128)(2,1)S(1)} %collective-permute-done.refs_1_), channel_id=1, source_target_pairs={{0,2},{1,3},{2,0},{3,1},{4,6},{5,7},{6,4},{7,5},{8,10},{9,11},{10,... | collective-permute-start | bytes 294920 | tf_op jit(solution)/shard_map/ppermute | solution.py:194
  20.1 0.8 %pad_add_fusion.scalars = s32[176]{0:T(256)S(1)} fusion(s32[16]{0:T(128)} %constant.21.clone, s32[64]{0:T(128)} %param.10, s32[48]{0:T(128)} %param.9, s32[48]{0:T(128)} %param.8), kind=kLoop, calls=%fused_computation.1 | loop fusion | flops 528 | bytes 1408 | tf_op jit(solution)/shard_map/concatenate | solution.py:234
  20.8 0.9 %copy-done = bf16[48,768]{1,0:T(8,128)(2,1)S(1)} copy-done((bf16[48,768]{1,0:T(8,128)(2,1)S(1)}, bf16[48,768]{1,0:T(8,128)(2,1)}, u32[]{:S(2)}) %copy-start) | copy-done | bytes 73752
  21.7 3.4 %shard_map.64 = (bf16[2,24,16,1280]{3,2,1,0:T(8,128)(2,1)S(1)}, f32[2,24,768]{2,1,0:T(8,128)S(1)}) custom-call(s32[176]{0:T(256)S(1)} %pad_add_fusion.scalars, bf16[48,768]{1,0:T(8,128)(2,1)S(1)} %copy-done, bf16[48,768]{1,0:T(8,128)(2,1)S(1)} %collective-permute-done.3.refs_0_, bf16[48,768]{1,0:T(8,128)(2,1)S(1)} %collective-permute-done.4.refs_1_, ...), custom_call_target="tpu_custom_call" | custom-call | flops 1 | bytes 1000000 | tf_op jit(solution)/shard_map/pallas_call | solution.py:95
  25.1 0.0 collective-permute-done.6.refs_4_
  25.1 0.6 %collective-permute-done.7.refs_5_ = bf16[4,24,512]{2,1,0:T(8,128)(2,1)S(1)} collective-permute-done((bf16[4,24,512]{2,1,0:T(8,128)(2,1)S(1)}, bf16[4,24,512]{2,1,0:T(8,128)(2,1)S(1)}, u32[]{:S(2)}, u32[]{:S(2)}) %collective-permute-start.7) | collective-permute-done | bytes 98336 | tf_op jit(solution)/shard_map/ppermute | solution.py:194
  25.7 0.0 collective-permute-done.8.refs_6_
  25.7 0.0 collective-permute-done.9.refs_7_
  25.7 0.7 %collective-permute-start.10 = (bf16[4,24,512]{2,1,0:T(8,128)(2,1)S(1)}, bf16[4,24,512]{2,1,0:T(8,128)(2,1)S(1)}, u32[]{:S(2)}, u32[]{:S(2)}) collective-permute-start(bf16[4,24,512]{2,1,0:T(8,128)(2,1)S(1)} %get-tuple-element.33.refs_0_), channel_id=1, source_target_pairs={{0,1},{1,0},{2,3},{3,2},{4,5},{5,4},{6,7},{7,6},{8,9},{9,8},{10,11... | collective-permute-start | bytes 294920 | tf_op jit(solution)/shard_map/ppermute | solution.py:194
  26.5 0.1 collective-permute-start.11
  26.6 0.4 collective-permute-start.12
  27.0 0.1 collective-permute-start.13
  27.1 0.4 collective-permute-start.14
  27.5 0.0 collective-permute-done.10.refs_8_
  27.5 0.3 collective-permute-start.15
  27.8 0.0 collective-permute-done.11.refs_9_
  27.8 0.2 collective-permute-start.16
  28.0 0.0 collective-permute-done.12.refs_10_
  28.0 0.3 collective-permute-start.17
  28.3 0.0 collective-permute-done.13.refs_11_
  28.3 0.1 collective-permute-done.14.refs_12_
  28.5 0.4 collective-permute-done.15.refs_13_
  28.8 0.3 collective-permute-done.16.refs_14_
  29.1 0.2 collective-permute-done.17.refs_15_
  29.3 7.4 %shard_map.65 = (f32[32,768]{1,0:T(8,128)S(1)}, f32[32,768]{1,0:T(8,128)S(1)}, f32[32,768]{1,0:T(8,128)S(1)}, f32[32,768]{1,0:T(8,128)S(1)}) custom-call(s32[176]{0:T(256)S(1)} %pad_add_fusion.scalars, bf16[2,24,16,1280]{3,2,1,0:T(8,128)(2,1)S(1)} %get-tuple-element.31.base, f32[2,24,768]{2,1,0:T(8,128)S(1)} %get-tuple-element.32.level, ...), custom_call_target="tpu_custom_call" | custom-call | flops 2415919104 | bytes 10000000 | tf_op jit(solution)/shard_map/pallas_call | solution.py:177
  36.7 1.3 %collective-permute-start.18 = (f32[32,768]{1,0:T(8,128)S(1)}, f32[32,768]{1,0:T(8,128)S(1)}, u32[]{:S(2)}, u32[]{:S(2)}) collective-permute-start(f32[32,768]{1,0:T(8,128)S(1)} %get-tuple-element.42), channel_id=1, source_target_pairs={{0,4},{1,5},{2,6},{3,7},{4,0},{5,1},{6,2},{7,3},{8,12},{9,13},{10,... | collective-permute-start | bytes 294920 | tf_op jit(solution)/shard_map/ppermute | solution.py:257
  38.0 1.7 %collective-permute-start.19 = (f32[32,768]{1,0:T(8,128)S(1)}, f32[32,768]{1,0:T(8,128)S(1)}, u32[]{:S(2)}, u32[]{:S(2)}) collective-permute-start(f32[32,768]{1,0:T(8,128)S(1)} %get-tuple-element.43), channel_id=1, source_target_pairs={{0,20},{1,21},{2,22},{3,23},{4,16},{5,17},{6,18},{7,19},{8,28},{9,... | collective-permute-start | bytes 294920 | tf_op jit(solution)/shard_map/ppermute | solution.py:257
  39.8 0.5 %collective-permute-start.20 = (f32[32,768]{1,0:T(8,128)S(1)}, f32[32,768]{1,0:T(8,128)S(1)}, u32[]{:S(2)}, u32[]{:S(2)}) collective-permute-start(f32[32,768]{1,0:T(8,128)S(1)} %get-tuple-element.44), channel_id=1, source_target_pairs={{0,16},{16,0},{1,17},{17,1},{2,18},{18,2},{3,19},{19,3},{4,20},{20... | collective-permute-start | bytes 294920 | tf_op jit(solution)/shard_map/ppermute | solution.py:260
  40.3 1.7 %collective-permute-done.18 = f32[32,768]{1,0:T(8,128)S(1)} collective-permute-done((f32[32,768]{1,0:T(8,128)S(1)}, f32[32,768]{1,0:T(8,128)S(1)}, u32[]{:S(2)}, u32[]{:S(2)}) %collective-permute-start.18) | collective-permute-done | bytes 98336 | tf_op jit(solution)/shard_map/ppermute | solution.py:257
  42.0 2.9 %collective-permute-done.19 = f32[32,768]{1,0:T(8,128)S(1)} collective-permute-done((f32[32,768]{1,0:T(8,128)S(1)}, f32[32,768]{1,0:T(8,128)S(1)}, u32[]{:S(2)}, u32[]{:S(2)}) %collective-permute-start.19) | collective-permute-done | bytes 98336 | tf_op jit(solution)/shard_map/ppermute | solution.py:257
  44.9 1.3 %collective-permute-done.20 = f32[32,768]{1,0:T(8,128)S(1)} collective-permute-done((f32[32,768]{1,0:T(8,128)S(1)}, f32[32,768]{1,0:T(8,128)S(1)}, u32[]{:S(2)}, u32[]{:S(2)}) %collective-permute-start.20) | collective-permute-done | bytes 98336 | tf_op jit(solution)/shard_map/ppermute | solution.py:260
  46.3 0.7 %add_add_fusion = f32[32,768]{1,0:T(8,128)} fusion(f32[32,768]{1,0:T(8,128)S(1)} %collective-permute-done.20, f32[32,768]{1,0:T(8,128)S(1)} %collective-permute-done.19, f32[32,768]{1,0:T(8,128)S(1)} %get-tuple-element.41, f32[32,768]{1,0:T(8,128)S(1)} %collective-permute-done.18), kind=kLoop, calls=%fused_computation | loop fusion | flops 73728 | bytes 491520 | tf_op jit(solution)/shard_map/add | solution.py:260
  (1 shorter events, 0.0 us)
Async XLA Ops:
  0.0 9.7 %collective-permute-start.4 = (bf16[48,768]{1,0:T(8,128)(2,1)}, bf16[48,768]{1,0:T(8,128)(2,1)S(1)}, u32[]{:S(2)}, u32[]{:S(2)}) collective-permute-start(bf16[48,768]{1,0:T(8,128)(2,1)} %record.1), channel_id=1, source_target_pairs={{0,4},{1,5},{2,6},{3,7},{4,0},{5,1},{6,2},{7,3},{8,12},{9,13},{10,... | collective-permute-start | bytes 221192 | tf_op jit(solution)/shard_map/ppermute | solution.py:194
  4.0 12.6 %collective-permute-start.1 = (bf16[4,24,512]{2,1,0:T(8,128)(2,1)S(1)}, bf16[4,24,512]{2,1,0:T(8,128)(2,1)S(1)}, u32[]{:S(2)}, u32[]{:S(2)}) collective-permute-start(bf16[4,24,512]{2,1,0:T(8,128)(2,1)S(1)} %get-tuple-element.45), channel_id=1, source_target_pairs={{0,12},{1,13},{2,14},{3,15},{4,8},{5,9},{6,10},{7,11},{8,4},{9,5},... | collective-permute-start | bytes 294920 | tf_op jit(solution)/shard_map/ppermute | solution.py:194
  6.5 10.0 %collective-permute-start.2 = (bf16[4,24,512]{2,1,0:T(8,128)(2,1)S(1)}, bf16[4,24,512]{2,1,0:T(8,128)(2,1)S(1)}, u32[]{:S(2)}, u32[]{:S(2)}) collective-permute-start(bf16[4,24,512]{2,1,0:T(8,128)(2,1)S(1)} %get-tuple-element.33.refs_0_), channel_id=1, source_target_pairs={{0,8},{1,9},{2,10},{3,11},{4,12},{5,13},{6,14},{7,15},{8,0},{9,1},... | collective-permute-start | bytes 294920 | tf_op jit(solution)/shard_map/ppermute | solution.py:194
  6.7 11.9 %collective-permute-start = (bf16[4,24,512]{2,1,0:T(8,128)(2,1)S(1)}, bf16[4,24,512]{2,1,0:T(8,128)(2,1)S(1)}, u32[]{:S(2)}, u32[]{:S(2)}) collective-permute-start(bf16[4,24,512]{2,1,0:T(8,128)(2,1)S(1)} %get-tuple-element.45), channel_id=1, source_target_pairs={{0,4},{1,5},{2,6},{3,7},{4,0},{5,1},{6,2},{7,3},{8,12},{9,13},{10,... | collective-permute-start | bytes 294920 | tf_op jit(solution)/shard_map/ppermute | solution.py:194
  8.4 3.4 %collective-permute-start.3 = (bf16[48,768]{1,0:T(8,128)(2,1)}, bf16[48,768]{1,0:T(8,128)(2,1)S(1)}, u32[]{:S(2)}, u32[]{:S(2)}) collective-permute-start(bf16[48,768]{1,0:T(8,128)(2,1)} %record.1), channel_id=1, source_target_pairs={{1,0},{2,1},{3,2},{4,3},{5,4},{6,5},{7,6},{8,7},{9,8},{10,9},{11,1... | collective-permute-start | bytes 221192 | tf_op jit(solution)/shard_map/ppermute | solution.py:216
  9.7 6.8 %collective-permute-start.5 = (bf16[48,768]{1,0:T(8,128)(2,1)}, bf16[48,768]{1,0:T(8,128)(2,1)S(1)}, u32[]{:S(2)}, u32[]{:S(2)}) collective-permute-start(bf16[48,768]{1,0:T(8,128)(2,1)} %record.1), channel_id=1, source_target_pairs={{1,4},{2,5},{3,6},{4,7},{5,0},{6,1},{7,2},{8,3},{9,12},{10,13},{11... | collective-permute-start | bytes 221192 | tf_op jit(solution)/shard_map/ppermute | solution.py:218
  11.8 13.3 %collective-permute-start.6 = (bf16[4,24,512]{2,1,0:T(8,128)(2,1)S(1)}, bf16[4,24,512]{2,1,0:T(8,128)(2,1)S(1)}, u32[]{:S(2)}, u32[]{:S(2)}) collective-permute-start(bf16[4,24,512]{2,1,0:T(8,128)(2,1)S(1)} %get-tuple-element.33.refs_0_), channel_id=1, source_target_pairs={{0,2},{1,3},{2,0},{3,1},{4,6},{5,7},{6,4},{7,5},{8,10},{9,11},{10,... | collective-permute-start | bytes 294920 | tf_op jit(solution)/shard_map/ppermute | solution.py:194
  16.5 9.2 %collective-permute-start.8 = (bf16[4,24,512]{2,1,0:T(8,128)(2,1)S(1)}, bf16[4,24,512]{2,1,0:T(8,128)(2,1)S(1)}, u32[]{:S(2)}, u32[]{:S(2)}) collective-permute-start(bf16[4,24,512]{2,1,0:T(8,128)(2,1)S(1)} %collective-permute-done.2.refs_2_), channel_id=1, source_target_pairs={{0,2},{1,3},{2,0},{3,1},{4,6},{5,7},{6,4},{7,5},{8,10},{9,11},{10,... | collective-permute-start | bytes 294920 | tf_op jit(solution)/shard_map/ppermute | solution.py:194
  18.0 7.7 %collective-permute-start.9 = (bf16[4,24,512]{2,1,0:T(8,128)(2,1)S(1)}, bf16[4,24,512]{2,1,0:T(8,128)(2,1)S(1)}, u32[]{:S(2)}, u32[]{:S(2)}) collective-permute-start(bf16[4,24,512]{2,1,0:T(8,128)(2,1)S(1)} %collective-permute-done.1.refs_3_), channel_id=1, source_target_pairs={{0,2},{1,3},{2,0},{3,1},{4,6},{5,7},{6,4},{7,5},{8,10},{9,11},{10,... | collective-permute-start | bytes 294920 | tf_op jit(solution)/shard_map/ppermute | solution.py:194
  18.6 7.2 %collective-permute-start.7 = (bf16[4,24,512]{2,1,0:T(8,128)(2,1)S(1)}, bf16[4,24,512]{2,1,0:T(8,128)(2,1)S(1)}, u32[]{:S(2)}, u32[]{:S(2)}) collective-permute-start(bf16[4,24,512]{2,1,0:T(8,128)(2,1)S(1)} %collective-permute-done.refs_1_), channel_id=1, source_target_pairs={{0,2},{1,3},{2,0},{3,1},{4,6},{5,7},{6,4},{7,5},{8,10},{9,11},{10,... | collective-permute-start | bytes 294920 | tf_op jit(solution)/shard_map/ppermute | solution.py:194
  20.8 0.9 %copy-start = (bf16[48,768]{1,0:T(8,128)(2,1)S(1)}, bf16[48,768]{1,0:T(8,128)(2,1)}, u32[]{:S(2)}) copy-start(bf16[48,768]{1,0:T(8,128)(2,1)} %record.1) | copy-start | bytes 221188
  25.7 1.8 %collective-permute-start.10 = (bf16[4,24,512]{2,1,0:T(8,128)(2,1)S(1)}, bf16[4,24,512]{2,1,0:T(8,128)(2,1)S(1)}, u32[]{:S(2)}, u32[]{:S(2)}) collective-permute-start(bf16[4,24,512]{2,1,0:T(8,128)(2,1)S(1)} %get-tuple-element.33.refs_0_), channel_id=1, source_target_pairs={{0,1},{1,0},{2,3},{3,2},{4,5},{5,4},{6,7},{7,6},{8,9},{9,8},{10,11... | collective-permute-start | bytes 294920 | tf_op jit(solution)/shard_map/ppermute | solution.py:194
  26.5 1.3 %collective-permute-start.11 = (bf16[4,24,512]{2,1,0:T(8,128)(2,1)S(1)}, bf16[4,24,512]{2,1,0:T(8,128)(2,1)S(1)}, u32[]{:S(2)}, u32[]{:S(2)}) collective-permute-start(bf16[4,24,512]{2,1,0:T(8,128)(2,1)S(1)} %collective-permute-done.refs_1_), channel_id=1, source_target_pairs={{0,1},{1,0},{2,3},{3,2},{4,5},{5,4},{6,7},{7,6},{8,9},{9,8},{10,11... | collective-permute-start | bytes 294920 | tf_op jit(solution)/shard_map/ppermute | solution.py:194
  26.6 1.5 %collective-permute-start.12 = (bf16[4,24,512]{2,1,0:T(8,128)(2,1)S(1)}, bf16[4,24,512]{2,1,0:T(8,128)(2,1)S(1)}, u32[]{:S(2)}, u32[]{:S(2)}) collective-permute-start(bf16[4,24,512]{2,1,0:T(8,128)(2,1)S(1)} %collective-permute-done.2.refs_2_), channel_id=1, source_target_pairs={{0,1},{1,0},{2,3},{3,2},{4,5},{5,4},{6,7},{7,6},{8,9},{9,8},{10,11... | collective-permute-start | bytes 294920 | tf_op jit(solution)/shard_map/ppermute | solution.py:194
  27.0 1.3 %collective-permute-start.13 = (bf16[4,24,512]{2,1,0:T(8,128)(2,1)S(1)}, bf16[4,24,512]{2,1,0:T(8,128)(2,1)S(1)}, u32[]{:S(2)}, u32[]{:S(2)}) collective-permute-start(bf16[4,24,512]{2,1,0:T(8,128)(2,1)S(1)} %collective-permute-done.1.refs_3_), channel_id=1, source_target_pairs={{0,1},{1,0},{2,3},{3,2},{4,5},{5,4},{6,7},{7,6},{8,9},{9,8},{10,11... | collective-permute-start | bytes 294920 | tf_op jit(solution)/shard_map/ppermute | solution.py:194
  27.1 1.4 %collective-permute-start.14 = (bf16[4,24,512]{2,1,0:T(8,128)(2,1)S(1)}, bf16[4,24,512]{2,1,0:T(8,128)(2,1)S(1)}, u32[]{:S(2)}, u32[]{:S(2)}) collective-permute-start(bf16[4,24,512]{2,1,0:T(8,128)(2,1)S(1)} %collective-permute-done.6.refs_4_), channel_id=1, source_target_pairs={{0,1},{1,0},{2,3},{3,2},{4,5},{5,4},{6,7},{7,6},{8,9},{9,8},{10,11... | collective-permute-start | bytes 294920 | tf_op jit(solution)/shard_map/ppermute | solution.py:194
  27.5 1.3 %collective-permute-start.15 = (bf16[4,24,512]{2,1,0:T(8,128)(2,1)S(1)}, bf16[4,24,512]{2,1,0:T(8,128)(2,1)S(1)}, u32[]{:S(2)}, u32[]{:S(2)}) collective-permute-start(bf16[4,24,512]{2,1,0:T(8,128)(2,1)S(1)} %collective-permute-done.7.refs_5_), channel_id=1, source_target_pairs={{0,1},{1,0},{2,3},{3,2},{4,5},{5,4},{6,7},{7,6},{8,9},{9,8},{10,11... | collective-permute-start | bytes 294920 | tf_op jit(solution)/shard_map/ppermute | solution.py:194
  27.8 1.3 %collective-permute-start.16 = (bf16[4,24,512]{2,1,0:T(8,128)(2,1)S(1)}, bf16[4,24,512]{2,1,0:T(8,128)(2,1)S(1)}, u32[]{:S(2)}, u32[]{:S(2)}) collective-permute-start(bf16[4,24,512]{2,1,0:T(8,128)(2,1)S(1)} %collective-permute-done.8.refs_6_), channel_id=1, source_target_pairs={{0,1},{1,0},{2,3},{3,2},{4,5},{5,4},{6,7},{7,6},{8,9},{9,8},{10,11... | collective-permute-start | bytes 294920 | tf_op jit(solution)/shard_map/ppermute | solution.py:194
  28.0 1.3 %collective-permute-start.17 = (bf16[4,24,512]{2,1,0:T(8,128)(2,1)S(1)}, bf16[4,24,512]{2,1,0:T(8,128)(2,1)S(1)}, u32[]{:S(2)}, u32[]{:S(2)}) collective-permute-start(bf16[4,24,512]{2,1,0:T(8,128)(2,1)S(1)} %collective-permute-done.9.refs_7_), channel_id=1, source_target_pairs={{0,1},{1,0},{2,3},{3,2},{4,5},{5,4},{6,7},{7,6},{8,9},{9,8},{10,11... | collective-permute-start | bytes 294920 | tf_op jit(solution)/shard_map/ppermute | solution.py:194
  36.7 5.3 %collective-permute-start.18 = (f32[32,768]{1,0:T(8,128)S(1)}, f32[32,768]{1,0:T(8,128)S(1)}, u32[]{:S(2)}, u32[]{:S(2)}) collective-permute-start(f32[32,768]{1,0:T(8,128)S(1)} %get-tuple-element.42), channel_id=1, source_target_pairs={{0,4},{1,5},{2,6},{3,7},{4,0},{5,1},{6,2},{7,3},{8,12},{9,13},{10,... | collective-permute-start | bytes 294920 | tf_op jit(solution)/shard_map/ppermute | solution.py:257
  38.0 6.9 %collective-permute-start.19 = (f32[32,768]{1,0:T(8,128)S(1)}, f32[32,768]{1,0:T(8,128)S(1)}, u32[]{:S(2)}, u32[]{:S(2)}) collective-permute-start(f32[32,768]{1,0:T(8,128)S(1)} %get-tuple-element.43), channel_id=1, source_target_pairs={{0,20},{1,21},{2,22},{3,23},{4,16},{5,17},{6,18},{7,19},{8,28},{9,... | collective-permute-start | bytes 294920 | tf_op jit(solution)/shard_map/ppermute | solution.py:257
  39.8 6.5 %collective-permute-start.20 = (f32[32,768]{1,0:T(8,128)S(1)}, f32[32,768]{1,0:T(8,128)S(1)}, u32[]{:S(2)}, u32[]{:S(2)}) collective-permute-start(f32[32,768]{1,0:T(8,128)S(1)} %get-tuple-element.44), channel_id=1, source_target_pairs={{0,16},{16,0},{1,17},{17,1},{2,18},{18,2},{3,19},{19,3},{4,20},{20... | collective-permute-start | bytes 294920 | tf_op jit(solution)/shard_map/ppermute | solution.py:260

commit v5 on v4

--- a/solution.py
+++ b/solution.py
@@ -31,21 +31,22 @@
 
 def prep_kernel(half, scalars, record, *refs):
     blocks, (base, level, lines, flat, ext) = refs[:-5], refs[-5:]
-    segs = (len(blocks) + 1) // 2
+    segs = len(blocks)
     chans, span = record.shape
     kept = base.shape[1]
     taps = base.shape[3] - span
     width, long = 2 * span, span + taps
     start = half() * kept
 
-    sides = (record, *blocks)
+    rim, *others = blocks
+    for side, block in enumerate((record, rim)):
+        ext[:, side * span : (side + 1) * span] = block[...].astype(jnp.float32)
     for seg in range(segs):
-        for side in range(2):
-            ext[seg, :, side * span : (side + 1) * span] = sides[2 * seg + side][...].astype(
-                jnp.float32
-            )
         for first in range(0, kept, 8):
-            both = ext[seg, pl.ds(pl.multiple_of(start + first, 8), 8), :]
+            if seg == 0:
+                both = ext[pl.ds(pl.multiple_of(start + first, 8), 8), :]
+            else:
+                both = others[seg - 1][...].astype(jnp.float32)[first : first + 8, :]
             window, reach = both * both, 1
             while reach < taps:
                 window = window + rolled_left(window, reach)
@@ -89,7 +90,7 @@
 
 
 def prepare(half, scalars, record, blocks, taps):
-    segs = (len(blocks) + 1) // 2
+    segs = len(blocks)
     chans, span = record.shape
     kept = chans // 2
     return pl.pallas_call(
@@ -103,7 +104,7 @@
         scratch_shapes=[
             pltpu.VMEM((4, 8, span + taps), jnp.float32),
             pltpu.VMEM((2 * span // LANES, kept * 8, LANES), jnp.float32),
-            pltpu.VMEM((segs, chans, 2 * span), jnp.float32),
+            pltpu.VMEM((chans, 2 * span), jnp.float32),
         ],
         compiler_params=pltpu.CompilerParams(vmem_limit_bytes=VMEM_BYTES),
         cost_estimate=pl.CostEstimate(flops=1, bytes_accessed=10**6, transcendentals=0),
@@ -148,7 +149,7 @@
                 found = found + product[k * tmpl : (k + 1) * tmpl, k * half : k * half + span]
             total[seg] += found * level[seg, pl.ds(chan, 1), :] * weight
 
-    unroll = 4
+    unroll = math.gcd(chans, 8)
 
     def body(trip, carry):
         for u in range(unroll):
@@ -212,11 +213,11 @@
     for mask in range(count - shared, 0, -shared):
         banks[mask] = crossed(other if mask & shared else mine, mask)
     after = [(i, i - 1) for i in range(1, count)]
-    moved = [
-        lax.ppermute(record, "tm", after),
-        crossed(record, shared),
-        lax.ppermute(record, "tm", [(i, j ^ shared) for i, j in after]),
-    ]
+    rim = lax.ppermute(record, "tm", after)
+    given = jnp.concatenate(
+        [lax.dynamic_slice_in_dim(v, (1 - half()) * kept, kept, 0) for v in (record, rim)], axis=1
+    )
+    moved = [rim, crossed(given, shared)]
     bit = shared // 2
     late = [mask for mask in banks if mask & (count // 2)]
     banks[bit] = crossed(mine, bit)
@@ -233,8 +234,6 @@
         places[mask] = place * per
     scalars = jnp.concatenate([shifts, live_mask, plan, jnp.asarray(places)])
 
-    *held, moved = lax.optimization_barrier((*(banks[mask] for mask in late), moved))
-    banks.update(zip(late, held))
     base, level = prepare(half, scalars, record, moved, taps)
     for mask in late:
         banks[mask | bit] = crossed(banks[mask], bit)

time: 47.2 us -> 44.1 us (0.934)
  starting transfers between devices: 22.1 us -> 18.9 us
  local copies, waits for them, and re-layouts: 1.84 us -> 2.62 us
  Pallas kernels: 10.8 us -> 10.2 us
    ppermute x16, starting transfers between devices: 16 us -> 14.1 us  [crossed(): lax.ppermute(values, 'tm', [(i, i ^ bit) for i in range(lax.axis_size('tm...]
    ppermute x2 -> x1, waiting for transfers between devices: 3.07 us -> 1.29 us  [per_device(): rim = lax.ppermute(record, 'tm', after)]
    ppermute x16, waiting for transfers between devices: 1.66 us -> 3.35 us  [crossed(): lax.ppermute(values, 'tm', [(i, i ^ bit) for i in range(lax.axis_size('tm...]
    ppermute x2 -> x1, starting transfers between devices: 2.57 us -> 1.28 us  [per_device(): rim = lax.ppermute(record, 'tm', after)]
    dynamic_slice x0 -> x2, local copies, waits for them, and re-layouts: none -> 0.78 us  [per_device(): lax.dynamic_slice_in_dim(v, (1 - half()) * kept, kept, 0)]
    pallas_call x1, Pallas kernels: 7.4 us -> 6.79 us  [correlate(): pl.pallas_call(functools.partial(corr_kernel, len(banks), groups, overall...]
  transfers between devices with their start and end apart: 21 -> 20, of which waited for: 10 -> 10; matrix products, arithmetic and copies ran while one was open for 4% -> 4% of each run, Pallas kernels for 7% -> 8%
where the time goes in v5:
time: 44.1 us; the launch traced here: 43.8 us
  starting transfers between devices  18.9 us (43%)
  waiting for transfers between devices  10.6 us (24%)
  Pallas kernels  10.2 us (23%)
  local copies, waits for them, and re-layouts  2.62 us (6%)
  other arithmetic  1.45 us (3%)
    ppermute x16, starting transfers between devices, crossed(): lax.ppermute(values, 'tm', [(i, i ^ bit) for i in range(lax.axis_size('tm...  14.1 us
    pallas_call x1, Pallas kernels, correlate(): pl.pallas_call(functools.partial(corr_kernel, len(banks), groups, overall...  6.79 us
    ppermute x2, waiting for transfers between devices, per_device(): total = total + lax.ppermute(stacks[groups + by], ('sta', 'tm'), pairs)  4.59 us
    pallas_call x1, Pallas kernels, prepare(): pl.pallas_call(functools.partial(prep_kernel, half), out_shape=[jax.Shape...  3.38 us
    ppermute x16, waiting for transfers between devices, crossed(): lax.ppermute(values, 'tm', [(i, i ^ bit) for i in range(lax.axis_size('tm...  3.35 us
    ppermute x2, starting transfers between devices, per_device(): total = total + lax.ppermute(stacks[groups + by], ('sta', 'tm'), pairs)  3.03 us
    ppermute x1, waiting for transfers between devices, per_device(): total = total + lax.ppermute(stacks[by], 'sta', pairs)  1.33 us
    ppermute x1, waiting for transfers between devices, per_device(): rim = lax.ppermute(record, 'tm', after)  1.29 us
  transfers between devices with their start and end apart: 20, of which 10 were waited for; matrix products, arithmetic and copies ran while one was open for 4% of the time, Pallas kernels for 8%

profile of v5, /device:TPU:0, one launch (start us, length us, event | category | flops | bytes accessed | tf_op | source)
XLA Modules:
  0.0 43.8 jit_solution(1676599044393512293)
XLA Ops:
  0.0 1.0 %constant_dynamic-slice_fusion.2 = (bf16[4,24,512]{2,1,0:T(8,128)(2,1)S(1)}, bf16[4,24,512]{2,1,0:T(8,128)(2,1)S(1)}) fusion(bf16[4,48,512]{2,1,0:T(8,128)(2,1)} %param.7, s32[]{:T(128)S(6)} %select_n.9, s32[]{:T(128)S(6)} %select_n.8), kind=kLoop, calls=%fused_computation.5 | loop fusion | bytes 393224 | tf_op jit(solution)/shard_map/dynamic_slice | solution.py:211
  1.0 5.1 %collective-permute-start.2 = (bf16[4,24,512]{2,1,0:T(8,128)(2,1)S(1)}, bf16[4,24,512]{2,1,0:T(8,128)(2,1)S(1)}, u32[]{:S(2)}, u32[]{:S(2)}) collective-permute-start(bf16[4,24,512]{2,1,0:T(8,128)(2,1)S(1)} %get-tuple-element.35), channel_id=1, source_target_pairs={{0,12},{1,13},{2,14},{3,15},{4,8},{5,9},{6,10},{7,11},{8,4},{9,5},... | collective-permute-start | bytes 294920 | tf_op jit(solution)/shard_map/ppermute | solution.py:195
  6.1 0.0 collective-permute-start
  6.1 1.5 %collective-permute-start.3 = (bf16[4,24,512]{2,1,0:T(8,128)(2,1)S(1)}, bf16[4,24,512]{2,1,0:T(8,128)(2,1)S(1)}, u32[]{:S(2)}, u32[]{:S(2)}) collective-permute-start(bf16[4,24,512]{2,1,0:T(8,128)(2,1)S(1)} %get-tuple-element.23.refs_0_), channel_id=1, source_target_pairs={{0,2},{1,3},{2,0},{3,1},{4,6},{5,7},{6,4},{7,5},{8,10},{9,11},{10,... | collective-permute-start | bytes 294920 | tf_op jit(solution)/shard_map/ppermute | solution.py:195
  7.6 0.8 %collective-permute-start.1 = (bf16[4,24,512]{2,1,0:T(8,128)(2,1)S(1)}, bf16[4,24,512]{2,1,0:T(8,128)(2,1)S(1)}, u32[]{:S(2)}, u32[]{:S(2)}) collective-permute-start(bf16[4,24,512]{2,1,0:T(8,128)(2,1)S(1)} %get-tuple-element.23.refs_0_), channel_id=1, source_target_pairs={{0,8},{1,9},{2,10},{3,11},{4,12},{5,13},{6,14},{7,15},{8,0},{9,1},... | collective-permute-start | bytes 294920 | tf_op jit(solution)/shard_map/ppermute | solution.py:195
  8.4 1.3 %collective-permute-start.7 = (bf16[48,768]{1,0:T(8,128)(2,1)}, bf16[48,768]{1,0:T(8,128)(2,1)S(1)}, u32[]{:S(2)}, u32[]{:S(2)}) collective-permute-start(bf16[48,768]{1,0:T(8,128)(2,1)} %record.1), channel_id=1, source_target_pairs={{1,0},{2,1},{3,2},{4,3},{5,4},{6,5},{7,6},{8,7},{9,8},{10,9},{11,1... | collective-permute-start | bytes 221192 | tf_op jit(solution)/shard_map/ppermute | solution.py:216
  9.7 0.8 %constant_dynamic-slice_fusion.1 = bf16[24,768]{1,0:T(8,128)(2,1)S(1)} fusion(bf16[48,768]{1,0:T(8,128)(2,1)} %record.1, s32[]{:T(128)S(6)} %select_n.9), kind=kLoop, calls=%fused_computation.4 | loop fusion | bytes 73732 | tf_op jit(solution)/shard_map/dynamic_slice | solution.py:218
  10.4 1.3 %collective-permute-done.7.refs_0_ = bf16[48,768]{1,0:T(8,128)(2,1)S(1)} collective-permute-done((bf16[48,768]{1,0:T(8,128)(2,1)}, bf16[48,768]{1,0:T(8,128)(2,1)S(1)}, u32[]{:S(2)}, u32[]{:S(2)}) %collective-permute-start.7) | collective-permute-done | bytes 73760 | tf_op jit(solution)/shard_map/ppermute | solution.py:216
  11.8 2.4 %collective-permute-start.8 = (bf16[24,1536]{1,0:T(8,128)(2,1)S(1)}, bf16[24,1536]{1,0:T(8,128)(2,1)S(1)}, u32[]{:S(2)}, u32[]{:S(2)}) collective-permute-start(bf16[24,1536]{1,0:T(8,128)(2,1)S(1)} %pad_maximum_fusion), channel_id=1, source_target_pairs={{0,4},{1,5},{2,6},{3,7},{4,0},{5,1},{6,2},{7,3},{8,12},{9,13},{10,... | collective-permute-start | bytes 221192 | tf_op jit(solution)/shard_map/ppermute | solution.py:195
  14.1 0.0 collective-permute-done.2.refs_3_
  14.1 0.4 collective-permute-start.6
  14.5 0.0 collective-permute-done.refs_1_
  14.5 1.7 %collective-permute-start.4 = (bf16[4,24,512]{2,1,0:T(8,128)(2,1)S(1)}, bf16[4,24,512]{2,1,0:T(8,128)(2,1)S(1)}, u32[]{:S(2)}, u32[]{:S(2)}) collective-permute-start(bf16[4,24,512]{2,1,0:T(8,128)(2,1)S(1)} %collective-permute-done.refs_1_), channel_id=1, source_target_pairs={{0,2},{1,3},{2,0},{3,1},{4,6},{5,7},{6,4},{7,5},{8,10},{9,11},{10,... | collective-permute-start | bytes 294920 | tf_op jit(solution)/shard_map/ppermute | solution.py:195
  16.2 0.0 collective-permute-done.1.refs_2_
  16.2 0.4 collective-permute-start.5
  16.5 0.8 %pad_add_fusion.scalars = s32[176]{0:T(256)S(1)} fusion(s32[16]{0:T(128)} %constant.21.clone, s32[64]{0:T(128)} %param.10, s32[48]{0:T(128)} %param.9, s32[48]{0:T(128)} %param.8), kind=kLoop, calls=%fused_computation.2 | loop fusion | flops 528 | bytes 1408 | tf_op jit(solution)/shard_map/concatenate | solution.py:235
  17.3 0.0 collective-permute-done.8.refs_1_
  17.3 0.0 copy-start
  17.3 0.9 %copy-done = bf16[48,768]{1,0:T(8,128)(2,1)S(1)} copy-done((bf16[48,768]{1,0:T(8,128)(2,1)S(1)}, bf16[48,768]{1,0:T(8,128)(2,1)}, u32[]{:S(2)}) %copy-start) | copy-done | bytes 73752
  18.2 3.4 %shard_map.64 = (bf16[2,24,16,1280]{3,2,1,0:T(8,128)(2,1)S(1)}, f32[2,24,768]{2,1,0:T(8,128)S(1)}) custom-call(s32[176]{0:T(256)S(1)} %pad_add_fusion.scalars, bf16[48,768]{1,0:T(8,128)(2,1)S(1)} %copy-done, bf16[48,768]{1,0:T(8,128)(2,1)S(1)} %collective-permute-done.7.refs_0_, bf16[24,1536]{1,0:T(8,128)(2,1)S(1)} %collective-permute-done.8.refs_1_), custom_call_target="tpu_custom_call" | custom-call | flops 1 | bytes 1000000 | tf_op jit(solution)/shard_map/pallas_call | solution.py:96
  21.6 0.0 collective-permute-done.3.refs_4_
  21.6 0.0 collective-permute-done.6.refs_7_
  21.6 0.0 collective-permute-done.4.refs_5_
  21.6 2.1 %collective-permute-done.5.refs_6_ = bf16[4,24,512]{2,1,0:T(8,128)(2,1)S(1)} collective-permute-done((bf16[4,24,512]{2,1,0:T(8,128)(2,1)S(1)}, bf16[4,24,512]{2,1,0:T(8,128)(2,1)S(1)}, u32[]{:S(2)}, u32[]{:S(2)}) %collective-permute-start.5) | collective-permute-done | bytes 98336 | tf_op jit(solution)/shard_map/ppermute | solution.py:195
  23.7 0.1 collective-permute-start.9
  23.9 0.4 collective-permute-start.10
  24.3 0.1 collective-permute-start.11
  24.4 0.4 collective-permute-start.12
  24.8 0.1 collective-permute-start.13
  24.9 0.2 collective-permute-done.9.refs_8_
  25.0 0.2 collective-permute-start.14
  25.3 0.0 collective-permute-done.10.refs_9_
  25.3 0.3 collective-permute-start.15
  25.6 0.0 collective-permute-done.11.refs_10_
  25.6 0.2 collective-permute-start.16
  25.8 0.0 collective-permute-done.12.refs_11_
  25.8 0.3 collective-permute-done.13.refs_12_
  26.1 0.3 collective-permute-done.14.refs_13_
  26.3 0.2 collective-permute-done.15.refs_14_
  26.6 0.3 collective-permute-done.16.refs_15_
  26.9 6.8 %shard_map.65 = (f32[32,768]{1,0:T(8,128)S(1)}, f32[32,768]{1,0:T(8,128)S(1)}, f32[32,768]{1,0:T(8,128)S(1)}, f32[32,768]{1,0:T(8,128)S(1)}) custom-call(s32[176]{0:T(256)S(1)} %pad_add_fusion.scalars, bf16[2,24,16,1280]{3,2,1,0:T(8,128)(2,1)S(1)} %get-tuple-element.21.base, f32[2,24,768]{2,1,0:T(8,128)S(1)} %get-tuple-element.22.level, ...), custom_call_target="tpu_custom_call" | custom-call | flops 2415919104 | bytes 10000000 | tf_op jit(solution)/shard_map/pallas_call | solution.py:178
  33.7 0.2 collective-permute-start.17
  33.9 2.8 %collective-permute-start.18 = (f32[32,768]{1,0:T(8,128)S(1)}, f32[32,768]{1,0:T(8,128)S(1)}, u32[]{:S(2)}, u32[]{:S(2)}) collective-permute-start(f32[32,768]{1,0:T(8,128)S(1)} %get-tuple-element.33), channel_id=1, source_target_pairs={{0,20},{1,21},{2,22},{3,23},{4,16},{5,17},{6,18},{7,19},{8,28},{9,... | collective-permute-start | bytes 294920 | tf_op jit(solution)/shard_map/ppermute | solution.py:256
  36.7 0.5 %collective-permute-start.19 = (f32[32,768]{1,0:T(8,128)S(1)}, f32[32,768]{1,0:T(8,128)S(1)}, u32[]{:S(2)}, u32[]{:S(2)}) collective-permute-start(f32[32,768]{1,0:T(8,128)S(1)} %get-tuple-element.34), channel_id=1, source_target_pairs={{0,16},{16,0},{1,17},{17,1},{2,18},{18,2},{3,19},{19,3},{4,20},{20... | collective-permute-start | bytes 294920 | tf_op jit(solution)/shard_map/ppermute | solution.py:259
  37.2 2.1 %collective-permute-done.17 = f32[32,768]{1,0:T(8,128)S(1)} collective-permute-done((f32[32,768]{1,0:T(8,128)S(1)}, f32[32,768]{1,0:T(8,128)S(1)}, u32[]{:S(2)}, u32[]{:S(2)}) %collective-permute-start.17) | collective-permute-done | bytes 98336 | tf_op jit(solution)/shard_map/ppermute | solution.py:256
  39.4 2.5 %collective-permute-done.18 = f32[32,768]{1,0:T(8,128)S(1)} collective-permute-done((f32[32,768]{1,0:T(8,128)S(1)}, f32[32,768]{1,0:T(8,128)S(1)}, u32[]{:S(2)}, u32[]{:S(2)}) %collective-permute-start.18) | collective-permute-done | bytes 98336 | tf_op jit(solution)/shard_map/ppermute | solution.py:256
  41.8 1.3 %collective-permute-done.19 = f32[32,768]{1,0:T(8,128)S(1)} collective-permute-done((f32[32,768]{1,0:T(8,128)S(1)}, f32[32,768]{1,0:T(8,128)S(1)}, u32[]{:S(2)}, u32[]{:S(2)}) %collective-permute-start.19) | collective-permute-done | bytes 98336 | tf_op jit(solution)/shard_map/ppermute | solution.py:259
  43.1 0.7 %add_add_fusion = f32[32,768]{1,0:T(8,128)} fusion(f32[32,768]{1,0:T(8,128)S(1)} %collective-permute-done.19, f32[32,768]{1,0:T(8,128)S(1)} %collective-permute-done.18, f32[32,768]{1,0:T(8,128)S(1)} %get-tuple-element.31, f32[32,768]{1,0:T(8,128)S(1)} %collective-permute-done.17), kind=kLoop, calls=%fused_computation | loop fusion | flops 73728 | bytes 491520 | tf_op jit(solution)/shard_map/add | solution.py:259
  (2 shorter events, 0.0 us)
Async XLA Ops:
  1.0 13.2 %collective-permute-start.2 = (bf16[4,24,512]{2,1,0:T(8,128)(2,1)S(1)}, bf16[4,24,512]{2,1,0:T(8,128)(2,1)S(1)}, u32[]{:S(2)}, u32[]{:S(2)}) collective-permute-start(bf16[4,24,512]{2,1,0:T(8,128)(2,1)S(1)} %get-tuple-element.35), channel_id=1, source_target_pairs={{0,12},{1,13},{2,14},{3,15},{4,8},{5,9},{6,10},{7,11},{8,4},{9,5},... | collective-permute-start | bytes 294920 | tf_op jit(solution)/shard_map/ppermute | solution.py:195
  6.1 8.4 %collective-permute-start = (bf16[4,24,512]{2,1,0:T(8,128)(2,1)S(1)}, bf16[4,24,512]{2,1,0:T(8,128)(2,1)S(1)}, u32[]{:S(2)}, u32[]{:S(2)}) collective-permute-start(bf16[4,24,512]{2,1,0:T(8,128)(2,1)S(1)} %get-tuple-element.35), channel_id=1, source_target_pairs={{0,4},{1,5},{2,6},{3,7},{4,0},{5,1},{6,2},{7,3},{8,12},{9,13},{10,... | collective-permute-start | bytes 294920 | tf_op jit(solution)/shard_map/ppermute | solution.py:195
  6.1 15.5 %collective-permute-start.3 = (bf16[4,24,512]{2,1,0:T(8,128)(2,1)S(1)}, bf16[4,24,512]{2,1,0:T(8,128)(2,1)S(1)}, u32[]{:S(2)}, u32[]{:S(2)}) collective-permute-start(bf16[4,24,512]{2,1,0:T(8,128)(2,1)S(1)} %get-tuple-element.23.refs_0_), channel_id=1, source_target_pairs={{0,2},{1,3},{2,0},{3,1},{4,6},{5,7},{6,4},{7,5},{8,10},{9,11},{10,... | collective-permute-start | bytes 294920 | tf_op jit(solution)/shard_map/ppermute | solution.py:195
  7.6 8.6 %collective-permute-start.1 = (bf16[4,24,512]{2,1,0:T(8,128)(2,1)S(1)}, bf16[4,24,512]{2,1,0:T(8,128)(2,1)S(1)}, u32[]{:S(2)}, u32[]{:S(2)}) collective-permute-start(bf16[4,24,512]{2,1,0:T(8,128)(2,1)S(1)} %get-tuple-element.23.refs_0_), channel_id=1, source_target_pairs={{0,8},{1,9},{2,10},{3,11},{4,12},{5,13},{6,14},{7,15},{8,0},{9,1},... | collective-permute-start | bytes 294920 | tf_op jit(solution)/shard_map/ppermute | solution.py:195
  8.4 3.4 %collective-permute-start.7 = (bf16[48,768]{1,0:T(8,128)(2,1)}, bf16[48,768]{1,0:T(8,128)(2,1)S(1)}, u32[]{:S(2)}, u32[]{:S(2)}) collective-permute-start(bf16[48,768]{1,0:T(8,128)(2,1)} %record.1), channel_id=1, source_target_pairs={{1,0},{2,1},{3,2},{4,3},{5,4},{6,5},{7,6},{8,7},{9,8},{10,9},{11,1... | collective-permute-start | bytes 221192 | tf_op jit(solution)/shard_map/ppermute | solution.py:216
  11.8 5.6 %collective-permute-start.8 = (bf16[24,1536]{1,0:T(8,128)(2,1)S(1)}, bf16[24,1536]{1,0:T(8,128)(2,1)S(1)}, u32[]{:S(2)}, u32[]{:S(2)}) collective-permute-start(bf16[24,1536]{1,0:T(8,128)(2,1)S(1)} %pad_maximum_fusion), channel_id=1, source_target_pairs={{0,4},{1,5},{2,6},{3,7},{4,0},{5,1},{6,2},{7,3},{8,12},{9,13},{10,... | collective-permute-start | bytes 221192 | tf_op jit(solution)/shard_map/ppermute | solution.py:195
  14.1 7.5 %collective-permute-start.6 = (bf16[4,24,512]{2,1,0:T(8,128)(2,1)S(1)}, bf16[4,24,512]{2,1,0:T(8,128)(2,1)S(1)}, u32[]{:S(2)}, u32[]{:S(2)}) collective-permute-start(bf16[4,24,512]{2,1,0:T(8,128)(2,1)S(1)} %collective-permute-done.2.refs_3_), channel_id=1, source_target_pairs={{0,2},{1,3},{2,0},{3,1},{4,6},{5,7},{6,4},{7,5},{8,10},{9,11},{10,... | collective-permute-start | bytes 294920 | tf_op jit(solution)/shard_map/ppermute | solution.py:195
  14.5 7.1 %collective-permute-start.4 = (bf16[4,24,512]{2,1,0:T(8,128)(2,1)S(1)}, bf16[4,24,512]{2,1,0:T(8,128)(2,1)S(1)}, u32[]{:S(2)}, u32[]{:S(2)}) collective-permute-start(bf16[4,24,512]{2,1,0:T(8,128)(2,1)S(1)} %collective-permute-done.refs_1_), channel_id=1, source_target_pairs={{0,2},{1,3},{2,0},{3,1},{4,6},{5,7},{6,4},{7,5},{8,10},{9,11},{10,... | collective-permute-start | bytes 294920 | tf_op jit(solution)/shard_map/ppermute | solution.py:195
  16.2 7.6 %collective-permute-start.5 = (bf16[4,24,512]{2,1,0:T(8,128)(2,1)S(1)}, bf16[4,24,512]{2,1,0:T(8,128)(2,1)S(1)}, u32[]{:S(2)}, u32[]{:S(2)}) collective-permute-start(bf16[4,24,512]{2,1,0:T(8,128)(2,1)S(1)} %collective-permute-done.1.refs_2_), channel_id=1, source_target_pairs={{0,2},{1,3},{2,0},{3,1},{4,6},{5,7},{6,4},{7,5},{8,10},{9,11},{10,... | collective-permute-start | bytes 294920 | tf_op jit(solution)/shard_map/ppermute | solution.py:195
  17.3 0.9 %copy-start = (bf16[48,768]{1,0:T(8,128)(2,1)S(1)}, bf16[48,768]{1,0:T(8,128)(2,1)}, u32[]{:S(2)}) copy-start(bf16[48,768]{1,0:T(8,128)(2,1)} %record.1) | copy-start | bytes 221188
  23.7 1.3 %collective-permute-start.9 = (bf16[4,24,512]{2,1,0:T(8,128)(2,1)S(1)}, bf16[4,24,512]{2,1,0:T(8,128)(2,1)S(1)}, u32[]{:S(2)}, u32[]{:S(2)}) collective-permute-start(bf16[4,24,512]{2,1,0:T(8,128)(2,1)S(1)} %get-tuple-element.23.refs_0_), channel_id=1, source_target_pairs={{0,1},{1,0},{2,3},{3,2},{4,5},{5,4},{6,7},{7,6},{8,9},{9,8},{10,11... | collective-permute-start | bytes 294920 | tf_op jit(solution)/shard_map/ppermute | solution.py:195
  23.9 1.4 %collective-permute-start.10 = (bf16[4,24,512]{2,1,0:T(8,128)(2,1)S(1)}, bf16[4,24,512]{2,1,0:T(8,128)(2,1)S(1)}, u32[]{:S(2)}, u32[]{:S(2)}) collective-permute-start(bf16[4,24,512]{2,1,0:T(8,128)(2,1)S(1)} %collective-permute-done.refs_1_), channel_id=1, source_target_pairs={{0,1},{1,0},{2,3},{3,2},{4,5},{5,4},{6,7},{7,6},{8,9},{9,8},{10,11... | collective-permute-start | bytes 294920 | tf_op jit(solution)/shard_map/ppermute | solution.py:195
  24.3 1.3 %collective-permute-start.11 = (bf16[4,24,512]{2,1,0:T(8,128)(2,1)S(1)}, bf16[4,24,512]{2,1,0:T(8,128)(2,1)S(1)}, u32[]{:S(2)}, u32[]{:S(2)}) collective-permute-start(bf16[4,24,512]{2,1,0:T(8,128)(2,1)S(1)} %collective-permute-done.1.refs_2_), channel_id=1, source_target_pairs={{0,1},{1,0},{2,3},{3,2},{4,5},{5,4},{6,7},{7,6},{8,9},{9,8},{10,11... | collective-permute-start | bytes 294920 | tf_op jit(solution)/shard_map/ppermute | solution.py:195
  24.4 1.4 %collective-permute-start.12 = (bf16[4,24,512]{2,1,0:T(8,128)(2,1)S(1)}, bf16[4,24,512]{2,1,0:T(8,128)(2,1)S(1)}, u32[]{:S(2)}, u32[]{:S(2)}) collective-permute-start(bf16[4,24,512]{2,1,0:T(8,128)(2,1)S(1)} %collective-permute-done.2.refs_3_), channel_id=1, source_target_pairs={{0,1},{1,0},{2,3},{3,2},{4,5},{5,4},{6,7},{7,6},{8,9},{9,8},{10,11... | collective-permute-start | bytes 294920 | tf_op jit(solution)/shard_map/ppermute | solution.py:195
  24.8 1.3 %collective-permute-start.13 = (bf16[4,24,512]{2,1,0:T(8,128)(2,1)S(1)}, bf16[4,24,512]{2,1,0:T(8,128)(2,1)S(1)}, u32[]{:S(2)}, u32[]{:S(2)}) collective-permute-start(bf16[4,24,512]{2,1,0:T(8,128)(2,1)S(1)} %collective-permute-done.3.refs_4_), channel_id=1, source_target_pairs={{0,1},{1,0},{2,3},{3,2},{4,5},{5,4},{6,7},{7,6},{8,9},{9,8},{10,11... | collective-permute-start | bytes 294920 | tf_op jit(solution)/shard_map/ppermute | solution.py:195
  25.0 1.3 %collective-permute-start.14 = (bf16[4,24,512]{2,1,0:T(8,128)(2,1)S(1)}, bf16[4,24,512]{2,1,0:T(8,128)(2,1)S(1)}, u32[]{:S(2)}, u32[]{:S(2)}) collective-permute-start(bf16[4,24,512]{2,1,0:T(8,128)(2,1)S(1)} %collective-permute-done.4.refs_5_), channel_id=1, source_target_pairs={{0,1},{1,0},{2,3},{3,2},{4,5},{5,4},{6,7},{7,6},{8,9},{9,8},{10,11... | collective-permute-start | bytes 294920 | tf_op jit(solution)/shard_map/ppermute | solution.py:195
  25.3 1.3 %collective-permute-start.15 = (bf16[4,24,512]{2,1,0:T(8,128)(2,1)S(1)}, bf16[4,24,512]{2,1,0:T(8,128)(2,1)S(1)}, u32[]{:S(2)}, u32[]{:S(2)}) collective-permute-start(bf16[4,24,512]{2,1,0:T(8,128)(2,1)S(1)} %collective-permute-done.5.refs_6_), channel_id=1, source_target_pairs={{0,1},{1,0},{2,3},{3,2},{4,5},{5,4},{6,7},{7,6},{8,9},{9,8},{10,11... | collective-permute-start | bytes 294920 | tf_op jit(solution)/shard_map/ppermute | solution.py:195
  25.6 1.3 %collective-permute-start.16 = (bf16[4,24,512]{2,1,0:T(8,128)(2,1)S(1)}, bf16[4,24,512]{2,1,0:T(8,128)(2,1)S(1)}, u32[]{:S(2)}, u32[]{:S(2)}) collective-permute-start(bf16[4,24,512]{2,1,0:T(8,128)(2,1)S(1)} %collective-permute-done.6.refs_7_), channel_id=1, source_target_pairs={{0,1},{1,0},{2,3},{3,2},{4,5},{5,4},{6,7},{7,6},{8,9},{9,8},{10,11... | collective-permute-start | bytes 294920 | tf_op jit(solution)/shard_map/ppermute | solution.py:195
  33.7 5.7 %collective-permute-start.17 = (f32[32,768]{1,0:T(8,128)S(1)}, f32[32,768]{1,0:T(8,128)S(1)}, u32[]{:S(2)}, u32[]{:S(2)}) collective-permute-start(f32[32,768]{1,0:T(8,128)S(1)} %get-tuple-element.32), channel_id=1, source_target_pairs={{0,4},{1,5},{2,6},{3,7},{4,0},{5,1},{6,2},{7,3},{8,12},{9,13},{10,... | collective-permute-start | bytes 294920 | tf_op jit(solution)/shard_map/ppermute | solution.py:256
  33.9 7.9 %collective-permute-start.18 = (f32[32,768]{1,0:T(8,128)S(1)}, f32[32,768]{1,0:T(8,128)S(1)}, u32[]{:S(2)}, u32[]{:S(2)}) collective-permute-start(f32[32,768]{1,0:T(8,128)S(1)} %get-tuple-element.33), channel_id=1, source_target_pairs={{0,20},{1,21},{2,22},{3,23},{4,16},{5,17},{6,18},{7,19},{8,28},{9,... | collective-permute-start | bytes 294920 | tf_op jit(solution)/shard_map/ppermute | solution.py:256
  36.7 6.4 %collective-permute-start.19 = (f32[32,768]{1,0:T(8,128)S(1)}, f32[32,768]{1,0:T(8,128)S(1)}, u32[]{:S(2)}, u32[]{:S(2)}) collective-permute-start(f32[32,768]{1,0:T(8,128)S(1)} %get-tuple-element.34), channel_id=1, source_target_pairs={{0,16},{16,0},{1,17},{17,1},{2,18},{18,2},{3,19},{19,3},{4,20},{20... | collective-permute-start | bytes 294920 | tf_op jit(solution)/shard_map/ppermute | solution.py:259

commit v6 on v5

--- a/solution.py
+++ b/solution.py
@@ -29,24 +29,17 @@
     return jnp.pad(values, widths)
 
 
-def prep_kernel(half, scalars, record, *refs):
-    blocks, (base, level, lines, flat, ext) = refs[:-5], refs[-5:]
-    segs = len(blocks)
-    chans, span = record.shape
-    kept = base.shape[1]
-    taps = base.shape[3] - span
-    width, long = 2 * span, span + taps
+def prep_kernel(half, chans, scalars, *refs):
+    blocks, (base, level, lines, flat) = refs[:-4], refs[-4:]
+    segs, kept, _, long = base.shape
+    span = level.shape[2]
+    taps, width = long - span, 2 * span
     start = half() * kept
 
-    rim, *others = blocks
-    for side, block in enumerate((record, rim)):
-        ext[:, side * span : (side + 1) * span] = block[...].astype(jnp.float32)
-    for seg in range(segs):
+    for seg, block in enumerate(blocks):
+        whole = block[...].astype(jnp.float32)
         for first in range(0, kept, 8):
-            if seg == 0:
-                both = ext[pl.ds(pl.multiple_of(start + first, 8), 8), :]
-            else:
-                both = others[seg - 1][...].astype(jnp.float32)[first : first + 8, :]
+            both = whole[first : first + 8, :]
             window, reach = both * both, 1
             while reach < taps:
                 window = window + rolled_left(window, reach)
@@ -89,26 +82,25 @@
     lax.fori_loop(0, kept // unroll, body, 0)
 
 
-def prepare(half, scalars, record, blocks, taps):
+def prepare(half, chans, scalars, blocks, taps):
     segs = len(blocks)
-    chans, span = record.shape
-    kept = chans // 2
+    kept, width = blocks[0].shape
+    span = width // 2
     return pl.pallas_call(
-        functools.partial(prep_kernel, half),
+        functools.partial(prep_kernel, half, chans),
         out_shape=[
             jax.ShapeDtypeStruct((segs, kept, 16, span + taps), jnp.bfloat16),
             jax.ShapeDtypeStruct((segs, kept, span), jnp.float32),
         ],
-        in_specs=[SMEM] + [VMEM] * (1 + len(blocks)),
+        in_specs=[SMEM] + [VMEM] * segs,
         out_specs=[VMEM] * 2,
         scratch_shapes=[
-            pltpu.VMEM((4, 8, span + taps), jnp.float32),
-            pltpu.VMEM((2 * span // LANES, kept * 8, LANES), jnp.float32),
-            pltpu.VMEM((chans, 2 * span), jnp.float32),
+            pltpu.VMEM((8, 8, span + taps), jnp.float32),
+            pltpu.VMEM((width // LANES, kept * 8, LANES), jnp.float32),
         ],
         compiler_params=pltpu.CompilerParams(vmem_limit_bytes=VMEM_BYTES),
         cost_estimate=pl.CostEstimate(flops=1, bytes_accessed=10**6, transcendentals=0),
-    )(scalars, record, *blocks)
+    )(scalars, *blocks)
 
 
 def corr_kernel(pieces, groups, overall, per, skip, scalars, base, level, *refs):
@@ -214,10 +206,14 @@
         banks[mask] = crossed(other if mask & shared else mine, mask)
     after = [(i, i - 1) for i in range(1, count)]
     rim = lax.ppermute(record, "tm", after)
-    given = jnp.concatenate(
-        [lax.dynamic_slice_in_dim(v, (1 - half()) * kept, kept, 0) for v in (record, rim)], axis=1
-    )
-    moved = [rim, crossed(given, shared)]
+
+    def joined(part):
+        return jnp.concatenate(
+            [lax.dynamic_slice_in_dim(v, part * kept, kept, 0) for v in (record, rim)], axis=1
+        )
+
+    given, own = joined(1 - half()), joined(half())
+    moved = [own, crossed(given, shared)]
     bit = shared // 2
     late = [mask for mask in banks if mask & (count // 2)]
     banks[bit] = crossed(mine, bit)
@@ -234,12 +230,16 @@
         places[mask] = place * per
     scalars = jnp.concatenate([shifts, live_mask, plan, jnp.asarray(places)])
 
-    base, level = prepare(half, scalars, record, moved, taps)
+    base, level = prepare(half, record.shape[0], scalars, moved, taps)
     for mask in late:
         banks[mask | bit] = crossed(banks[mask], bit)
-    *pieces, base = lax.optimization_barrier(
-        (*(banks[mask] for mask in order if mask in banks), base)
-    )
+    last = [mask | bit for mask in range(shared, count, shared)]
+    soon = [mask for mask in banks if mask not in last]
+    *held, base = lax.optimization_barrier((*(banks[mask] for mask in soon), base))
+    banks.update(zip(soon, held))
+    *held, base = lax.optimization_barrier((*(banks[mask] for mask in last), base))
+    banks.update(zip(last, held))
+    pieces = [banks[mask] for mask in order if mask in banks]
     while bit > 1:
         bit //= 2
         pieces += [crossed(piece, bit) for piece in pieces]

time: 44.1 us -> 43.1 us (0.977)
  waiting for transfers between devices: 10.6 us -> 9.12 us
  starting transfers between devices: 18.9 us -> 20.2 us
  local copies, waits for them, and re-layouts: 2.62 us -> 1.76 us
    ppermute x16, starting transfers between devices: 14.1 us -> 15.4 us  [crossed(): lax.ppermute(values, 'tm', [(i, i ^ bit) for i in range(lax.axis_size('tm...]
    unnamed x2 -> x0, local copies, waits for them, and re-layouts: 0.88 us -> none
    ppermute x1, waiting for transfers between devices: 1.29 us -> 0.49 us  [per_device(): rim = lax.ppermute(record, 'tm', after)]
    ppermute x16, waiting for transfers between devices: 3.35 us -> 2.57 us  [crossed(): lax.ppermute(values, 'tm', [(i, i ^ bit) for i in range(lax.axis_size('tm...]
where the time goes in v6:
time: 43.1 us; the launch traced here: 42.8 us
  starting transfers between devices  20.2 us (47%)
  Pallas kernels  10.2 us (24%)
  waiting for transfers between devices  9.12 us (21%)
  local copies, waits for them, and re-layouts  1.76 us (4%)
  other arithmetic  1.45 us (3%)
    ppermute x16, starting transfers between devices, crossed(): lax.ppermute(values, 'tm', [(i, i ^ bit) for i in range(lax.axis_size('tm...  15.4 us
    pallas_call x1, Pallas kernels, correlate(): pl.pallas_call(functools.partial(corr_kernel, len(banks), groups, overall...  6.8 us
    ppermute x2, waiting for transfers between devices, per_device(): total = total + lax.ppermute(stacks[groups + by], ('sta', 'tm'), pairs)  4.7 us
    pallas_call x1, Pallas kernels, prepare(): pl.pallas_call(functools.partial(prep_kernel, half, chans), out_shape=[ja...  3.38 us
    ppermute x2, starting transfers between devices, per_device(): total = total + lax.ppermute(stacks[groups + by], ('sta', 'tm'), pairs)  3.04 us
    ppermute x16, waiting for transfers between devices, crossed(): lax.ppermute(values, 'tm', [(i, i ^ bit) for i in range(lax.axis_size('tm...  2.57 us
    ppermute x1, waiting for transfers between devices, per_device(): total = total + lax.ppermute(stacks[by], 'sta', pairs)  1.36 us
    ppermute x1, starting transfers between devices, per_device(): rim = lax.ppermute(record, 'tm', after)  1.28 us
  transfers between devices with their start and end apart: 20, of which 10 were waited for; matrix products, arithmetic and copies ran while one was open for 4% of the time, Pallas kernels for 8%

profile of v6, /device:TPU:0, one launch (start us, length us, event | category | flops | bytes accessed | tf_op | source)
XLA Modules:
  0.0 42.8 jit_solution(5722260893744400485)
XLA Ops:
  0.0 1.0 %constant_dynamic-slice_fusion.4 = (bf16[4,24,512]{2,1,0:T(8,128)(2,1)S(1)}, bf16[4,24,512]{2,1,0:T(8,128)(2,1)S(1)}) fusion(bf16[4,48,512]{2,1,0:T(8,128)(2,1)} %param.7, s32[]{:T(128)S(6)} %select_n.5, s32[]{:T(128)S(6)} %select_n.4), kind=kLoop, calls=%fused_computation.7 | loop fusion | bytes 393224 | tf_op jit(solution)/shard_map/dynamic_slice | solution.py:202
  1.0 5.1 %collective-permute-start.4 = (bf16[4,24,512]{2,1,0:T(8,128)(2,1)S(1)}, bf16[4,24,512]{2,1,0:T(8,128)(2,1)S(1)}, u32[]{:S(2)}, u32[]{:S(2)}) collective-permute-start(bf16[4,24,512]{2,1,0:T(8,128)(2,1)S(1)} %get-tuple-element.38), channel_id=1, source_target_pairs={{0,12},{1,13},{2,14},{3,15},{4,8},{5,9},{6,10},{7,11},{8,4},{9,5},... | collective-permute-start | bytes 294920 | tf_op jit(solution)/shard_map/ppermute | solution.py:187
  6.1 0.0 collective-permute-start
  6.1 1.5 %collective-permute-start.6 = (bf16[4,24,512]{2,1,0:T(8,128)(2,1)S(1)}, bf16[4,24,512]{2,1,0:T(8,128)(2,1)S(1)}, u32[]{:S(2)}, u32[]{:S(2)}) collective-permute-start(bf16[4,24,512]{2,1,0:T(8,128)(2,1)S(1)} %get-tuple-element.25.refs_0_), channel_id=1, source_target_pairs={{0,2},{1,3},{2,0},{3,1},{4,6},{5,7},{6,4},{7,5},{8,10},{9,11},{10,... | collective-permute-start | bytes 294920 | tf_op jit(solution)/shard_map/ppermute | solution.py:187
  7.6 0.8 %collective-permute-start.2 = (bf16[4,24,512]{2,1,0:T(8,128)(2,1)S(1)}, bf16[4,24,512]{2,1,0:T(8,128)(2,1)S(1)}, u32[]{:S(2)}, u32[]{:S(2)}) collective-permute-start(bf16[4,24,512]{2,1,0:T(8,128)(2,1)S(1)} %get-tuple-element.25.refs_0_), channel_id=1, source_target_pairs={{0,8},{1,9},{2,10},{3,11},{4,12},{5,13},{6,14},{7,15},{8,0},{9,1},... | collective-permute-start | bytes 294920 | tf_op jit(solution)/shard_map/ppermute | solution.py:187
  8.4 1.3 %collective-permute-start.7 = (bf16[48,768]{1,0:T(8,128)(2,1)}, bf16[48,768]{1,0:T(8,128)(2,1)S(1)}, u32[]{:S(2)}, u32[]{:S(2)}) collective-permute-start(bf16[48,768]{1,0:T(8,128)(2,1)} %param.6), channel_id=1, source_target_pairs={{1,0},{2,1},{3,2},{4,3},{5,4},{6,5},{7,6},{8,7},{9,8},{10,9},{11,1... | collective-permute-start | bytes 221192 | tf_op jit(solution)/shard_map/ppermute | solution.py:208
  9.7 0.8 %constant_dynamic-slice_fusion.1 = (bf16[24,768]{1,0:T(8,128)(2,1)S(1)}, bf16[24,768]{1,0:T(8,128)(2,1)S(1)}) fusion(bf16[48,768]{1,0:T(8,128)(2,1)} %param.6, s32[]{:T(128)S(6)} %select_n.4, s32[]{:T(128)S(6)} %select_n.5), kind=kLoop, calls=%fused_computation.4 | loop fusion | bytes 147464 | tf_op jit(solution)/shard_map/dynamic_slice | solution.py:212
  10.5 0.8 %pad_add_fusion.scalars = s32[176]{0:T(256)S(1)} fusion(s32[16]{0:T(128)} %constant.21.clone, s32[64]{0:T(128)} %param.10, s32[48]{0:T(128)} %param.9, s32[48]{0:T(128)} %param.8), kind=kLoop, calls=%fused_computation.9 | loop fusion | flops 528 | bytes 1408 | tf_op jit(solution)/shard_map/concatenate | solution.py:231
  11.2 0.5 %collective-permute-done.7 = bf16[48,768]{1,0:T(8,128)(2,1)S(1)} collective-permute-done((bf16[48,768]{1,0:T(8,128)(2,1)}, bf16[48,768]{1,0:T(8,128)(2,1)S(1)}, u32[]{:S(2)}, u32[]{:S(2)}) %collective-permute-start.7) | collective-permute-done | bytes 73760 | tf_op jit(solution)/shard_map/ppermute | solution.py:208
  11.8 2.4 %collective-permute-start.8 = (bf16[24,1536]{1,0:T(8,128)(2,1)S(1)}, bf16[24,1536]{1,0:T(8,128)(2,1)S(1)}, u32[]{:S(2)}, u32[]{:S(2)}) collective-permute-start(bf16[24,1536]{1,0:T(8,128)(2,1)S(1)} %pad_maximum_fusion.1), channel_id=1, source_target_pairs={{0,4},{1,5},{2,6},{3,7},{4,0},{5,1},{6,2},{7,3},{8,12},{9,13},{10,... | collective-permute-start | bytes 221192 | tf_op jit(solution)/shard_map/ppermute | solution.py:187
  14.1 0.0 collective-permute-done.4.refs_3_
  14.1 0.4 collective-permute-start.5
  14.5 0.0 collective-permute-done.refs_1_
  14.5 1.7 %collective-permute-start.1 = (bf16[4,24,512]{2,1,0:T(8,128)(2,1)S(1)}, bf16[4,24,512]{2,1,0:T(8,128)(2,1)S(1)}, u32[]{:S(2)}, u32[]{:S(2)}) collective-permute-start(bf16[4,24,512]{2,1,0:T(8,128)(2,1)S(1)} %collective-permute-done.refs_1_), channel_id=1, source_target_pairs={{0,2},{1,3},{2,0},{3,1},{4,6},{5,7},{6,4},{7,5},{8,10},{9,11},{10,... | collective-permute-start | bytes 294920 | tf_op jit(solution)/shard_map/ppermute | solution.py:187
  16.3 0.0 collective-permute-done.2.refs_2_
  16.3 0.4 collective-permute-start.3
  16.6 0.3 collective-permute-done.8.refs_1_
  17.0 3.4 %shard_map.64 = (bf16[2,24,16,1280]{3,2,1,0:T(8,128)(2,1)S(1)}, f32[2,24,768]{2,1,0:T(8,128)S(1)}) custom-call(s32[176]{0:T(256)S(1)} %pad_add_fusion.scalars, bf16[24,1536]{1,0:T(8,128)(2,1)S(1)} %pad_maximum_fusion.refs_0_, bf16[24,1536]{1,0:T(8,128)(2,1)S(1)} %collective-permute-done.8.refs_1_), custom_call_target="tpu_custom_call" | custom-call | flops 1 | bytes 1000000 | tf_op jit(solution)/shard_map/pallas_call | solution.py:89
  20.4 0.0 collective-permute-done.6.refs_4_
  20.4 1.5 %collective-permute-start.9 = (bf16[4,24,512]{2,1,0:T(8,128)(2,1)S(1)}, bf16[4,24,512]{2,1,0:T(8,128)(2,1)S(1)}, u32[]{:S(2)}, u32[]{:S(2)}) collective-permute-start(bf16[4,24,512]{2,1,0:T(8,128)(2,1)S(1)} %get-tuple-element.25.refs_0_), channel_id=1, source_target_pairs={{0,1},{1,0},{2,3},{3,2},{4,5},{5,4},{6,7},{7,6},{8,9},{9,8},{10,11... | collective-permute-start | bytes 294920 | tf_op jit(solution)/shard_map/ppermute | solution.py:187
  21.9 0.1 collective-permute-start.10
  22.0 0.0 collective-permute-done.5.refs_7_
  22.0 0.4 %collective-permute-start.11 = (bf16[4,24,512]{2,1,0:T(8,128)(2,1)S(1)}, bf16[4,24,512]{2,1,0:T(8,128)(2,1)S(1)}, u32[]{:S(2)}, u32[]{:S(2)}) collective-permute-start(bf16[4,24,512]{2,1,0:T(8,128)(2,1)S(1)} %collective-permute-done.2.refs_2_), channel_id=1, source_target_pairs={{0,1},{1,0},{2,3},{3,2},{4,5},{5,4},{6,7},{7,6},{8,9},{9,8},{10,11... | collective-permute-start | bytes 294920 | tf_op jit(solution)/shard_map/ppermute | solution.py:187
  22.4 0.0 collective-permute-done.1.refs_5_
  22.4 0.1 collective-permute-start.12
  22.5 1.3 %collective-permute-done.3.refs_6_ = bf16[4,24,512]{2,1,0:T(8,128)(2,1)S(1)} collective-permute-done((bf16[4,24,512]{2,1,0:T(8,128)(2,1)S(1)}, bf16[4,24,512]{2,1,0:T(8,128)(2,1)S(1)}, u32[]{:S(2)}, u32[]{:S(2)}) %collective-permute-start.3) | collective-permute-done | bytes 98336 | tf_op jit(solution)/shard_map/ppermute | solution.py:187
  23.7 0.1 collective-permute-start.13
  23.9 0.0 collective-permute-done.9.refs_8_
  23.9 0.4 collective-permute-start.14
  24.3 0.0 collective-permute-done.10.refs_9_
  24.3 0.1 collective-permute-start.15
  24.4 0.0 collective-permute-done.11.refs_10_
  24.4 0.4 collective-permute-start.16
  24.8 0.0 collective-permute-done.12.refs_11_
  24.8 0.3 collective-permute-done.13.refs_12_
  25.0 0.2 collective-permute-done.14.refs_13_
  25.2 0.4 collective-permute-done.15.refs_14_
  25.6 0.2 collective-permute-done.16.refs_15_
  25.7 6.8 %shard_map.65 = (f32[32,768]{1,0:T(8,128)S(1)}, f32[32,768]{1,0:T(8,128)S(1)}, f32[32,768]{1,0:T(8,128)S(1)}, f32[32,768]{1,0:T(8,128)S(1)}) custom-call(s32[176]{0:T(256)S(1)} %pad_add_fusion.scalars, bf16[2,24,16,1280]{3,2,1,0:T(8,128)(2,1)S(1)} %get-tuple-element.23.base, f32[2,24,768]{2,1,0:T(8,128)S(1)} %get-tuple-element.24.level, ...), custom_call_target="tpu_custom_call" | custom-call | flops 2415919104 | bytes 10000000 | tf_op jit(solution)/shard_map/pallas_call | solution.py:170
  32.5 0.1 collective-permute-start.17
  32.6 2.9 %collective-permute-start.18 = (f32[32,768]{1,0:T(8,128)S(1)}, f32[32,768]{1,0:T(8,128)S(1)}, u32[]{:S(2)}, u32[]{:S(2)}) collective-permute-start(f32[32,768]{1,0:T(8,128)S(1)} %get-tuple-element.35), channel_id=1, source_target_pairs={{0,20},{1,21},{2,22},{3,23},{4,16},{5,17},{6,18},{7,19},{8,28},{9,... | collective-permute-start | bytes 294920 | tf_op jit(solution)/shard_map/ppermute | solution.py:256
  35.6 0.5 %collective-permute-start.19 = (f32[32,768]{1,0:T(8,128)S(1)}, f32[32,768]{1,0:T(8,128)S(1)}, u32[]{:S(2)}, u32[]{:S(2)}) collective-permute-start(f32[32,768]{1,0:T(8,128)S(1)} %get-tuple-element.36), channel_id=1, source_target_pairs={{0,16},{16,0},{1,17},{17,1},{2,18},{18,2},{3,19},{19,3},{4,20},{20... | collective-permute-start | bytes 294920 | tf_op jit(solution)/shard_map/ppermute | solution.py:259
  36.1 2.1 %collective-permute-done.17 = f32[32,768]{1,0:T(8,128)S(1)} collective-permute-done((f32[32,768]{1,0:T(8,128)S(1)}, f32[32,768]{1,0:T(8,128)S(1)}, u32[]{:S(2)}, u32[]{:S(2)}) %collective-permute-start.17) | collective-permute-done | bytes 98336 | tf_op jit(solution)/shard_map/ppermute | solution.py:256
  38.2 2.6 %collective-permute-done.18 = f32[32,768]{1,0:T(8,128)S(1)} collective-permute-done((f32[32,768]{1,0:T(8,128)S(1)}, f32[32,768]{1,0:T(8,128)S(1)}, u32[]{:S(2)}, u32[]{:S(2)}) %collective-permute-start.18) | collective-permute-done | bytes 98336 | tf_op jit(solution)/shard_map/ppermute | solution.py:256
  40.8 1.4 %collective-permute-done.19 = f32[32,768]{1,0:T(8,128)S(1)} collective-permute-done((f32[32,768]{1,0:T(8,128)S(1)}, f32[32,768]{1,0:T(8,128)S(1)}, u32[]{:S(2)}, u32[]{:S(2)}) %collective-permute-start.19) | collective-permute-done | bytes 98336 | tf_op jit(solution)/shard_map/ppermute | solution.py:259
  42.2 0.7 %add_add_fusion = f32[32,768]{1,0:T(8,128)} fusion(f32[32,768]{1,0:T(8,128)S(1)} %collective-permute-done.19, f32[32,768]{1,0:T(8,128)S(1)} %collective-permute-done.18, f32[32,768]{1,0:T(8,128)S(1)} %get-tuple-element.33, f32[32,768]{1,0:T(8,128)S(1)} %collective-permute-done.17), kind=kLoop, calls=%fused_computation | loop fusion | flops 73728 | bytes 491520 | tf_op jit(solution)/shard_map/add | solution.py:259
  (3 shorter events, 0.0 us)
Async XLA Ops:
  1.0 13.2 %collective-permute-start.4 = (bf16[4,24,512]{2,1,0:T(8,128)(2,1)S(1)}, bf16[4,24,512]{2,1,0:T(8,128)(2,1)S(1)}, u32[]{:S(2)}, u32[]{:S(2)}) collective-permute-start(bf16[4,24,512]{2,1,0:T(8,128)(2,1)S(1)} %get-tuple-element.38), channel_id=1, source_target_pairs={{0,12},{1,13},{2,14},{3,15},{4,8},{5,9},{6,10},{7,11},{8,4},{9,5},... | collective-permute-start | bytes 294920 | tf_op jit(solution)/shard_map/ppermute | solution.py:187
  6.1 8.5 %collective-permute-start = (bf16[4,24,512]{2,1,0:T(8,128)(2,1)S(1)}, bf16[4,24,512]{2,1,0:T(8,128)(2,1)S(1)}, u32[]{:S(2)}, u32[]{:S(2)}) collective-permute-start(bf16[4,24,512]{2,1,0:T(8,128)(2,1)S(1)} %get-tuple-element.38), channel_id=1, source_target_pairs={{0,4},{1,5},{2,6},{3,7},{4,0},{5,1},{6,2},{7,3},{8,12},{9,13},{10,... | collective-permute-start | bytes 294920 | tf_op jit(solution)/shard_map/ppermute | solution.py:187
  6.1 14.3 %collective-permute-start.6 = (bf16[4,24,512]{2,1,0:T(8,128)(2,1)S(1)}, bf16[4,24,512]{2,1,0:T(8,128)(2,1)S(1)}, u32[]{:S(2)}, u32[]{:S(2)}) collective-permute-start(bf16[4,24,512]{2,1,0:T(8,128)(2,1)S(1)} %get-tuple-element.25.refs_0_), channel_id=1, source_target_pairs={{0,2},{1,3},{2,0},{3,1},{4,6},{5,7},{6,4},{7,5},{8,10},{9,11},{10,... | collective-permute-start | bytes 294920 | tf_op jit(solution)/shard_map/ppermute | solution.py:187
  7.6 8.7 %collective-permute-start.2 = (bf16[4,24,512]{2,1,0:T(8,128)(2,1)S(1)}, bf16[4,24,512]{2,1,0:T(8,128)(2,1)S(1)}, u32[]{:S(2)}, u32[]{:S(2)}) collective-permute-start(bf16[4,24,512]{2,1,0:T(8,128)(2,1)S(1)} %get-tuple-element.25.refs_0_), channel_id=1, source_target_pairs={{0,8},{1,9},{2,10},{3,11},{4,12},{5,13},{6,14},{7,15},{8,0},{9,1},... | collective-permute-start | bytes 294920 | tf_op jit(solution)/shard_map/ppermute | solution.py:187
  8.4 3.4 %collective-permute-start.7 = (bf16[48,768]{1,0:T(8,128)(2,1)}, bf16[48,768]{1,0:T(8,128)(2,1)S(1)}, u32[]{:S(2)}, u32[]{:S(2)}) collective-permute-start(bf16[48,768]{1,0:T(8,128)(2,1)} %param.6), channel_id=1, source_target_pairs={{1,0},{2,1},{3,2},{4,3},{5,4},{6,5},{7,6},{8,7},{9,8},{10,9},{11,1... | collective-permute-start | bytes 221192 | tf_op jit(solution)/shard_map/ppermute | solution.py:208
  11.8 5.2 %collective-permute-start.8 = (bf16[24,1536]{1,0:T(8,128)(2,1)S(1)}, bf16[24,1536]{1,0:T(8,128)(2,1)S(1)}, u32[]{:S(2)}, u32[]{:S(2)}) collective-permute-start(bf16[24,1536]{1,0:T(8,128)(2,1)S(1)} %pad_maximum_fusion.1), channel_id=1, source_target_pairs={{0,4},{1,5},{2,6},{3,7},{4,0},{5,1},{6,2},{7,3},{8,12},{9,13},{10,... | collective-permute-start | bytes 221192 | tf_op jit(solution)/shard_map/ppermute | solution.py:187
  14.1 7.8 %collective-permute-start.5 = (bf16[4,24,512]{2,1,0:T(8,128)(2,1)S(1)}, bf16[4,24,512]{2,1,0:T(8,128)(2,1)S(1)}, u32[]{:S(2)}, u32[]{:S(2)}) collective-permute-start(bf16[4,24,512]{2,1,0:T(8,128)(2,1)S(1)} %collective-permute-done.4.refs_3_), channel_id=1, source_target_pairs={{0,2},{1,3},{2,0},{3,1},{4,6},{5,7},{6,4},{7,5},{8,10},{9,11},{10,... | collective-permute-start | bytes 294920 | tf_op jit(solution)/shard_map/ppermute | solution.py:187
  14.5 7.9 %collective-permute-start.1 = (bf16[4,24,512]{2,1,0:T(8,128)(2,1)S(1)}, bf16[4,24,512]{2,1,0:T(8,128)(2,1)S(1)}, u32[]{:S(2)}, u32[]{:S(2)}) collective-permute-start(bf16[4,24,512]{2,1,0:T(8,128)(2,1)S(1)} %collective-permute-done.refs_1_), channel_id=1, source_target_pairs={{0,2},{1,3},{2,0},{3,1},{4,6},{5,7},{6,4},{7,5},{8,10},{9,11},{10,... | collective-permute-start | bytes 294920 | tf_op jit(solution)/shard_map/ppermute | solution.py:187
  16.3 7.5 %collective-permute-start.3 = (bf16[4,24,512]{2,1,0:T(8,128)(2,1)S(1)}, bf16[4,24,512]{2,1,0:T(8,128)(2,1)S(1)}, u32[]{:S(2)}, u32[]{:S(2)}) collective-permute-start(bf16[4,24,512]{2,1,0:T(8,128)(2,1)S(1)} %collective-permute-done.2.refs_2_), channel_id=1, source_target_pairs={{0,2},{1,3},{2,0},{3,1},{4,6},{5,7},{6,4},{7,5},{8,10},{9,11},{10,... | collective-permute-start | bytes 294920 | tf_op jit(solution)/shard_map/ppermute | solution.py:187
  20.4 3.5 %collective-permute-start.9 = (bf16[4,24,512]{2,1,0:T(8,128)(2,1)S(1)}, bf16[4,24,512]{2,1,0:T(8,128)(2,1)S(1)}, u32[]{:S(2)}, u32[]{:S(2)}) collective-permute-start(bf16[4,24,512]{2,1,0:T(8,128)(2,1)S(1)} %get-tuple-element.25.refs_0_), channel_id=1, source_target_pairs={{0,1},{1,0},{2,3},{3,2},{4,5},{5,4},{6,7},{7,6},{8,9},{9,8},{10,11... | collective-permute-start | bytes 294920 | tf_op jit(solution)/shard_map/ppermute | solution.py:187
  21.9 2.4 %collective-permute-start.10 = (bf16[4,24,512]{2,1,0:T(8,128)(2,1)S(1)}, bf16[4,24,512]{2,1,0:T(8,128)(2,1)S(1)}, u32[]{:S(2)}, u32[]{:S(2)}) collective-permute-start(bf16[4,24,512]{2,1,0:T(8,128)(2,1)S(1)} %collective-permute-done.refs_1_), channel_id=1, source_target_pairs={{0,1},{1,0},{2,3},{3,2},{4,5},{5,4},{6,7},{7,6},{8,9},{9,8},{10,11... | collective-permute-start | bytes 294920 | tf_op jit(solution)/shard_map/ppermute | solution.py:187
  22.0 2.4 %collective-permute-start.11 = (bf16[4,24,512]{2,1,0:T(8,128)(2,1)S(1)}, bf16[4,24,512]{2,1,0:T(8,128)(2,1)S(1)}, u32[]{:S(2)}, u32[]{:S(2)}) collective-permute-start(bf16[4,24,512]{2,1,0:T(8,128)(2,1)S(1)} %collective-permute-done.2.refs_2_), channel_id=1, source_target_pairs={{0,1},{1,0},{2,3},{3,2},{4,5},{5,4},{6,7},{7,6},{8,9},{9,8},{10,11... | collective-permute-start | bytes 294920 | tf_op jit(solution)/shard_map/ppermute | solution.py:187
  22.4 2.4 %collective-permute-start.12 = (bf16[4,24,512]{2,1,0:T(8,128)(2,1)S(1)}, bf16[4,24,512]{2,1,0:T(8,128)(2,1)S(1)}, u32[]{:S(2)}, u32[]{:S(2)}) collective-permute-start(bf16[4,24,512]{2,1,0:T(8,128)(2,1)S(1)} %collective-permute-done.4.refs_3_), channel_id=1, source_target_pairs={{0,1},{1,0},{2,3},{3,2},{4,5},{5,4},{6,7},{7,6},{8,9},{9,8},{10,11... | collective-permute-start | bytes 294920 | tf_op jit(solution)/shard_map/ppermute | solution.py:187
  23.7 1.3 %collective-permute-start.13 = (bf16[4,24,512]{2,1,0:T(8,128)(2,1)S(1)}, bf16[4,24,512]{2,1,0:T(8,128)(2,1)S(1)}, u32[]{:S(2)}, u32[]{:S(2)}) collective-permute-start(bf16[4,24,512]{2,1,0:T(8,128)(2,1)S(1)} %collective-permute-done.6.refs_4_), channel_id=1, source_target_pairs={{0,1},{1,0},{2,3},{3,2},{4,5},{5,4},{6,7},{7,6},{8,9},{9,8},{10,11... | collective-permute-start | bytes 294920 | tf_op jit(solution)/shard_map/ppermute | solution.py:187
  23.9 1.3 %collective-permute-start.14 = (bf16[4,24,512]{2,1,0:T(8,128)(2,1)S(1)}, bf16[4,24,512]{2,1,0:T(8,128)(2,1)S(1)}, u32[]{:S(2)}, u32[]{:S(2)}) collective-permute-start(bf16[4,24,512]{2,1,0:T(8,128)(2,1)S(1)} %collective-permute-done.1.refs_5_), channel_id=1, source_target_pairs={{0,1},{1,0},{2,3},{3,2},{4,5},{5,4},{6,7},{7,6},{8,9},{9,8},{10,11... | collective-permute-start | bytes 294920 | tf_op jit(solution)/shard_map/ppermute | solution.py:187
  24.3 1.3 %collective-permute-start.15 = (bf16[4,24,512]{2,1,0:T(8,128)(2,1)S(1)}, bf16[4,24,512]{2,1,0:T(8,128)(2,1)S(1)}, u32[]{:S(2)}, u32[]{:S(2)}) collective-permute-start(bf16[4,24,512]{2,1,0:T(8,128)(2,1)S(1)} %collective-permute-done.3.refs_6_), channel_id=1, source_target_pairs={{0,1},{1,0},{2,3},{3,2},{4,5},{5,4},{6,7},{7,6},{8,9},{9,8},{10,11... | collective-permute-start | bytes 294920 | tf_op jit(solution)/shard_map/ppermute | solution.py:187
  24.4 1.3 %collective-permute-start.16 = (bf16[4,24,512]{2,1,0:T(8,128)(2,1)S(1)}, bf16[4,24,512]{2,1,0:T(8,128)(2,1)S(1)}, u32[]{:S(2)}, u32[]{:S(2)}) collective-permute-start(bf16[4,24,512]{2,1,0:T(8,128)(2,1)S(1)} %collective-permute-done.5.refs_7_), channel_id=1, source_target_pairs={{0,1},{1,0},{2,3},{3,2},{4,5},{5,4},{6,7},{7,6},{8,9},{9,8},{10,11... | collective-permute-start | bytes 294920 | tf_op jit(solution)/shard_map/ppermute | solution.py:187
  32.5 5.7 %collective-permute-start.17 = (f32[32,768]{1,0:T(8,128)S(1)}, f32[32,768]{1,0:T(8,128)S(1)}, u32[]{:S(2)}, u32[]{:S(2)}) collective-permute-start(f32[32,768]{1,0:T(8,128)S(1)} %get-tuple-element.34), channel_id=1, source_target_pairs={{0,4},{1,5},{2,6},{3,7},{4,0},{5,1},{6,2},{7,3},{8,12},{9,13},{10,... | collective-permute-start | bytes 294920 | tf_op jit(solution)/shard_map/ppermute | solution.py:256
  32.6 8.2 %collective-permute-start.18 = (f32[32,768]{1,0:T(8,128)S(1)}, f32[32,768]{1,0:T(8,128)S(1)}, u32[]{:S(2)}, u32[]{:S(2)}) collective-permute-start(f32[32,768]{1,0:T(8,128)S(1)} %get-tuple-element.35), channel_id=1, source_target_pairs={{0,20},{1,21},{2,22},{3,23},{4,16},{5,17},{6,18},{7,19},{8,28},{9,... | collective-permute-start | bytes 294920 | tf_op jit(solution)/shard_map/ppermute | solution.py:256
  35.6 6.6 %collective-permute-start.19 = (f32[32,768]{1,0:T(8,128)S(1)}, f32[32,768]{1,0:T(8,128)S(1)}, u32[]{:S(2)}, u32[]{:S(2)}) collective-permute-start(f32[32,768]{1,0:T(8,128)S(1)} %get-tuple-element.36), channel_id=1, source_target_pairs={{0,16},{16,0},{1,17},{17,1},{2,18},{18,2},{3,19},{19,3},{4,20},{20... | collective-permute-start | bytes 294920 | tf_op jit(solution)/shard_map/ppermute | solution.py:259

commit v7 on v6

--- a/solution.py
+++ b/solution.py
@@ -96,7 +96,7 @@
         out_specs=[VMEM] * 2,
         scratch_shapes=[
             pltpu.VMEM((8, 8, span + taps), jnp.float32),
-            pltpu.VMEM((width // LANES, kept * 8, LANES), jnp.float32),
+            pltpu.VMEM((width // LANES, (kept + 1) * 8, LANES), jnp.float32),
         ],
         compiler_params=pltpu.CompilerParams(vmem_limit_bytes=VMEM_BYTES),
         cost_estimate=pl.CostEstimate(flops=1, bytes_accessed=10**6, transcendentals=0),
@@ -174,7 +174,7 @@
         out_specs=[VMEM] * count,
         scratch_shapes=[
             pltpu.VMEM((segs, tmpl, span), jnp.float32),
-            pltpu.VMEM((taps // LANES, tmpl * chans, LANES), jnp.float32),
+            pltpu.VMEM((taps // LANES, (tmpl + 1) * chans, LANES), jnp.float32),
         ],
         compiler_params=pltpu.CompilerParams(vmem_limit_bytes=VMEM_BYTES),
         cost_estimate=pl.CostEstimate(
@@ -246,17 +246,21 @@
 
     skip = shifts.shape[0] + live_mask.shape[0]
     stacks = correlate(per, skip, scalars, base, level, pieces, groups, overall)
-    total = stacks[0]
+    found = []
+    for by in range(groups):
+        if by:
+            pairs = [(i, (i + by) % groups) for i in range(groups)]
+            found.append(lax.ppermute(stacks[by], "sta", pairs))
     for by in range(groups):
         pairs = [
             (i * count + j, (i + by) % groups * count + (j ^ shared))
             for i in range(groups)
             for j in range(count)
         ]
-        total = total + lax.ppermute(stacks[groups + by], ("sta", "tm"), pairs)
-        if by:
-            pairs = [(i, (i + by) % groups) for i in range(groups)]
-            total = total + lax.ppermute(stacks[by], "sta", pairs)
+        found.append(lax.ppermute(stacks[groups + by], ("sta", "tm"), pairs))
+    total = stacks[0]
+    for part in found:
+        total = total + part
     return total
 
 

time: 43.1 us -> 41.8 us (0.970)
  waiting for transfers between devices: 9.12 us -> 7.9 us
    ppermute x3, waiting for transfers between devices: 6.06 us -> 4.83 us  [the longest x2 3.29 us: per_device(): found.append(lax.ppermute(stacks[groups + by], ('sta', 'tm'), pairs))]
where the time goes in v7:
time: 41.8 us; the launch traced here: 41.6 us
  starting transfers between devices  20.2 us (48%)
  Pallas kernels  10.2 us (24%)
  waiting for transfers between devices  7.9 us (19%)
  local copies, waits for them, and re-layouts  1.76 us (4%)
  other arithmetic  1.45 us (3%)
    ppermute x16, starting transfers between devices, crossed(): lax.ppermute(values, 'tm', [(i, i ^ bit) for i in range(lax.axis_size('tm...  15.4 us
    pallas_call x1, Pallas kernels, correlate(): pl.pallas_call(functools.partial(corr_kernel, len(banks), groups, overall...  6.82 us
    pallas_call x1, Pallas kernels, prepare(): pl.pallas_call(functools.partial(prep_kernel, half, chans), out_shape=[ja...  3.38 us
    ppermute x2, waiting for transfers between devices, per_device(): found.append(lax.ppermute(stacks[groups + by], ('sta', 'tm'), pairs))  3.29 us
    ppermute x16, waiting for transfers between devices, crossed(): lax.ppermute(values, 'tm', [(i, i ^ bit) for i in range(lax.axis_size('tm...  2.58 us
    ppermute x2, starting transfers between devices, per_device(): found.append(lax.ppermute(stacks[groups + by], ('sta', 'tm'), pairs))  2.01 us
    ppermute x1, waiting for transfers between devices, per_device(): found.append(lax.ppermute(stacks[by], 'sta', pairs))  1.54 us
    ppermute x1, starting transfers between devices, per_device(): found.append(lax.ppermute(stacks[by], 'sta', pairs))  1.54 us
  transfers between devices with their start and end apart: 20, of which 10 were waited for; matrix products, arithmetic and copies ran while one was open for 4% of the time, Pallas kernels for 8%

profile of v7, /device:TPU:0, one launch (start us, length us, event | category | flops | bytes accessed | tf_op | source)
XLA Modules:
  0.0 41.6 jit_solution(7758026019584486426)
XLA Ops:
  0.0 1.0 %constant_dynamic-slice_fusion.4 = (bf16[4,24,512]{2,1,0:T(8,128)(2,1)S(1)}, bf16[4,24,512]{2,1,0:T(8,128)(2,1)S(1)}) fusion(bf16[4,48,512]{2,1,0:T(8,128)(2,1)} %param.7, s32[]{:T(128)S(6)} %select_n.5, s32[]{:T(128)S(6)} %select_n.4), kind=kLoop, calls=%fused_computation.7 | loop fusion | bytes 393224 | tf_op jit(solution)/shard_map/dynamic_slice | solution.py:202
  1.0 5.1 %collective-permute-start.4 = (bf16[4,24,512]{2,1,0:T(8,128)(2,1)S(1)}, bf16[4,24,512]{2,1,0:T(8,128)(2,1)S(1)}, u32[]{:S(2)}, u32[]{:S(2)}) collective-permute-start(bf16[4,24,512]{2,1,0:T(8,128)(2,1)S(1)} %get-tuple-element.38), channel_id=1, source_target_pairs={{0,12},{1,13},{2,14},{3,15},{4,8},{5,9},{6,10},{7,11},{8,4},{9,5},... | collective-permute-start | bytes 294920 | tf_op jit(solution)/shard_map/ppermute | solution.py:187
  6.1 0.0 collective-permute-start
  6.1 1.5 %collective-permute-start.6 = (bf16[4,24,512]{2,1,0:T(8,128)(2,1)S(1)}, bf16[4,24,512]{2,1,0:T(8,128)(2,1)S(1)}, u32[]{:S(2)}, u32[]{:S(2)}) collective-permute-start(bf16[4,24,512]{2,1,0:T(8,128)(2,1)S(1)} %get-tuple-element.25.refs_0_), channel_id=1, source_target_pairs={{0,2},{1,3},{2,0},{3,1},{4,6},{5,7},{6,4},{7,5},{8,10},{9,11},{10,... | collective-permute-start | bytes 294920 | tf_op jit(solution)/shard_map/ppermute | solution.py:187
  7.6 0.8 %collective-permute-start.2 = (bf16[4,24,512]{2,1,0:T(8,128)(2,1)S(1)}, bf16[4,24,512]{2,1,0:T(8,128)(2,1)S(1)}, u32[]{:S(2)}, u32[]{:S(2)}) collective-permute-start(bf16[4,24,512]{2,1,0:T(8,128)(2,1)S(1)} %get-tuple-element.25.refs_0_), channel_id=1, source_target_pairs={{0,8},{1,9},{2,10},{3,11},{4,12},{5,13},{6,14},{7,15},{8,0},{9,1},... | collective-permute-start | bytes 294920 | tf_op jit(solution)/shard_map/ppermute | solution.py:187
  8.4 1.3 %collective-permute-start.7 = (bf16[48,768]{1,0:T(8,128)(2,1)}, bf16[48,768]{1,0:T(8,128)(2,1)S(1)}, u32[]{:S(2)}, u32[]{:S(2)}) collective-permute-start(bf16[48,768]{1,0:T(8,128)(2,1)} %param.6), channel_id=1, source_target_pairs={{1,0},{2,1},{3,2},{4,3},{5,4},{6,5},{7,6},{8,7},{9,8},{10,9},{11,1... | collective-permute-start | bytes 221192 | tf_op jit(solution)/shard_map/ppermute | solution.py:208
  9.7 0.8 %constant_dynamic-slice_fusion.1 = (bf16[24,768]{1,0:T(8,128)(2,1)S(1)}, bf16[24,768]{1,0:T(8,128)(2,1)S(1)}) fusion(bf16[48,768]{1,0:T(8,128)(2,1)} %param.6, s32[]{:T(128)S(6)} %select_n.4, s32[]{:T(128)S(6)} %select_n.5), kind=kLoop, calls=%fused_computation.4 | loop fusion | bytes 147464 | tf_op jit(solution)/shard_map/dynamic_slice | solution.py:212
  10.5 0.8 %pad_add_fusion.scalars = s32[176]{0:T(256)S(1)} fusion(s32[16]{0:T(128)} %constant.21.clone, s32[64]{0:T(128)} %param.10, s32[48]{0:T(128)} %param.9, s32[48]{0:T(128)} %param.8), kind=kLoop, calls=%fused_computation.9 | loop fusion | flops 528 | bytes 1408 | tf_op jit(solution)/shard_map/concatenate | solution.py:231
  11.2 0.5 %collective-permute-done.7 = bf16[48,768]{1,0:T(8,128)(2,1)S(1)} collective-permute-done((bf16[48,768]{1,0:T(8,128)(2,1)}, bf16[48,768]{1,0:T(8,128)(2,1)S(1)}, u32[]{:S(2)}, u32[]{:S(2)}) %collective-permute-start.7) | collective-permute-done | bytes 73760 | tf_op jit(solution)/shard_map/ppermute | solution.py:208
  11.8 2.4 %collective-permute-start.8 = (bf16[24,1536]{1,0:T(8,128)(2,1)S(1)}, bf16[24,1536]{1,0:T(8,128)(2,1)S(1)}, u32[]{:S(2)}, u32[]{:S(2)}) collective-permute-start(bf16[24,1536]{1,0:T(8,128)(2,1)S(1)} %pad_maximum_fusion.1), channel_id=1, source_target_pairs={{0,4},{1,5},{2,6},{3,7},{4,0},{5,1},{6,2},{7,3},{8,12},{9,13},{10,... | collective-permute-start | bytes 221192 | tf_op jit(solution)/shard_map/ppermute | solution.py:187
  14.1 0.0 collective-permute-done.4.refs_3_
  14.1 0.4 collective-permute-start.5
  14.5 0.0 collective-permute-done.refs_1_
  14.5 1.7 %collective-permute-start.1 = (bf16[4,24,512]{2,1,0:T(8,128)(2,1)S(1)}, bf16[4,24,512]{2,1,0:T(8,128)(2,1)S(1)}, u32[]{:S(2)}, u32[]{:S(2)}) collective-permute-start(bf16[4,24,512]{2,1,0:T(8,128)(2,1)S(1)} %collective-permute-done.refs_1_), channel_id=1, source_target_pairs={{0,2},{1,3},{2,0},{3,1},{4,6},{5,7},{6,4},{7,5},{8,10},{9,11},{10,... | collective-permute-start | bytes 294920 | tf_op jit(solution)/shard_map/ppermute | solution.py:187
  16.3 0.0 collective-permute-done.2.refs_2_
  16.3 0.4 collective-permute-start.3
  16.6 0.3 collective-permute-done.8.refs_1_
  17.0 3.4 %shard_map.64 = (bf16[2,24,16,1280]{3,2,1,0:T(8,128)(2,1)S(1)}, f32[2,24,768]{2,1,0:T(8,128)S(1)}) custom-call(s32[176]{0:T(256)S(1)} %pad_add_fusion.scalars, bf16[24,1536]{1,0:T(8,128)(2,1)S(1)} %pad_maximum_fusion.refs_0_, bf16[24,1536]{1,0:T(8,128)(2,1)S(1)} %collective-permute-done.8.refs_1_), custom_call_target="tpu_custom_call" | custom-call | flops 1 | bytes 1000000 | tf_op jit(solution)/shard_map/pallas_call | solution.py:89
  20.3 0.0 collective-permute-done.6.refs_4_
  20.4 1.5 %collective-permute-start.9 = (bf16[4,24,512]{2,1,0:T(8,128)(2,1)S(1)}, bf16[4,24,512]{2,1,0:T(8,128)(2,1)S(1)}, u32[]{:S(2)}, u32[]{:S(2)}) collective-permute-start(bf16[4,24,512]{2,1,0:T(8,128)(2,1)S(1)} %get-tuple-element.25.refs_0_), channel_id=1, source_target_pairs={{0,1},{1,0},{2,3},{3,2},{4,5},{5,4},{6,7},{7,6},{8,9},{9,8},{10,11... | collective-permute-start | bytes 294920 | tf_op jit(solution)/shard_map/ppermute | solution.py:187
  21.9 0.1 collective-permute-start.10
  22.0 0.0 collective-permute-done.5.refs_7_
  22.0 0.4 %collective-permute-start.11 = (bf16[4,24,512]{2,1,0:T(8,128)(2,1)S(1)}, bf16[4,24,512]{2,1,0:T(8,128)(2,1)S(1)}, u32[]{:S(2)}, u32[]{:S(2)}) collective-permute-start(bf16[4,24,512]{2,1,0:T(8,128)(2,1)S(1)} %collective-permute-done.2.refs_2_), channel_id=1, source_target_pairs={{0,1},{1,0},{2,3},{3,2},{4,5},{5,4},{6,7},{7,6},{8,9},{9,8},{10,11... | collective-permute-start | bytes 294920 | tf_op jit(solution)/shard_map/ppermute | solution.py:187
  22.4 0.0 collective-permute-done.1.refs_5_
  22.4 0.1 collective-permute-start.12
  22.5 1.3 %collective-permute-done.3.refs_6_ = bf16[4,24,512]{2,1,0:T(8,128)(2,1)S(1)} collective-permute-done((bf16[4,24,512]{2,1,0:T(8,128)(2,1)S(1)}, bf16[4,24,512]{2,1,0:T(8,128)(2,1)S(1)}, u32[]{:S(2)}, u32[]{:S(2)}) %collective-permute-start.3) | collective-permute-done | bytes 98336 | tf_op jit(solution)/shard_map/ppermute | solution.py:187
  23.7 0.1 collective-permute-start.13
  23.9 0.0 collective-permute-done.9.refs_8_
  23.9 0.4 collective-permute-start.14
  24.3 0.0 collective-permute-done.10.refs_9_
  24.3 0.1 collective-permute-start.15
  24.4 0.0 collective-permute-done.11.refs_10_
  24.4 0.4 collective-permute-start.16
  24.8 0.0 collective-permute-done.12.refs_11_
  24.8 0.3 collective-permute-done.13.refs_12_
  25.0 0.2 collective-permute-done.14.refs_13_
  25.2 0.4 collective-permute-done.15.refs_14_
  25.6 0.2 collective-permute-done.16.refs_15_
  25.7 6.8 %shard_map.65 = (f32[32,768]{1,0:T(8,128)S(1)}, f32[32,768]{1,0:T(8,128)S(1)}, f32[32,768]{1,0:T(8,128)S(1)}, f32[32,768]{1,0:T(8,128)S(1)}) custom-call(s32[176]{0:T(256)S(1)} %pad_add_fusion.scalars, bf16[2,24,16,1280]{3,2,1,0:T(8,128)(2,1)S(1)} %get-tuple-element.23.base, f32[2,24,768]{2,1,0:T(8,128)S(1)} %get-tuple-element.24.level, ...), custom_call_target="tpu_custom_call" | custom-call | flops 2415919104 | bytes 10000000 | tf_op jit(solution)/shard_map/pallas_call | solution.py:170
  32.6 1.5 %collective-permute-start.17 = (f32[32,768]{1,0:T(8,128)S(1)}, f32[32,768]{1,0:T(8,128)S(1)}, u32[]{:S(2)}, u32[]{:S(2)}) collective-permute-start(f32[32,768]{1,0:T(8,128)S(1)} %get-tuple-element.34), channel_id=1, source_target_pairs={{0,16},{16,0},{1,17},{17,1},{2,18},{18,2},{3,19},{19,3},{4,20},{20... | collective-permute-start | bytes 294920 | tf_op jit(solution)/shard_map/ppermute | solution.py:253
  34.1 0.0 collective-permute-start.18
  34.1 2.0 %collective-permute-start.19 = (f32[32,768]{1,0:T(8,128)S(1)}, f32[32,768]{1,0:T(8,128)S(1)}, u32[]{:S(2)}, u32[]{:S(2)}) collective-permute-start(f32[32,768]{1,0:T(8,128)S(1)} %get-tuple-element.36), channel_id=1, source_target_pairs={{0,20},{1,21},{2,22},{3,23},{4,16},{5,17},{6,18},{7,19},{8,28},{9,... | collective-permute-start | bytes 294920 | tf_op jit(solution)/shard_map/ppermute | solution.py:260
  36.1 1.5 %collective-permute-done.17 = f32[32,768]{1,0:T(8,128)S(1)} collective-permute-done((f32[32,768]{1,0:T(8,128)S(1)}, f32[32,768]{1,0:T(8,128)S(1)}, u32[]{:S(2)}, u32[]{:S(2)}) %collective-permute-start.17) | collective-permute-done | bytes 98336 | tf_op jit(solution)/shard_map/ppermute | solution.py:253
  37.6 2.1 %collective-permute-done.18 = f32[32,768]{1,0:T(8,128)S(1)} collective-permute-done((f32[32,768]{1,0:T(8,128)S(1)}, f32[32,768]{1,0:T(8,128)S(1)}, u32[]{:S(2)}, u32[]{:S(2)}) %collective-permute-start.18) | collective-permute-done | bytes 98336 | tf_op jit(solution)/shard_map/ppermute | solution.py:260
  39.7 1.2 %collective-permute-done.19 = f32[32,768]{1,0:T(8,128)S(1)} collective-permute-done((f32[32,768]{1,0:T(8,128)S(1)}, f32[32,768]{1,0:T(8,128)S(1)}, u32[]{:S(2)}, u32[]{:S(2)}) %collective-permute-start.19) | collective-permute-done | bytes 98336 | tf_op jit(solution)/shard_map/ppermute | solution.py:260
  40.9 0.7 %add_add_fusion = f32[32,768]{1,0:T(8,128)} fusion(f32[32,768]{1,0:T(8,128)S(1)} %collective-permute-done.19, f32[32,768]{1,0:T(8,128)S(1)} %collective-permute-done.18, f32[32,768]{1,0:T(8,128)S(1)} %get-tuple-element.33, f32[32,768]{1,0:T(8,128)S(1)} %collective-permute-done.17), kind=kLoop, calls=%fused_computation | loop fusion | flops 73728 | bytes 491520 | tf_op jit(solution)/shard_map/add | solution.py:263
  (3 shorter events, 0.0 us)
Async XLA Ops:
  1.0 13.2 %collective-permute-start.4 = (bf16[4,24,512]{2,1,0:T(8,128)(2,1)S(1)}, bf16[4,24,512]{2,1,0:T(8,128)(2,1)S(1)}, u32[]{:S(2)}, u32[]{:S(2)}) collective-permute-start(bf16[4,24,512]{2,1,0:T(8,128)(2,1)S(1)} %get-tuple-element.38), channel_id=1, source_target_pairs={{0,12},{1,13},{2,14},{3,15},{4,8},{5,9},{6,10},{7,11},{8,4},{9,5},... | collective-permute-start | bytes 294920 | tf_op jit(solution)/shard_map/ppermute | solution.py:187
  6.1 8.5 %collective-permute-start = (bf16[4,24,512]{2,1,0:T(8,128)(2,1)S(1)}, bf16[4,24,512]{2,1,0:T(8,128)(2,1)S(1)}, u32[]{:S(2)}, u32[]{:S(2)}) collective-permute-start(bf16[4,24,512]{2,1,0:T(8,128)(2,1)S(1)} %get-tuple-element.38), channel_id=1, source_target_pairs={{0,4},{1,5},{2,6},{3,7},{4,0},{5,1},{6,2},{7,3},{8,12},{9,13},{10,... | collective-permute-start | bytes 294920 | tf_op jit(solution)/shard_map/ppermute | solution.py:187
  6.1 14.3 %collective-permute-start.6 = (bf16[4,24,512]{2,1,0:T(8,128)(2,1)S(1)}, bf16[4,24,512]{2,1,0:T(8,128)(2,1)S(1)}, u32[]{:S(2)}, u32[]{:S(2)}) collective-permute-start(bf16[4,24,512]{2,1,0:T(8,128)(2,1)S(1)} %get-tuple-element.25.refs_0_), channel_id=1, source_target_pairs={{0,2},{1,3},{2,0},{3,1},{4,6},{5,7},{6,4},{7,5},{8,10},{9,11},{10,... | collective-permute-start | bytes 294920 | tf_op jit(solution)/shard_map/ppermute | solution.py:187
  7.6 8.7 %collective-permute-start.2 = (bf16[4,24,512]{2,1,0:T(8,128)(2,1)S(1)}, bf16[4,24,512]{2,1,0:T(8,128)(2,1)S(1)}, u32[]{:S(2)}, u32[]{:S(2)}) collective-permute-start(bf16[4,24,512]{2,1,0:T(8,128)(2,1)S(1)} %get-tuple-element.25.refs_0_), channel_id=1, source_target_pairs={{0,8},{1,9},{2,10},{3,11},{4,12},{5,13},{6,14},{7,15},{8,0},{9,1},... | collective-permute-start | bytes 294920 | tf_op jit(solution)/shard_map/ppermute | solution.py:187
  8.4 3.4 %collective-permute-start.7 = (bf16[48,768]{1,0:T(8,128)(2,1)}, bf16[48,768]{1,0:T(8,128)(2,1)S(1)}, u32[]{:S(2)}, u32[]{:S(2)}) collective-permute-start(bf16[48,768]{1,0:T(8,128)(2,1)} %param.6), channel_id=1, source_target_pairs={{1,0},{2,1},{3,2},{4,3},{5,4},{6,5},{7,6},{8,7},{9,8},{10,9},{11,1... | collective-permute-start | bytes 221192 | tf_op jit(solution)/shard_map/ppermute | solution.py:208
  11.8 5.2 %collective-permute-start.8 = (bf16[24,1536]{1,0:T(8,128)(2,1)S(1)}, bf16[24,1536]{1,0:T(8,128)(2,1)S(1)}, u32[]{:S(2)}, u32[]{:S(2)}) collective-permute-start(bf16[24,1536]{1,0:T(8,128)(2,1)S(1)} %pad_maximum_fusion.1), channel_id=1, source_target_pairs={{0,4},{1,5},{2,6},{3,7},{4,0},{5,1},{6,2},{7,3},{8,12},{9,13},{10,... | collective-permute-start | bytes 221192 | tf_op jit(solution)/shard_map/ppermute | solution.py:187
  14.1 7.8 %collective-permute-start.5 = (bf16[4,24,512]{2,1,0:T(8,128)(2,1)S(1)}, bf16[4,24,512]{2,1,0:T(8,128)(2,1)S(1)}, u32[]{:S(2)}, u32[]{:S(2)}) collective-permute-start(bf16[4,24,512]{2,1,0:T(8,128)(2,1)S(1)} %collective-permute-done.4.refs_3_), channel_id=1, source_target_pairs={{0,2},{1,3},{2,0},{3,1},{4,6},{5,7},{6,4},{7,5},{8,10},{9,11},{10,... | collective-permute-start | bytes 294920 | tf_op jit(solution)/shard_map/ppermute | solution.py:187
  14.5 7.9 %collective-permute-start.1 = (bf16[4,24,512]{2,1,0:T(8,128)(2,1)S(1)}, bf16[4,24,512]{2,1,0:T(8,128)(2,1)S(1)}, u32[]{:S(2)}, u32[]{:S(2)}) collective-permute-start(bf16[4,24,512]{2,1,0:T(8,128)(2,1)S(1)} %collective-permute-done.refs_1_), channel_id=1, source_target_pairs={{0,2},{1,3},{2,0},{3,1},{4,6},{5,7},{6,4},{7,5},{8,10},{9,11},{10,... | collective-permute-start | bytes 294920 | tf_op jit(solution)/shard_map/ppermute | solution.py:187
  16.3 7.5 %collective-permute-start.3 = (bf16[4,24,512]{2,1,0:T(8,128)(2,1)S(1)}, bf16[4,24,512]{2,1,0:T(8,128)(2,1)S(1)}, u32[]{:S(2)}, u32[]{:S(2)}) collective-permute-start(bf16[4,24,512]{2,1,0:T(8,128)(2,1)S(1)} %collective-permute-done.2.refs_2_), channel_id=1, source_target_pairs={{0,2},{1,3},{2,0},{3,1},{4,6},{5,7},{6,4},{7,5},{8,10},{9,11},{10,... | collective-permute-start | bytes 294920 | tf_op jit(solution)/shard_map/ppermute | solution.py:187
  20.4 3.5 %collective-permute-start.9 = (bf16[4,24,512]{2,1,0:T(8,128)(2,1)S(1)}, bf16[4,24,512]{2,1,0:T(8,128)(2,1)S(1)}, u32[]{:S(2)}, u32[]{:S(2)}) collective-permute-start(bf16[4,24,512]{2,1,0:T(8,128)(2,1)S(1)} %get-tuple-element.25.refs_0_), channel_id=1, source_target_pairs={{0,1},{1,0},{2,3},{3,2},{4,5},{5,4},{6,7},{7,6},{8,9},{9,8},{10,11... | collective-permute-start | bytes 294920 | tf_op jit(solution)/shard_map/ppermute | solution.py:187
  21.9 2.4 %collective-permute-start.10 = (bf16[4,24,512]{2,1,0:T(8,128)(2,1)S(1)}, bf16[4,24,512]{2,1,0:T(8,128)(2,1)S(1)}, u32[]{:S(2)}, u32[]{:S(2)}) collective-permute-start(bf16[4,24,512]{2,1,0:T(8,128)(2,1)S(1)} %collective-permute-done.refs_1_), channel_id=1, source_target_pairs={{0,1},{1,0},{2,3},{3,2},{4,5},{5,4},{6,7},{7,6},{8,9},{9,8},{10,11... | collective-permute-start | bytes 294920 | tf_op jit(solution)/shard_map/ppermute | solution.py:187
  22.0 2.4 %collective-permute-start.11 = (bf16[4,24,512]{2,1,0:T(8,128)(2,1)S(1)}, bf16[4,24,512]{2,1,0:T(8,128)(2,1)S(1)}, u32[]{:S(2)}, u32[]{:S(2)}) collective-permute-start(bf16[4,24,512]{2,1,0:T(8,128)(2,1)S(1)} %collective-permute-done.2.refs_2_), channel_id=1, source_target_pairs={{0,1},{1,0},{2,3},{3,2},{4,5},{5,4},{6,7},{7,6},{8,9},{9,8},{10,11... | collective-permute-start | bytes 294920 | tf_op jit(solution)/shard_map/ppermute | solution.py:187
  22.4 2.4 %collective-permute-start.12 = (bf16[4,24,512]{2,1,0:T(8,128)(2,1)S(1)}, bf16[4,24,512]{2,1,0:T(8,128)(2,1)S(1)}, u32[]{:S(2)}, u32[]{:S(2)}) collective-permute-start(bf16[4,24,512]{2,1,0:T(8,128)(2,1)S(1)} %collective-permute-done.4.refs_3_), channel_id=1, source_target_pairs={{0,1},{1,0},{2,3},{3,2},{4,5},{5,4},{6,7},{7,6},{8,9},{9,8},{10,11... | collective-permute-start | bytes 294920 | tf_op jit(solution)/shard_map/ppermute | solution.py:187
  23.7 1.3 %collective-permute-start.13 = (bf16[4,24,512]{2,1,0:T(8,128)(2,1)S(1)}, bf16[4,24,512]{2,1,0:T(8,128)(2,1)S(1)}, u32[]{:S(2)}, u32[]{:S(2)}) collective-permute-start(bf16[4,24,512]{2,1,0:T(8,128)(2,1)S(1)} %collective-permute-done.6.refs_4_), channel_id=1, source_target_pairs={{0,1},{1,0},{2,3},{3,2},{4,5},{5,4},{6,7},{7,6},{8,9},{9,8},{10,11... | collective-permute-start | bytes 294920 | tf_op jit(solution)/shard_map/ppermute | solution.py:187
  23.9 1.3 %collective-permute-start.14 = (bf16[4,24,512]{2,1,0:T(8,128)(2,1)S(1)}, bf16[4,24,512]{2,1,0:T(8,128)(2,1)S(1)}, u32[]{:S(2)}, u32[]{:S(2)}) collective-permute-start(bf16[4,24,512]{2,1,0:T(8,128)(2,1)S(1)} %collective-permute-done.1.refs_5_), channel_id=1, source_target_pairs={{0,1},{1,0},{2,3},{3,2},{4,5},{5,4},{6,7},{7,6},{8,9},{9,8},{10,11... | collective-permute-start | bytes 294920 | tf_op jit(solution)/shard_map/ppermute | solution.py:187
  24.3 1.3 %collective-permute-start.15 = (bf16[4,24,512]{2,1,0:T(8,128)(2,1)S(1)}, bf16[4,24,512]{2,1,0:T(8,128)(2,1)S(1)}, u32[]{:S(2)}, u32[]{:S(2)}) collective-permute-start(bf16[4,24,512]{2,1,0:T(8,128)(2,1)S(1)} %collective-permute-done.3.refs_6_), channel_id=1, source_target_pairs={{0,1},{1,0},{2,3},{3,2},{4,5},{5,4},{6,7},{7,6},{8,9},{9,8},{10,11... | collective-permute-start | bytes 294920 | tf_op jit(solution)/shard_map/ppermute | solution.py:187
  24.4 1.3 %collective-permute-start.16 = (bf16[4,24,512]{2,1,0:T(8,128)(2,1)S(1)}, bf16[4,24,512]{2,1,0:T(8,128)(2,1)S(1)}, u32[]{:S(2)}, u32[]{:S(2)}) collective-permute-start(bf16[4,24,512]{2,1,0:T(8,128)(2,1)S(1)} %collective-permute-done.5.refs_7_), channel_id=1, source_target_pairs={{0,1},{1,0},{2,3},{3,2},{4,5},{5,4},{6,7},{7,6},{8,9},{9,8},{10,11... | collective-permute-start | bytes 294920 | tf_op jit(solution)/shard_map/ppermute | solution.py:187
  32.6 5.1 %collective-permute-start.17 = (f32[32,768]{1,0:T(8,128)S(1)}, f32[32,768]{1,0:T(8,128)S(1)}, u32[]{:S(2)}, u32[]{:S(2)}) collective-permute-start(f32[32,768]{1,0:T(8,128)S(1)} %get-tuple-element.34), channel_id=1, source_target_pairs={{0,16},{16,0},{1,17},{17,1},{2,18},{18,2},{3,19},{19,3},{4,20},{20... | collective-permute-start | bytes 294920 | tf_op jit(solution)/shard_map/ppermute | solution.py:253
  34.1 5.7 %collective-permute-start.18 = (f32[32,768]{1,0:T(8,128)S(1)}, f32[32,768]{1,0:T(8,128)S(1)}, u32[]{:S(2)}, u32[]{:S(2)}) collective-permute-start(f32[32,768]{1,0:T(8,128)S(1)} %get-tuple-element.35), channel_id=1, source_target_pairs={{0,4},{1,5},{2,6},{3,7},{4,0},{5,1},{6,2},{7,3},{8,12},{9,13},{10,... | collective-permute-start | bytes 294920 | tf_op jit(solution)/shard_map/ppermute | solution.py:260
  34.1 6.8 %collective-permute-start.19 = (f32[32,768]{1,0:T(8,128)S(1)}, f32[32,768]{1,0:T(8,128)S(1)}, u32[]{:S(2)}, u32[]{:S(2)}) collective-permute-start(f32[32,768]{1,0:T(8,128)S(1)} %get-tuple-element.36), channel_id=1, source_target_pairs={{0,20},{1,21},{2,22},{3,23},{4,16},{5,17},{6,18},{7,19},{8,28},{9,... | collective-permute-start | bytes 294920 | tf_op jit(solution)/shard_map/ppermute | solution.py:260
